TPU v7x, 32 devices: a whole 2x2x4 slice. The times are simulated.
32 devices in a mesh: seq: 4 (over z), dp: 2 (over core), head: 4 (over y, x).
Axes of the slice: x: 2, y: 2, z: 4, core: 2. Of those that a mesh axis runs over, the one named last changes fastest.
Arguments:
- hidden_in: bfloat16 [16, 1024, 1024], P('dp', 'seq', 'head'), may hold values from -6 to 6
- norm_gain: bfloat16 [1024], P('head'), may hold values from 0.5 to 1.5
- w_z: bfloat16 [1024, 2048], P(None, 'head'), may hold values from -0.1875 to 0.1875
- w_x: bfloat16 [1024, 2048], P(None, 'head'), may hold values from -0.1875 to 0.1875
- w_bc: bfloat16 [1024, 256], P(None, 'head'), may hold values from -0.1875 to 0.1875
- w_dt: bfloat16 [1024, 32], P(None, 'head'), may hold values from -0.1875 to 0.1875
- conv_x: float32 [4, 2048], P(None, 'head'), may hold values from -0.5 to 0.5
- conv_x_bias: float32 [2048], P('head'), may hold values from -0.5 to 0.5
- conv_bc: float32 [4, 256], P(None, 'head'), may hold values from -0.5 to 0.5
- conv_bc_bias: float32 [256], P('head'), may hold values from -0.5 to 0.5
- dt_bias: float32 [32], P('head'), may hold values from -3.5 to -2.5
- a_log: float32 [32], P('head'), may hold values from -8 to 0
- skip: float32 [32], P('head'), may hold values from 0.5 to 1.5
- gate_gain: float32 [2048], P('head'), may hold values from 0.5 to 1.5
- w_out: bfloat16 [2048, 1024], P('head'), may hold values from -0.1875 to 0.1875
- out_grad: bfloat16 [16, 1024, 1024], P('dp', 'seq', 'head'), may hold values from -6 to 6
Outputs:
- block_out: bfloat16 [16, 1024, 1024], P('dp', 'seq', 'head')
- grad_in: float32 [16, 1024, 1024], P('dp', 'seq', 'head')
- grad_norm_gain: float32 [1024], P('head')
- grad_w_z: float32 [1024, 2048], P(None, 'head')
- grad_w_x: float32 [1024, 2048], P(None, 'head')
- grad_w_bc: float32 [1024, 256], P(None, 'head')
- grad_w_dt: float32 [1024, 32], P(None, 'head')
- grad_conv_x: float32 [4, 2048], P(None, 'head')
- grad_conv_x_bias: float32 [2048], P('head')
- grad_conv_bc: float32 [4, 256], P(None, 'head')
- grad_conv_bc_bias: float32 [256], P('head')
- grad_dt_bias: float32 [32], P('head')
- grad_a_log: float32 [32], P('head')
- grad_skip: float32 [32], P('head')
- grad_gate_gain: float32 [2048], P('head')
- grad_w_out: float32 [2048, 1024], P('head')
All inputs are finite; a program needn't handle non-finite values.
Results may differ from a plain program's by a relative error of at most 0.0025.
The roundings to bfloat16 on the way count: a program that leaves them out, or rounds other values in their place, can miss the bound.
Values may be sent and summed in bfloat16 or wider, within the bound.
No kernel may reach another device: no remote copies, remote signals or barrier semaphores. Data moves between devices by JAX's collectives and lax.ppermute only.
A program may use at most 320 MiB of HBM per device.

v0:
```python
import jax
import jax.numpy as jnp
from jax import lax
from jax.sharding import PartitionSpec as P

HEAD_DIM = 64
STATE = 128


epsilon = 1e-05
highest = lax.Precision.HIGHEST


def from_behind(value, axis, steps):
    count = lax.axis_size(axis)
    leading, last = (max(0, -steps), min(count, count - steps))
    return lax.ppermute(value, axis, [(source, source + steps) for source in range(leading, last)])


def prefix(value, axis, join, neutral, backward):
    count, mine = (lax.axis_size(axis), lax.axis_index(axis))
    pieces = jax.tree.map(lambda part: lax.all_gather(part, axis), value)
    if backward:
        pieces = jax.tree.map(lambda part: part[::-1], pieces)
        mine = count - 1 - mine
    total = jax.tree.map(
        lambda part, zero: jnp.full_like(part, 0) + jnp.asarray(zero, part.dtype), value, neutral
    )

    def turn(position, total):
        longer = join(total, jax.tree.map(lambda part: part[position], pieces))
        return jax.tree.map(lambda new, old: jnp.where(position < mine, new, old), longer, total)

    return lax.fori_loop(0, count - 1, turn, total)


def silu_grad(pre_value):
    gate_sig = jax.nn.sigmoid(pre_value)
    return gate_sig * (1.0 + pre_value * (1.0 - gate_sig))


def chain_step(earlier, later):
    return (earlier[0] + later[0], earlier[1] * jnp.exp(later[0])[:, :, None, None] + later[1])


def on_device(
    hidden_in,
    norm_gain,
    w_z,
    w_x,
    w_bc,
    w_dt,
    conv_x,
    conv_x_bias,
    conv_bc,
    conv_bc_bias,
    dt_bias,
    a_log,
    skip,
    gate_gain,
    w_out,
    out_grad,
):
    seq_count, local_len, part_width = hidden_in.shape
    heads_here = dt_bias.shape[0]
    inner_here = w_x.shape[1]
    bc_here = w_bc.shape[1]
    kernel_span = conv_x.shape[0]
    edge_len = kernel_span - 1
    row_count = seq_count * local_len
    whole_x, whole_cot, whole_gain = (
        lax.all_gather(hidden_in, "head", axis=2, tiled=True),
        lax.all_gather(out_grad, "head", axis=2, tiled=True),
        lax.all_gather(norm_gain, "head", axis=0, tiled=True),
    )
    full_width = whole_x.shape[2]
    x_full = whole_x.astype(jnp.float32)
    inv_rms = lax.rsqrt(jnp.mean(x_full * x_full, axis=-1, keepdims=True) + epsilon)
    normed = (
        (x_full * inv_rms * whole_gain.astype(jnp.float32))
        .astype(jnp.bfloat16)
        .reshape(row_count, full_width)
    )
    w_cat = jnp.concatenate([w_z, w_x, w_bc, w_dt], axis=1)
    projected = jnp.dot(normed, w_cat, preferred_element_type=jnp.float32).reshape(
        seq_count, local_len, -1
    )
    conv_end = 2 * inner_here + bc_here
    gate_pre = projected[:, :, :inner_here]
    conv_in = projected[:, :, inner_here:conv_end]
    dt_raw = projected[:, :, conv_end:]
    edge_in = from_behind(conv_in[:, local_len - edge_len :, :], "seq", 1)
    extended = jnp.concatenate([edge_in, conv_in], axis=1)
    kernel = jnp.concatenate([conv_x, conv_bc], axis=1)
    kernel_bias = jnp.concatenate([conv_x_bias, conv_bc_bias], axis=0)
    pre_act = jnp.broadcast_to(kernel_bias, conv_in.shape)
    for tap_index in range(kernel_span):
        pre_act = pre_act + kernel[tap_index] * extended[:, tap_index : tap_index + local_len]
    activated = jax.nn.silu(pre_act)
    x_conv = activated[:, :, :inner_here].astype(jnp.bfloat16)
    bc_all = lax.all_gather(
        activated[:, :, inner_here:].astype(jnp.bfloat16), "head", axis=2, tiled=True
    )
    b_rows = bc_all[:, :, :STATE].astype(jnp.float32)
    c_rows = bc_all[:, :, STATE:].astype(jnp.float32)
    values = x_conv.astype(jnp.float32).reshape(seq_count, local_len, heads_here, HEAD_DIM)
    step_size = jax.nn.softplus(dt_raw + dt_bias)
    decay_rate = -jnp.exp(a_log)
    step_log = step_size * decay_rate
    cumulative = jnp.cumsum(step_log, axis=1)
    total_log = cumulative[:, -1, :]
    cum_heads = cumulative.transpose(0, 2, 1)
    step_heads = step_size.transpose(0, 2, 1)
    causal = jnp.arange(local_len)[:, None] >= jnp.arange(local_len)[None, :]
    gap_log = cum_heads[:, :, :, None] - cum_heads[:, :, None, :]
    decay_mat = jnp.where(causal, jnp.exp(jnp.where(causal, gap_log, 0.0)), 0.0)
    scores = jnp.einsum("btn,bsn->bts", c_rows, b_rows, precision=highest)
    decayed = scores[:, None, :, :] * decay_mat
    weights = decayed * step_heads[:, :, None, :]
    local_out = jnp.einsum("bhts,bshp->bthp", weights, values, precision=highest)
    carry_scale = jnp.exp(total_log[:, None, :] - cumulative)
    carry_weight = carry_scale * step_size
    weighted_values = values * carry_weight[..., None]
    local_state = jnp.einsum("bshp,bsn->bhpn", weighted_values, b_rows, precision=highest)
    empty = (jnp.zeros_like(total_log), jnp.zeros_like(local_state))
    _, state_in = prefix((total_log, local_state), "seq", chain_step, empty, False)
    cum_exp = jnp.exp(cumulative)
    cross_out = cum_exp[..., None] * jnp.einsum(
        "btn,bhpn->bthp", c_rows, state_in, precision=highest
    )
    ssd_out = (local_out + cross_out + skip[:, None] * values).reshape(
        seq_count, local_len, inner_here
    )
    gate_act = jax.nn.silu(gate_pre)
    gated_out = ssd_out * gate_act
    inner_width = inner_here * lax.axis_size("head")
    square_sum = lax.psum(jnp.sum(gated_out * gated_out, axis=-1), "head")
    gate_rms = lax.rsqrt(square_sum / inner_width + epsilon)[..., None]
    scaled = (gated_out * gate_rms * gate_gain).astype(jnp.bfloat16).reshape(row_count, inner_here)
    out_own = lax.psum_scatter(
        lax.dot_general(
            w_out, scaled, (((0,), (1,)), ((), ())), preferred_element_type=jnp.float32
        ),
        "head",
        scatter_dimension=0,
        tiled=True,
    )
    x_own = hidden_in.astype(jnp.float32)
    block_out = (x_own + out_own.T.reshape(seq_count, local_len, part_width)).astype(jnp.bfloat16)
    cot_rows = whole_cot.reshape(row_count, full_width)
    g_w_out = lax.dot_general(
        scaled, cot_rows, (((0,), (0,)), ((), ())), preferred_element_type=jnp.float32
    )
    d_scaled = lax.dot_general(
        cot_rows, w_out, (((1,), (1,)), ((), ())), preferred_element_type=jnp.float32
    )
    d_scaled = d_scaled.reshape(seq_count, local_len, inner_here)
    g_gate_gain = jnp.sum(d_scaled * gated_out * gate_rms, axis=(0, 1))
    gain_term = d_scaled * gate_gain
    inner_dot = lax.psum(jnp.sum(gain_term * gated_out, axis=-1), "head")
    d_gated = gate_rms * gain_term - gated_out * gate_rms**3 * (inner_dot / inner_width)[..., None]
    d_gate = d_gated * ssd_out * silu_grad(gate_pre)
    d_out = (d_gated * gate_act).reshape(seq_count, local_len, heads_here, HEAD_DIM)
    g_skip = jnp.sum(d_out * values, axis=(0, 1, 3))
    gram = jnp.einsum("bthp,bshp->bhts", d_out, values, precision=highest)
    d_values = (
        jnp.einsum("bhts,bthp->bshp", weights, d_out, precision=highest) + skip[:, None] * d_out
    )
    masked = gram * decayed
    d_scores = jnp.sum(gram * decay_mat * step_heads[:, :, None, :], axis=1)
    d_step_intra = jnp.sum(masked, axis=2).transpose(0, 2, 1)
    d_gap = masked * step_heads[:, :, None, :]
    d_cum_intra = (jnp.sum(d_gap, axis=3) - jnp.sum(d_gap, axis=2)).transpose(0, 2, 1)
    d_c = jnp.einsum("bts,bsn->btn", d_scores, b_rows, precision=highest)
    d_b = jnp.einsum("bts,btn->bsn", d_scores, c_rows, precision=highest)
    d_out_exp = d_out * cum_exp[..., None]
    d_c = d_c + jnp.einsum("bthp,bhpn->btn", d_out_exp, state_in, precision=highest)
    d_state_in = jnp.einsum("bthp,btn->bhpn", d_out_exp, c_rows, precision=highest)
    d_cum_cross = jnp.sum(d_out * cross_out, axis=3)
    _, d_local_state = prefix((total_log, d_state_in), "seq", chain_step, empty, True)
    state_back = jnp.einsum("bhpn,bsn->bshp", d_local_state, b_rows, precision=highest)
    d_values = d_values + carry_weight[..., None] * state_back
    d_b = d_b + jnp.einsum("bshp,bhpn->bsn", weighted_values, d_local_state, precision=highest)
    d_carry = jnp.sum(values * state_back, axis=3)
    carry_prod = d_carry * carry_weight
    d_total = jnp.exp(total_log) * jnp.sum(state_in * d_local_state, axis=(2, 3)) + jnp.sum(
        carry_prod, axis=1
    )
    d_cum = d_cum_intra + d_cum_cross - carry_prod
    d_cum = d_cum.at[:, -1, :].add(d_total)
    d_step_log = jnp.cumsum(d_cum[:, ::-1, :], axis=1)[:, ::-1, :]
    d_step = d_step_intra + d_carry * carry_scale + d_step_log * decay_rate
    g_a_log = jnp.sum(d_step_log * step_log, axis=(0, 1))
    d_dt_pre = d_step * jax.nn.sigmoid(dt_raw + dt_bias)
    g_dt_bias = jnp.sum(d_dt_pre, axis=(0, 1))
    d_bc_own = lax.psum_scatter(
        jnp.concatenate([d_b, d_c], axis=2), "head", scatter_dimension=2, tiled=True
    )
    d_act = jnp.concatenate([d_values.reshape(seq_count, local_len, inner_here), d_bc_own], axis=2)
    d_pre = d_act * silu_grad(pre_act)
    g_kernel = jnp.stack(
        [
            jnp.sum(d_pre * extended[:, tap_index : tap_index + local_len], axis=(0, 1))
            for tap_index in range(kernel_span)
        ]
    )
    g_kernel_bias = jnp.sum(d_pre, axis=(0, 1))
    d_padded = jnp.pad(d_pre, ((0, 0), (edge_len, edge_len), (0, 0)))
    d_ext = jnp.zeros_like(extended)
    for tap_index in range(kernel_span):
        offset = edge_len - tap_index
        d_ext = d_ext + kernel[tap_index] * d_padded[:, offset : offset + local_len + edge_len]
    back_edge = from_behind(d_ext[:, :edge_len, :], "seq", -1)
    d_conv_in = d_ext[:, edge_len:, :].at[:, local_len - edge_len :, :].add(back_edge)
    d_proj = (
        jnp.concatenate([d_gate, d_conv_in, d_dt_pre], axis=2)
        .astype(jnp.bfloat16)
        .reshape(row_count, -1)
    )
    g_w_cat = lax.dot_general(
        normed, d_proj, (((0,), (0,)), ((), ())), preferred_element_type=jnp.float32
    )
    x_hat_own = x_own * inv_rms
    gain_own = norm_gain.astype(jnp.float32)
    d_own = lax.psum_scatter(
        lax.dot_general(
            w_cat, d_proj, (((1,), (1,)), ((), ())), preferred_element_type=jnp.float32
        ),
        "head",
        scatter_dimension=0,
        tiled=True,
    ).T.reshape(seq_count, local_len, part_width)
    d_hat_own = d_own * gain_own
    row_mean = lax.psum(jnp.sum(d_hat_own * x_hat_own, axis=-1), "head")[..., None] / full_width
    grad_in = out_grad.astype(jnp.float32) + inv_rms * (d_hat_own - x_hat_own * row_mean)
    g_norm_gain = jnp.sum(d_own * x_hat_own, axis=(0, 1))
    (
        g_norm_gain,
        g_w_cat,
        g_kernel,
        g_kernel_bias,
        g_dt_bias,
        g_a_log,
        g_skip,
        g_gate_gain,
        g_w_out,
    ) = lax.psum(
        (
            g_norm_gain,
            g_w_cat,
            g_kernel,
            g_kernel_bias,
            g_dt_bias,
            g_a_log,
            g_skip,
            g_gate_gain,
            g_w_out,
        ),
        ("seq", "dp"),
    )
    g_w_z = g_w_cat[:, :inner_here]
    g_w_x = g_w_cat[:, inner_here : 2 * inner_here]
    g_w_bc = g_w_cat[:, 2 * inner_here : conv_end]
    g_w_dt = g_w_cat[:, conv_end:]
    return (
        block_out,
        grad_in,
        g_norm_gain,
        g_w_z,
        g_w_x,
        g_w_bc,
        g_w_dt,
        g_kernel[:, :inner_here],
        g_kernel_bias[:inner_here],
        g_kernel[:, inner_here:],
        g_kernel_bias[inner_here:],
        g_dt_bias,
        g_a_log,
        g_skip,
        g_gate_gain,
        g_w_out,
    )


def solution(mesh):
    in_specs = (
        P("dp", "seq", "head"),
        P("head"),
        P(None, "head"),
        P(None, "head"),
        P(None, "head"),
        P(None, "head"),
        P(None, "head"),
        P("head"),
        P(None, "head"),
        P("head"),
        P("head"),
        P("head"),
        P("head"),
        P("head"),
        P("head", None),
        P("dp", "seq", "head"),
    )
    out_specs = (
        P("dp", "seq", "head"),
        P("dp", "seq", "head"),
        P("head"),
        P(None, "head"),
        P(None, "head"),
        P(None, "head"),
        P(None, "head"),
        P(None, "head"),
        P("head"),
        P(None, "head"),
        P("head"),
        P("head"),
        P("head"),
        P("head"),
        P("head"),
        P("head", None),
    )
    return jax.shard_map(
        on_device, mesh=mesh, in_specs=in_specs, out_specs=out_specs, check_vma=False
    )
```

profile of v0, /device:TPU:0, one launch (start us, length us, event | category | flops | bytes accessed | tf_op | source)
XLA Modules:
  0.0 1009.9 jit_solution(8339535904604674644)
XLA Ops:
  11.5 9.5 all-gather.3
  21.1 44.0 %all-gather.10.cloned.1.call-done = bf16[8,256,1024]{2,1,0:T(8,128)(2,1)} async-done(((bf16[8,256,256]{2,1,0:T(8,128)(2,1)}), bf16[8,256,1024]{2,1,0:T(8,128)(2,1)}) %all-gather.10.cloned.1.call-update) | async-done | bytes 4194320 | tf_op jit(solution)/shard_map/all_gather | solution.py:72
  68.6 5.0 fusion.62
  82.1 4.9 slice.197
  90.5 13.8 %multiply_convert_fusion = (bf16[8,256,576]{1,2,0:T(8,128)(2,1)S(1)}, f32[8,256,576]{1,2,0:T(8,128)}) fusion(f32[8,256,576]{1,2,0:T(8,128)} %slice.197, f32[576]{0:T(1024)S(1)} %get-tuple-element.429, f32[8,3,576]{1,2,0:T(8,128)} %copy.191, f32[576]{0:T(1024)S(1)} %get-tuple-element.430, f32[576]{0:T(1024)S(1)} %get-tuple-element.431, ...), kind=kLoop, calls=%fused_computation.56 | loop fusion | flops 18874368 | bytes 11863296 | tf_op jit(solution)/shard_map/convert.10
  109.7 4.5 reduce-window.14
  117.2 3.9 fusion.121
  125.8 5.1 all-gather.12.cloned.1.call-done
  130.9 5.7 fusion.59
  142.0 13.7 %all-gather = f32[32,1,8]{2,1,0:T(1,128)S(1)} all-gather(f32[8,1,8]{2,1,0:T(1,128)S(1)} %bitcast.186), channel_id=2, replica_groups=mesh['seq'=4,'dp'=2,'head'=4] {'seq'}, dimensions={0}, use_global_device_ids=true | all-gather | bytes 1280 | tf_op jit(solution)/shard_map/all_gather | solution.py:22
  158.7 127.9 %all-gather.16.cloned.1.call-done = f32[32,8,64,128]{3,2,1,0:T(8,128)} async-done(((f32[8,8,64,128]{3,2,1,0:T(8,128)}), f32[32,8,64,128]{3,2,1,0:T(8,128)}) %all-gather.16.cloned.1.call-update) | async-done | bytes 8388624 | tf_op jit(solution)/shard_map/all_gather | solution.py:22
  286.6 6.3 while.30
  293.0 3.6 fusion.97
  297.1 16.7 %fusion.51 = f32[8,256,8,64]{1,3,2,0:T(8,128)S(1)} fusion(f32[8,256,8,64]{1,3,2,0:T(8,128)S(1)} %bitcast.165, f32[8,256,8,64]{1,3,2,0:T(8,128)S(1)} %fusion.97, bf16[8,256,8,64]{1,3,2,0:T(8,128)(2,1)} %bitcast.182, f32[8,8,256]{2,1,0:T(8,128)S(1)} %copy.201, f32[8,8,256]{2,1,0:T(8,128)S(1)} %copy.199, f32[8,256,256]{2,1,0:T(8,128)S(1)} %copy-done.27, ...), kind=kOutput, calls=%fused_computation.80 | convolution fusion | flops 3246391296 | bytes 17039392 | tf_op jit(solution)/shard_map/bhts,bshp->bthp/dot_general | solution.py:120
  313.9 3.7 multiply_reduce_fusion.12
  317.6 10.5 %psum.84 = f32[8,256]{1,0:T(8,128)S(1)} all-reduce(f32[8,256]{1,0:T(8,128)S(1)} %get-tuple-element.466), channel_id=1, replica_groups=mesh['seq'=4,'dp'=2,'head'=4] {'head'}, use_global_device_ids=true, to_apply=%region_6.7 | all-reduce | flops 2048 | bytes 16384 | tf_op jit(solution)/shard_map/psum | solution.py:137
  328.7 10.9 %all-gather.14.cloned.1.call-done = bf16[8,256,1024]{2,1,0:T(8,128)(2,1)} async-done(((bf16[8,256,256]{2,1,0:T(8,128)(2,1)}), bf16[8,256,1024]{2,1,0:T(8,128)(2,1)}) %all-gather.14.cloned.1.call-update) | async-done | bytes 4194320 | tf_op jit(solution)/shard_map/all_gather | solution.py:73
  339.6 8.9 multiply_reduce_fusion.7
  348.4 9.9 psum.85
  359.1 10.0 multiply_reduce_fusion.8
  375.0 20.9 %multiply_reduce_fusion.1 = (f32[8,8,256]{2,1,0:T(8,128)}, f32[8,8,256]{2,1,0:T(8,128)}, f32[8,8,256]{2,1,0:T(8,128)S(1)}, f32[8,256,256]{2,1,0:T(8,128)}) fusion(f32[8,8,256]{2,1,0:T(8,128)S(1)} %copy-done.37, f32[8,8,256]{2,1,0:T(8,128)S(1)} %copy-done.40, pred[256,256]{1,0:T(8,128)(4,1)} %copy-done.41, f32[8,256,256]{2,1,0:T(8,128)} %fusion.105, ...), kind=kOutput, calls=%fused_computation.14 | convolution fusion | flops 3270983680 | bytes 10878976 | tf_op jit(solution)/shard_map/bthp,bshp->bhts/dot_general | solution.py:165
  400.2 6.9 fusion.87
  409.5 115.0 %all-gather.18.cloned.1.call-done = f32[32,8,64,128]{3,2,1,0:T(8,128)} async-done(((f32[8,8,64,128]{3,2,1,0:T(8,128)}), f32[32,8,64,128]{3,2,1,0:T(8,128)}) %all-gather.18.cloned.1.call-update) | async-done | bytes 8388624 | tf_op jit(solution)/shard_map/all_gather | solution.py:22
  524.5 8.3 rev.13
  532.8 7.0 while.31
  539.8 6.2 fusion.84
  548.9 4.8 multiply_reduce_fusion.9
  556.4 6.7 convolution_bitcast_fusion.1
  563.1 4.2 multiply_reduce_fusion.10
  574.1 4.7 reduce-window.16
  580.6 19.3 %fusion.48 = f32[8,256,8,64]{1,3,2,0:T(8,128)} fusion(f32[8,256,8,64]{1,3,2,0:T(8,128)} %get-tuple-element.492, f32[8,256,8,64]{1,3,2,0:T(8,128)} %bitcast.160, f32[8,8,256]{2,1,0:T(8,128)S(1)} %copy-done.38, f32[8,8,256]{2,1,0:T(8,128)} %copy-done.39, f32[8,256,256]{2,1,0:T(8,128)} %fusion.105, pred[256,256]{1,0:T(8,128)(4,1)} %copy-done.41, ...), kind=kOutput, calls=%fused_computation.74 | convolution fusion | flops 3246391296 | bytes 14942240 | tf_op jit(solution)/shard_map/bhts,bthp->bshp/dot_general | solution.py:167
  599.9 14.2 %fusion.122 = (f32[576]{0:T(1024)S(1)}, f32[576]{0:T(1024)S(1)}, f32[576]{0:T(1024)}, f32[576]{0:T(1024)S(1)}, f32[576]{0:T(1024)}, /*index=5*/f32[8,256,576]{1,2,0:T(8,128)S(1)}) fusion(f32[8,256,1096]{1,2,0:T(8,128)} %copy-done.3, f32[8,256,576]{1,2,0:T(8,128)} %slice.197, f32[8,3,576]{1,2,0:T(8,128)S(1)} %copy-done.9, ...), kind=kLoop, calls=%fused_computation.188 | loop fusion | flops 24769728 | bytes 23659776 | tf_op jit(solution)/shard_map/reduce_sum | solution.py:207
  614.1 6.1 fusion.27
  629.2 4.4 fusion.124
  634.9 3.9 slice.214
  643.6 21.1 %scatter-add.6 = bf16[8,256,576]{1,2,0:T(8,128)(2,1)S(1)} dynamic-update-slice(bf16[8,256,576]{1,2,0:T(8,128)(2,1)S(1)} %slice.214, bf16[8,3,576]{1,2,0:T(8,128)(2,1)} %copy.217, s32[]{:T(128)} %constant.132.clone.1, s32[]{:T(128)} %constant.136.clone.1, s32[]{:T(128)} %constant.132.clone.1) | dynamic-update-slice | bytes 55300 | tf_op jit(solution)/shard_map/scatter-add | solution.py:214
  664.7 10.0 fusion.45
  674.8 3.9 copy.211
  678.7 4.0 copy.230
  684.8 8.1 fusion.33
  697.2 7.2 convolution_bitcast_fusion
  705.4 112.7 %all-reduce.5.cloned.1.call-done = (f32[1024,1096]{0,1:T(8,128)}, f32[512,1024]{1,0:T(8,128)}) async-done(((f32[1024,1096]{0,1:T(8,128)}, f32[512,1024]{1,0:T(8,128)}), (f32[1024,1096]{0,1:T(8,128)}, f32[512,1024]{1,0:T(8,128)})) %all-reduce.5.cloned.1.call-update) | async-done | bytes 6586384 | tf_op jit(solution)/shard_map/psum | solution.py:247
  821.1 4.0 fusion.127
  829.8 77.6 %reduce-scatter.8.cloned.1.call-done = f32[256,2048]{1,0:T(8,128)} async-done(((f32[1024,2048]{1,0:T(8,128)}), f32[256,2048]{1,0:T(8,128)}) %reduce-scatter.8.cloned.1.call-update) | async-done | bytes 2097168 | tf_op jit(solution)/shard_map/reduce_scatter | solution.py:225
  911.6 29.1 %all-reduce.1 = (f32[256]{0:T(256)}, f32[4,576]{1,0:T(4,128)S(1)}, f32[576]{0:T(1024)S(1)}, f32[8]{0:T(128)}, f32[8]{0:T(128)}, /*index=5*/f32[8]{0:T(128)}, f32[512]{0:T(512)}) all-reduce(f32[256]{0:T(256)S(1)} %get-tuple-element.426, f32[4,576]{1,0:T(4,128)S(1)} %pad_maximum_fusion.5, ...), channel_id=1, replica_groups=mesh['seq'=4,'dp'=2,'head'=4] {'seq','dp'}, use_global_device_ids=true, to_apply=%region_27.28 | all-reduce | flops 3672 | bytes 29376 | tf_op jit(solution)/shard_map/psum | solution.py:247
  942.9 9.5 psum.86
  952.5 45.2 %reduce-scatter.4.cloned.1.call-done = f32[256,2048]{0,1:T(8,128)} async-done(((f32[1024,2048]{0,1:T(8,128)}), f32[256,2048]{0,1:T(8,128)}) %reduce-scatter.4.cloned.1.call-update) | async-done | bytes 2097168 | tf_op jit(solution)/shard_map/reduce_scatter | solution.py:140
  997.6 3.9 fusion.76
  (292 shorter events, 119.5 us)
Async XLA Ops:
  7.2 332.4 %copy-start = (bf16[512,1024]{1,0:T(8,128)(2,1)S(1)}, bf16[512,1024]{1,0:T(8,128)(2,1)}, u32[]{:S(2)}) copy-start(bf16[512,1024]{1,0:T(8,128)(2,1)} %param.38) | copy-start | bytes 3145732
  7.2 13.8 %copy-start.56 = (f32[4,512]{1,0:T(4,128)S(1)}, f32[4,512]{1,0:T(4,128)}, u32[]{:S(2)}) copy-start(f32[4,512]{1,0:T(4,128)} %param.30) | copy-start | bytes 24580
  7.2 13.8 %copy-start.63 = (f32[4,64]{1,0:T(4,128)S(1)}, f32[4,64]{1,0:T(4,128)}, u32[]{:S(2)}) copy-start(f32[4,64]{1,0:T(4,128)} %param.32) | copy-start | bytes 3076
  7.2 13.8 %copy-start.72 = (f32[8]{0:T(128)S(1)}, f32[8]{0:T(128)}, u32[]{:S(2)}) copy-start(f32[8]{0:T(128)} %param.35) | copy-start | bytes 100
  7.2 58.0 %all-gather.10.cloned.1.call-start = ((), (), s32[]{:S(2)}) async-start(), calls=%async_computation.3 | async-start | bytes 5242880 | tf_op jit(solution)/shard_map/all_gather | solution.py:72
  8.0 60.5 %copy-start.68 = (bf16[1024,64]{0,1:T(8,128)(2,1)S(1)}, bf16[1024,64]{0,1:T(8,128)(2,1)}, u32[]{:S(2)}) copy-start(bf16[1024,64]{0,1:T(8,128)(2,1)} %param.28) | copy-start | bytes 393220
  8.0 60.5 %copy-start.70 = (bf16[1024,8]{0,1:T(8,128)(2,1)S(1)}, bf16[1024,8]{0,1:T(8,128)(2,1)}, u32[]{:S(2)}) copy-start(bf16[1024,8]{0,1:T(8,128)(2,1)} %param.29) | copy-start | bytes 49156
  8.0 122.9 %all-gather.12.cloned.1.call-start = ((), (), s32[]{:S(2)}) async-start(), calls=%async_computation.4 | async-start | bytes 1310720 | tf_op jit(solution)/shard_map/all_gather | solution.py:101
  9.5 58.9 %copy-start.30 = (bf16[1024,512]{0,1:T(8,128)(2,1)}, bf16[1024,512]{0,1:T(8,128)(2,1)S(1)}, u32[]{:S(2)}) copy-start(bf16[1024,512]{0,1:T(8,128)(2,1)S(1)} %copy.188) | copy-start | bytes 3145732
  11.4 57.0 %copy-start.32 = (bf16[1024,512]{0,1:T(8,128)(2,1)}, bf16[1024,512]{0,1:T(8,128)(2,1)S(1)}, u32[]{:S(2)}) copy-start(bf16[1024,512]{0,1:T(8,128)(2,1)S(1)} %copy.189) | copy-start | bytes 3145732
  21.0 47.5 %copy-start.59 = (f32[4,1,256]{2,1,0:T(1,128)}, f32[4,1,256]{2,1,0:T(1,128)S(1)}, u32[]{:S(2)}) copy-start(f32[4,1,256]{2,1,0:T(1,128)S(1)} %convert_element_type.44) | copy-start | bytes 12292
  21.1 69.4 %copy-start.44 = (f32[576]{0:T(1024)}, f32[576]{0:T(1024)S(1)}, u32[]{:S(2)}) copy-start(f32[576]{0:T(1024)S(1)} %get-tuple-element.428) | copy-start | bytes 6916
  21.1 69.4 %copy-start.46 = (f32[576]{0:T(1024)}, f32[576]{0:T(1024)S(1)}, u32[]{:S(2)}) copy-start(f32[576]{0:T(1024)S(1)} %get-tuple-element.429) | copy-start | bytes 6916
  21.1 69.3 %copy-start.48 = (f32[576]{0:T(1024)}, f32[576]{0:T(1024)S(1)}, u32[]{:S(2)}) copy-start(f32[576]{0:T(1024)S(1)} %get-tuple-element.430) | copy-start | bytes 6916
  21.1 69.3 %copy-start.50 = (f32[576]{0:T(1024)}, f32[576]{0:T(1024)S(1)}, u32[]{:S(2)}) copy-start(f32[576]{0:T(1024)S(1)} %get-tuple-element.431) | copy-start | bytes 6916
  21.1 84.2 %copy-start.65 = (f32[8]{0:T(128)}, f32[8]{0:T(128)S(1)}, u32[]{:S(2)}) copy-start(f32[8]{0:T(128)S(1)} %exponential_negate_fusion) | copy-start | bytes 100
  78.6 9.7 collective-permute-start
  90.5 14.9 %copy-start.57 = (f32[8]{0:T(128)S(1)}, f32[8]{0:T(128)}, u32[]{:S(2)}) copy-start(f32[8]{0:T(128)} %param.34) | copy-start | bytes 100
  104.3 18.4 %copy-start.5 = (bf16[8,256,576]{1,2,0:T(8,128)(2,1)}, bf16[8,256,576]{1,2,0:T(8,128)(2,1)S(1)}, u32[]{:S(2)}) copy-start(bf16[8,256,576]{1,2,0:T(8,128)(2,1)S(1)} %get-tuple-element.468) | copy-start | bytes 7077892
  105.1 181.5 %all-gather.16.cloned.1.call-start = ((), (), s32[]{:S(2)}) async-start(), calls=%async_computation.9 | async-start | bytes 10485760 | tf_op jit(solution)/shard_map/all_gather | solution.py:22
  136.7 202.9 %all-gather.14.cloned.1.call-start = ((), (), s32[]{:S(2)}) async-start(), calls=%async_computation.6 | async-start | bytes 5242880 | tf_op jit(solution)/shard_map/all_gather | solution.py:73
  137.2 387.2 %all-gather.18.cloned.1.call-start = ((), (), s32[]{:S(2)}) async-start(), calls=%async_computation.10 | async-start | bytes 10485760 | tf_op jit(solution)/shard_map/all_gather | solution.py:22
  137.3 159.3 %copy-start.41 = (pred[256,256]{1,0:T(8,128)(4,1)}, pred[256,256]{1,0:T(8,128)(4,1)S(1)}, u32[]{:S(2)}) copy-start(pred[256,256]{1,0:T(8,128)(4,1)S(1)} %iota_compare_fusion) | copy-start | bytes 196612
  140.4 156.2 %copy-start.36 = (f32[8,8,256]{2,1,0:T(8,128)}, f32[8,8,256]{2,1,0:T(8,128)S(1)}, u32[]{:S(2)}) copy-start(f32[8,8,256]{2,1,0:T(8,128)S(1)} %copy.201) | copy-start | bytes 196612
  142.0 154.6 %copy-start.39 = (f32[8,8,256]{2,1,0:T(8,128)}, f32[8,8,256]{2,1,0:T(8,128)S(1)}, u32[]{:S(2)}) copy-start(f32[8,8,256]{2,1,0:T(8,128)S(1)} %copy.199) | copy-start | bytes 196612
  292.9 20.9 %copy-start.1 = (f32[8,8,64,128]{3,2,1,0:T(8,128)}, f32[8,8,64,128]{3,2,1,0:T(8,128)S(1)}, u32[]{:S(2)}) copy-start(f32[8,8,64,128]{3,2,1,0:T(8,128)S(1)} %get-tuple-element.228) | copy-start | bytes 6291460
  293.0 20.9 %slice-start = ((s8[8978432]{0:T(1024)(128)(4,1)}), s8[4194304]{0:T(1024)(128)(4,1)S(1)}, s32[]{:S(2)}) async-start(s8[8978432]{0:T(1024)(128)(4,1)} %bitcast.161), calls=%async_computation.12 | async-start | bytes 8388608
  296.6 17.2 %copy-start.11 = (f32[8,256,8,64]{1,3,2,0:T(8,128)}, f32[8,256,8,64]{1,3,2,0:T(8,128)S(1)}, u32[]{:S(2)}) copy-start(f32[8,256,8,64]{1,3,2,0:T(8,128)S(1)} %fusion.97) | copy-start | bytes 12582916
  297.1 16.8 %slice-start.1 = ((s8[8978432]{0:T(1024)(128)(4,1)}), s8[4194304]{0:T(1024)(128)(4,1)S(1)}, s32[]{:S(2)}) async-start(s8[8978432]{0:T(1024)(128)(4,1)} %bitcast.161), calls=%async_computation.13 | async-start | bytes 8388608
  297.1 16.8 %slice-start.2 = ((s8[8978432]{0:T(1024)(128)(4,1)}), s8[589824]{0:T(1024)(128)(4,1)S(1)}, s32[]{:S(2)}) async-start(s8[8978432]{0:T(1024)(128)(4,1)} %bitcast.161), calls=%async_computation.14 | async-start | bytes 1179648
  339.6 19.5 %copy-start.6 = (bf16[8,256,576]{1,2,0:T(8,128)(2,1)S(1)}, bf16[8,256,576]{1,2,0:T(8,128)(2,1)}, u32[]{:S(2)}) copy-start(bf16[8,256,576]{1,2,0:T(8,128)(2,1)} %copy-done.5) | copy-start | bytes 7077892
  359.1 12.1 %copy-start.13 = (bf16[8,256,256]{1,2,0:T(8,128)(2,1)S(1)}, bf16[8,256,256]{1,2,0:T(8,128)(2,1)}, u32[]{:S(2)}) copy-start(bf16[8,256,256]{1,2,0:T(8,128)(2,1)} %all-gather.12.cloned.1.call-done) | copy-start | bytes 3145732
  374.8 225.0 %reduce-scatter.6.cloned.1.call-start = ((), (), s32[]{:S(2)}) async-start(), calls=%async_computation.7 | async-start | bytes 2621440 | tf_op jit(solution)/shard_map/reduce_scatter | solution.py:196
  548.9 269.2 %all-reduce.5.cloned.1.call-start = ((), (), s32[]{:S(2)}) async-start(), calls=%async_computation.11 | async-start | bytes 13172736 | tf_op jit(solution)/shard_map/psum | solution.py:247
  571.4 9.1 copy-start.38
  571.4 9.1 copy-start.74
  580.6 19.3 %copy-start.9 = (f32[8,3,576]{1,2,0:T(8,128)S(1)}, f32[8,3,576]{1,2,0:T(8,128)}, u32[]{:S(2)}) copy-start(f32[8,3,576]{1,2,0:T(8,128)} %copy.191) | copy-start | bytes 165892
  599.8 14.3 %copy-start.45 = (f32[576]{0:T(1024)S(1)}, f32[576]{0:T(1024)}, u32[]{:S(2)}) copy-start(f32[576]{0:T(1024)} %copy-done.44) | copy-start | bytes 6916
  599.8 14.3 %copy-start.47 = (f32[576]{0:T(1024)S(1)}, f32[576]{0:T(1024)}, u32[]{:S(2)}) copy-start(f32[576]{0:T(1024)} %copy-done.46) | copy-start | bytes 6916
  599.8 14.3 %copy-start.49 = (f32[576]{0:T(1024)S(1)}, f32[576]{0:T(1024)}, u32[]{:S(2)}) copy-start(f32[576]{0:T(1024)} %copy-done.48) | copy-start | bytes 6916
  599.9 14.3 %copy-start.51 = (f32[576]{0:T(1024)S(1)}, f32[576]{0:T(1024)}, u32[]{:S(2)}) copy-start(f32[576]{0:T(1024)} %copy-done.50) | copy-start | bytes 6916
  620.2 8.9 copy-start.10
  620.2 8.9 copy-start.12
  620.2 8.9 copy-start.43
  627.8 13.4 %collective-permute-start.1 = (f32[8,3,576]{2,0,1:T(8,128)}, f32[8,3,576]{2,0,1:T(8,128)}, u32[]{:S(2)}, u32[]{:S(2)}) collective-permute-start(f32[8,3,576]{2,0,1:T(8,128)} %copy.215), channel_id=1, source_target_pairs={{8,0},{16,8},{24,16},{9,1},{17,9},{25,17},{10,2},{18,10},{26,18},{... | collective-permute-start | bytes 165896 | tf_op jit(solution)/shard_map/ppermute | solution.py:17
  638.8 25.9 %copy-start.35 = (f32[8,256]{1,0:T(8,128)S(1)}, f32[8,256]{1,0:T(8,128)}, u32[]{:S(2)}) copy-start(f32[8,256]{1,0:T(8,128)} %copy-done.34) | copy-start | bytes 24580
  674.7 232.8 %reduce-scatter.8.cloned.1.call-start = ((), (), s32[]{:S(2)}) async-start(), calls=%async_computation.8 | async-start | bytes 10485760 | tf_op jit(solution)/shard_map/reduce_scatter | solution.py:225
  692.9 304.7 %reduce-scatter.4.cloned.1.call-start = ((), (), s32[]{:S(2)}) async-start(), calls=%async_computation.5 | async-start | bytes 10485760 | tf_op jit(solution)/shard_map/reduce_scatter | solution.py:140
  (44 other events, 171.8 us)
Sparse Core Ops, SparseCore 0:
  9.9 55.2 all-gather.9
  105.2 25.6 all-gather.11
  136.8 149.7 all-gather.15
  288.2 51.2 all-gather.13
  374.9 149.5 all-gather.17
  549.0 33.3 reduce-scatter.5
  674.8 143.1 all-reduce.4
  821.1 86.2 reduce-scatter.7
  910.8 86.7 reduce-scatter.3
where the time goes:
time: 1020 us; the launch traced here: 1010 us
  waiting for transfers between devices  540 us (53%)
  matrix products  139 us (14%)
  local copies, waits for them, and re-layouts  121 us (12%)
  other arithmetic  106 us (10%)
  blocking collectives  82.3 us (8%)
  between operations  15.4 us (2%)
    all_gather x2, waiting for transfers between devices, prefix(): pieces = jax.tree.map(lambda part: lax.all_gather(part, axis), value)  243 us
    psum x1, waiting for transfers between devices, on_device(): lax.psum((g_norm_gain, g_w_cat, g_kernel, g_kernel_bias, g_dt_bias, g_a_l...  113 us
    reduce_scatter x1, waiting for transfers between devices, on_device(): lax.psum_scatter(lax.dot_general(w_cat, d_proj, (((1,), (1,)), ((), ())),...  77.6 us
    reduce_scatter x1, waiting for transfers between devices, on_device(): lax.psum_scatter(lax.dot_general(w_out, scaled, (((0,), (1,)), ((), ())),...  45.2 us
    all_gather x1, waiting for transfers between devices, on_device(): lax.all_gather(hidden_in, 'head', axis=2, tiled=True)  44 us
    psum x1, blocking collectives, on_device(): lax.psum((g_norm_gain, g_w_cat, g_kernel, g_kernel_bias, g_dt_bias, g_a_l...  29.1 us
    unnamed x168, local copies, waits for them, and re-layouts  24.1 us
    another operation x7, other arithmetic  23.3 us
  transfers between devices with their start and end apart: 11, of which 8 were waited for; matrix products, arithmetic and copies ran while one was open for 21% of the time, Pallas kernels for 0%

commit v1 on v0

--- a/solution.py
+++ b/solution.py
@@ -1,6 +1,9 @@
+import functools
 import jax
 import jax.numpy as jnp
 from jax import lax
+from jax.experimental import pallas as pl
+from jax.experimental.pallas import tpu as pltpu
 from jax.sharding import PartitionSpec as P
 
 HEAD_DIM = 64
@@ -43,7 +46,7 @@
     return (earlier[0] + later[0], earlier[1] * jnp.exp(later[0])[:, :, None, None] + later[1])
 
 
-def on_device(
+def on_device_general(
     hidden_in,
     norm_gain,
     w_z,
@@ -282,6 +285,782 @@
     )
 
 
+BF = jnp.bfloat16
+F32 = jnp.float32
+CHUNK = 256
+LANES = 128
+VMEM_LIMIT = 56 * 1024 * 1024
+
+
+def dot_nn(a, b):
+    return lax.dot_general(a, b, (((1,), (0,)), ((), ())), preferred_element_type=F32)
+
+
+def dot_nt(a, b):
+    return lax.dot_general(a, b, (((1,), (1,)), ((), ())), preferred_element_type=F32)
+
+
+def dot_tn(a, b):
+    return lax.dot_general(a, b, (((0,), (0,)), ((), ())), preferred_element_type=F32)
+
+
+def split2(value):
+    high = value.astype(BF)
+    return high, (value - high.astype(F32)).astype(BF)
+
+
+def split3(value):
+    high = value.astype(BF)
+    rest = value - high.astype(F32)
+    middle = rest.astype(BF)
+    return high, middle, (rest - middle.astype(F32)).astype(BF)
+
+
+def sigmoid(value):
+    return 1.0 / (1.0 + jnp.exp(-value))
+
+
+def silu_slope(value, sig):
+    return sig * (1.0 + value * (1.0 - sig))
+
+
+def step_values(dt_block, dt_params):
+    shifted = dt_block + dt_params[0:1]
+    step = jnp.maximum(shifted, 0.0) + jnp.log1p(jnp.exp(-jnp.abs(shifted)))
+    rate = -jnp.exp(dt_params[1:2])
+    return shifted, step, rate, step * rate
+
+
+def inverse_rms(blocks):
+    total = sum(jnp.sum(block * block, axis=1, keepdims=True) for block in blocks)
+    return lax.rsqrt(total / (len(blocks) * blocks[0].shape[1]) + epsilon)
+
+
+def normed_blocks(x_refs, gain_ref):
+    blocks = [ref[...].astype(F32) for ref in x_refs]
+    inverse = inverse_rms(blocks)
+    hats = [block * inverse for block in blocks]
+    return inverse, hats, [(hat * gain_ref[k : k + 1]).astype(BF) for k, hat in enumerate(hats)]
+
+
+def block_of(index_ref, k, size):
+    return pl.ds(pl.multiple_of(index_ref[k] * size, size), size)
+
+
+def column_of_sums(rows, lanes_here):
+    tile = jnp.zeros((CHUNK, LANES), F32)
+    lane = lax.broadcasted_iota(jnp.int32, (CHUNK, LANES), 1)
+    for position, value in enumerate(rows):
+        tile = jnp.where(lane == position, value, tile)
+    return jnp.transpose(tile)[0:lanes_here]
+
+
+def forward_kernel(
+    index_ref, x0, x1, x2, x3, w_ref, gain_ref, taps_ref, dt_ref, skip_ref, spread_ref, lower_ref,
+    gate_out, conv_out, ssd_out, state_out, extended, state,
+):
+    inner = skip_ref.shape[1]
+    heads = inner // HEAD_DIM
+    conv_width = inner + 2 * STATE
+
+    @pl.when(pl.program_id(0) == 0)
+    def _():
+        extended[0:8, :] = jnp.zeros((8, conv_width), F32)
+        state[...] = jnp.zeros(state.shape, F32)
+
+    x_refs = (x0, x1, x2, x3)
+    _, _, normed = normed_blocks(x_refs, gain_ref)
+    projected = sum(
+        dot_nn(part, w_ref[block_of(index_ref, k, part.shape[1]), :])
+        for k, part in enumerate(normed)
+    )
+    gate_out[...] = projected[:, :inner]
+    conv_out[...] = projected[:, inner:]
+    conv_in = projected[:, inner : inner + conv_width]
+    extended[8 : 8 + CHUNK, :] = conv_in
+    pre_act = taps_ref[4:5, :] + taps_ref[3:4, :] * conv_in
+    for k in range(3):
+        pre_act = pre_act + taps_ref[k : k + 1, :] * extended[5 + k : 5 + k + CHUNK, :]
+    extended[0:8, :] = conv_in[CHUNK - 8 :, :]
+    act = (pre_act * sigmoid(pre_act)).astype(BF)
+    values = act[:, :inner]
+    b_rows = act[:, inner : inner + STATE]
+    c_rows = act[:, inner + STATE :]
+
+    _, step, _, step_log = step_values(projected[:, inner + conv_width :], dt_ref)
+    cumulative = sum(dot_nn(lower_ref[...], part) for part in split3(step_log))
+    cum_t = jnp.transpose(cumulative)
+    step_t = jnp.transpose(step)
+    total = cumulative[CHUNK - 1 : CHUNK, :]
+    spread = spread_ref[...]
+    widened = jnp.concatenate([jnp.exp(cumulative), jnp.exp(total - cumulative) * step], axis=0)
+    high, low = split2(widened)
+    widened = dot_nn(high, spread) + dot_nn(low, spread)
+    cum_exp, carry_weight = widened[:CHUNK], widened[CHUNK:]
+
+    state_now = state[...]
+    state_out[...] = state_now
+    s_high, s_low = split2(state_now)
+    cross = dot_nt(c_rows, s_high) + dot_nt(c_rows, s_low)
+    values_f = values.astype(F32)
+    carried = cum_exp * cross + skip_ref[...] * values_f
+
+    scores = dot_nt(c_rows, b_rows)
+    row = lax.broadcasted_iota(jnp.int32, (CHUNK, CHUNK), 0)
+    column = lax.broadcasted_iota(jnp.int32, (CHUNK, CHUNK), 1)
+    causal = row >= column
+    lane = lax.broadcasted_iota(jnp.int32, (CHUNK, LANES), 1)
+    for pair in range(heads // 2):
+        lanes = slice(pair * LANES, (pair + 1) * LANES)
+        total_out = carried[:, lanes]
+        for side in range(2):
+            h = 2 * pair + side
+            mine = (lane >= HEAD_DIM) if side else (lane < HEAD_DIM)
+            own_values = jnp.where(mine, values[:, lanes], jnp.zeros((), BF))
+            gap = cumulative[:, h : h + 1] - cum_t[h : h + 1, :]
+            decay = jnp.exp(jnp.where(causal, gap, -1e30))
+            high, low = split2(scores * decay * step_t[h : h + 1, :])
+            total_out = total_out + dot_nn(high, own_values) + dot_nn(low, own_values)
+        ssd_out[:, lanes] = total_out
+
+    high, low = split2(values_f * carry_weight)
+    grown = dot_tn(high, b_rows) + dot_tn(low, b_rows)
+    total_t = jnp.exp(cum_t[:, CHUNK - 1 : CHUNK])
+    for h in range(heads):
+        part = slice(h * HEAD_DIM, (h + 1) * HEAD_DIM)
+        state[part, :] = total_t[h : h + 1, :] * state_now[part] + grown[part]
+
+
+def score_kernel(index_ref, g0, g1, g2, g3, w_ref, ssd_ref, gate_ref, gain_ref, d_out, sums_out):
+    d_scaled = sum(
+        dot_nn(ref[...], w_ref[block_of(index_ref, k, ref.shape[1]), :])
+        for k, ref in enumerate((g0, g1, g2, g3))
+    )
+    d_out[...] = d_scaled
+    gate = gate_ref[...]
+    gated = ssd_ref[...] * (gate * sigmoid(gate))
+    squares = jnp.sum(gated * gated, axis=1, keepdims=True)
+    inner_dot = jnp.sum(d_scaled * gain_ref[...] * gated, axis=1, keepdims=True)
+    sums_out[0] = column_of_sums((squares, inner_dot), 8)
+
+
+def backward_kernel(
+    inner_width, index_ref, q0, q1, q2, q3, ssd_ref, gate_ref, d_scaled_ref, conv_ref, before_ref,
+    state_ref, gain_ref, taps_ref, dt_ref, skip_ref, spread_ref, gather_ref, lower_ref, upper_ref,
+    scaled_out, d_gate_out, d_x_out, d_dt_out, d_bc_out, wide_out, dt_out,
+    extended, d_pre, state_grad,
+):
+    inner = skip_ref.shape[1]
+    heads = inner // HEAD_DIM
+    conv_width = inner + 2 * STATE
+    step_at = pl.program_id(0)
+    chunk_at = pl.num_programs(0) - 1 - step_at
+
+    @pl.when(step_at == 0)
+    def _():
+        d_pre[CHUNK : CHUNK + 8, :] = jnp.zeros((8, inner), F32)
+        state_grad[...] = jnp.zeros(state_grad.shape, F32)
+        wide_out[...] = jnp.zeros(wide_out.shape, F32)
+        dt_out[...] = jnp.zeros(dt_out.shape, F32)
+
+    sums = q0[0] + q1[0] + q2[0] + q3[0]
+    sums = jnp.transpose(jnp.concatenate([sums, jnp.zeros((LANES - 8, CHUNK), F32)], axis=0))
+    rms = lax.rsqrt(sums[:, 0:1] / inner_width + epsilon)
+    mean_dot = sums[:, 1:2] / inner_width
+    gate = gate_ref[...]
+    gate_sig = sigmoid(gate)
+    gate_act = gate * gate_sig
+    ssd = ssd_ref[...]
+    gated = ssd * gate_act
+    gated_rms = gated * rms
+    gain = gain_ref[...]
+    d_scaled = d_scaled_ref[...]
+    scaled_out[...] = (gated_rms * gain).astype(BF)
+    wide_out[5:6, :] += jnp.sum(d_scaled * gated_rms, axis=0, keepdims=True)
+    d_gated = rms * (d_scaled * gain) - gated * (rms * rms * rms * mean_dot)
+    d_gate_out[...] = (d_gated * ssd * silu_slope(gate, gate_sig)).astype(BF)
+    d_ssd = d_gated * gate_act
+
+    conv_in = conv_ref[:, :conv_width]
+    extended[0:8, :] = jnp.where(chunk_at > 0, before_ref[:, :conv_width], 0.0)
+    extended[8 : 8 + CHUNK, :] = conv_in
+    pre_act = taps_ref[4:5, :] + taps_ref[3:4, :] * conv_in
+    for k in range(3):
+        pre_act = pre_act + taps_ref[k : k + 1, :] * extended[5 + k : 5 + k + CHUNK, :]
+    sig = sigmoid(pre_act)
+    act = (pre_act * sig).astype(BF)
+    slope_x = silu_slope(pre_act[:, :inner], sig[:, :inner])
+    values = act[:, :inner]
+    values_f = values.astype(F32)
+    b_rows = act[:, inner : inner + STATE]
+    c_rows = act[:, inner + STATE :]
+    wide_out[6:7, :] += jnp.sum(d_ssd * values_f, axis=0, keepdims=True)
+
+    shifted, step, rate, step_log = step_values(conv_ref[:, conv_width:], dt_ref)
+    cumulative = sum(dot_nn(lower_ref[...], part) for part in split3(step_log))
+    cum_t = jnp.transpose(cumulative)
+    total = cumulative[CHUNK - 1 : CHUNK, :]
+    carry_scale = jnp.exp(total - cumulative)
+    carry = carry_scale * step
+    spread = spread_ref[...]
+    high, low = split2(jnp.concatenate([jnp.exp(cumulative), carry], axis=0))
+    widened = dot_nn(high, spread) + dot_nn(low, spread)
+    cum_exp, carry_weight = widened[:CHUNK], widened[CHUNK:]
+
+    scores = dot_nt(b_rows, c_rows)
+    row = lax.broadcasted_iota(jnp.int32, (CHUNK, CHUNK), 0)
+    column = lax.broadcasted_iota(jnp.int32, (CHUNK, CHUNK), 1)
+    causal = row <= column
+    lane = lax.broadcasted_iota(jnp.int32, (CHUNK, LANES), 1)
+
+    s_high, s_low = split2(state_ref[...])
+    r_now = state_grad[...]
+    r_high, r_low = split2(r_now)
+    cross = cum_exp * (dot_nt(c_rows, s_high) + dot_nt(c_rows, s_low))
+    back = dot_nt(b_rows, r_high) + dot_nt(b_rows, r_low)
+    d_values = carry_weight * back + skip_ref[...] * d_ssd
+
+    d_scores = jnp.zeros((CHUNK, CHUNK), F32)
+    step_intra = jnp.zeros((CHUNK, LANES), F32)
+    row_sums = []
+    d_parts = []
+    for pair in range(heads // 2):
+        lanes = slice(pair * LANES, (pair + 1) * LANES)
+        g_high, g_low = split2(d_ssd[:, lanes])
+        part = d_values[:, lanes]
+        for side in range(2):
+            h = 2 * pair + side
+            mine = (lane >= HEAD_DIM) if side else (lane < HEAD_DIM)
+            zero = jnp.zeros((), BF)
+            own_values = jnp.where(mine, values[:, lanes], zero)
+            own_high = jnp.where(mine, g_high, zero)
+            own_low = jnp.where(mine, g_low, zero)
+            gram = dot_nt(own_values, g_high) + dot_nt(own_values, g_low)
+            gap = cum_t[h : h + 1, :] - cumulative[:, h : h + 1]
+            decay = jnp.exp(jnp.where(causal, gap, -1e30))
+            step_column = step[:, h : h + 1]
+            pulled = gram * decay
+            masked = pulled * scores
+            d_scores = d_scores + pulled * step_column
+            step_intra = jnp.where(
+                lane == h, jnp.sum(masked, axis=1, keepdims=True), step_intra
+            )
+            row_sums.append(jnp.sum(masked * step_column, axis=0, keepdims=True))
+            w_high, w_low = split2(scores * decay * step_column)
+            part = part + dot_nn(w_high, own_high)
+            part = part + dot_nn(w_low, own_high)
+            part = part + dot_nn(w_high, own_low)
+        d_parts.append(part)
+    d_values = jnp.concatenate(d_parts, axis=1)
+
+    high, low = split2(d_scores)
+    d_b = dot_nn(high, c_rows) + dot_nn(low, c_rows)
+    d_c = dot_tn(high, b_rows) + dot_tn(low, b_rows)
+    d_ssd_exp = d_ssd * cum_exp
+    e_high, e_low = split2(d_ssd_exp)
+    d_c = d_c + dot_nn(e_high, s_high) + dot_nn(e_low, s_high) + dot_nn(e_high, s_low)
+    weighted = values_f * carry_weight
+    v_high, v_low = split2(weighted)
+    d_b = d_b + dot_nn(v_high, r_high) + dot_nn(v_low, r_high) + dot_nn(v_high, r_low)
+    d_bc_out[...] = jnp.concatenate([d_b, d_c], axis=1)
+
+    gather = gather_ref[...]
+    d_cum_cross = sum(dot_nn(p, gather) for p in split3(d_ssd * cross))
+    d_carry = sum(dot_nn(p, gather) for p in split3(values_f * back))
+    carry_prod = d_carry * carry
+    kept = state_ref[...] * r_now
+    kept = sum(dot_tn(gather, p) for p in split3(kept))
+    kept = jnp.sum(kept, axis=1, keepdims=True)
+    kept = jnp.transpose(jnp.broadcast_to(kept, (LANES, LANES)))[0:1]
+    d_total = jnp.exp(total) * kept + jnp.sum(carry_prod, axis=0, keepdims=True)
+    rows_t = jnp.concatenate(row_sums + [jnp.zeros((LANES - heads, CHUNK), F32)], axis=0)
+    d_cum = jnp.transpose(rows_t) - step * step_intra + d_cum_cross - carry_prod
+    last = lax.broadcasted_iota(jnp.int32, (CHUNK, LANES), 0) == CHUNK - 1
+    d_cum = d_cum + jnp.where(last, d_total, 0.0)
+    d_step_log = sum(dot_nn(upper_ref[...], p) for p in split3(d_cum))
+    d_step = step_intra + d_carry * carry_scale + d_step_log * rate
+    dt_out[0:1, :] += jnp.sum(d_step_log * step_log, axis=0, keepdims=True)
+    d_dt = d_step * sigmoid(shifted)
+    dt_out[1:2, :] += jnp.sum(d_dt, axis=0, keepdims=True)
+    d_dt_out[...] = d_dt.astype(BF)
+
+    grown = dot_tn(e_high, c_rows) + dot_tn(e_low, c_rows)
+    total_t = jnp.exp(cum_t[:, CHUNK - 1 : CHUNK])
+    for h in range(heads):
+        part = slice(h * HEAD_DIM, (h + 1) * HEAD_DIM)
+        state_grad[part, :] = total_t[h : h + 1, :] * r_now[part] + grown[part]
+
+    d_pre_now = d_values * slope_x
+    d_pre[0:CHUNK, :] = d_pre_now
+    wide_out[4:5, :] += jnp.sum(d_pre_now, axis=0, keepdims=True)
+    d_in = taps_ref[3:4, :inner] * d_pre_now
+    wide_out[3:4, :] += jnp.sum(d_pre_now * conv_in[:, :inner], axis=0, keepdims=True)
+    for k in range(3):
+        earlier = extended[5 + k : 5 + k + CHUNK, :inner]
+        wide_out[k : k + 1, :] += jnp.sum(d_pre_now * earlier, axis=0, keepdims=True)
+        d_in = d_in + taps_ref[k : k + 1, :inner] * d_pre[3 - k : 3 - k + CHUNK, :]
+    d_x_out[...] = d_in.astype(BF)
+    d_pre[CHUNK : CHUNK + 8, :] = d_pre_now[0:8, :]
+
+
+def weight_kernel(
+    index_ref, x0, x1, x2, x3, gain_ref, w_ref, d_gate_ref, d_x_ref, d_dt_ref,
+    d_normed_out, wide_out, dt_out,
+):
+    @pl.when(pl.program_id(0) == 0)
+    def _():
+        wide_out[...] = jnp.zeros(wide_out.shape, F32)
+        dt_out[...] = jnp.zeros(dt_out.shape, F32)
+
+    _, _, normed = normed_blocks((x0, x1, x2, x3), gain_ref)
+    d_wide = jnp.concatenate([d_gate_ref[...], d_x_ref[...]], axis=1)
+    d_dt = d_dt_ref[...]
+    d_all = jnp.concatenate([d_wide, d_dt], axis=1)
+    width = normed[0].shape[1]
+    for k, part in enumerate(normed):
+        rows = block_of(index_ref, k, width)
+        wide_out[rows, :] += dot_tn(part, d_wide)
+        dt_out[rows, :] += dot_tn(part, d_dt)
+        d_normed_out[:, k * width : (k + 1) * width] = dot_nn(d_all, w_ref[:, rows])
+
+
+def mixed_kernel(
+    index_ref, x0, x1, x2, x3, gain_ref, w_ref, r0, r1, r2, r3, conv_ref, before_ref, taps_ref,
+    d_normed_ref, own_out, send1, send2, send3, sums_out, grad_out, taps_out, extended, d_pre,
+):
+    step_at = pl.program_id(0)
+    chunk_at = pl.num_programs(0) - 1 - step_at
+    own = conv_ref.shape[1]
+
+    @pl.when(step_at == 0)
+    def _():
+        d_pre[CHUNK : CHUNK + 8, :] = jnp.zeros((8, own), F32)
+        grad_out[...] = jnp.zeros(grad_out.shape, F32)
+        taps_out[...] = jnp.zeros(taps_out.shape, F32)
+
+    conv_in = conv_ref[...]
+    extended[0:8, :] = jnp.where(chunk_at > 0, before_ref[...], 0.0)
+    extended[8 : 8 + CHUNK, :] = conv_in
+    pre_act = taps_ref[4:5, :] + taps_ref[3:4, :] * conv_in
+    for k in range(3):
+        pre_act = pre_act + taps_ref[k : k + 1, :] * extended[5 + k : 5 + k + CHUNK, :]
+    d_act = r0[...] + r1[...] + r2[...] + r3[...]
+    d_pre_now = d_act * silu_slope(pre_act, sigmoid(pre_act))
+    d_pre[0:CHUNK, :] = d_pre_now
+    taps_out[4:5, :] += jnp.sum(d_pre_now, axis=0, keepdims=True)
+    taps_out[3:4, :] += jnp.sum(d_pre_now * conv_in, axis=0, keepdims=True)
+    d_in = taps_ref[3:4, :] * d_pre_now
+    for k in range(3):
+        earlier = extended[5 + k : 5 + k + CHUNK, :]
+        taps_out[k : k + 1, :] += jnp.sum(d_pre_now * earlier, axis=0, keepdims=True)
+        d_in = d_in + taps_ref[k : k + 1, :] * d_pre[3 - k : 3 - k + CHUNK, :]
+    d_pre[CHUNK : CHUNK + 8, :] = d_pre_now[0:8, :]
+    d_in = d_in.astype(BF)
+
+    _, hats, normed = normed_blocks((x0, x1, x2, x3), gain_ref)
+    width = normed[0].shape[1]
+    row_dot = jnp.zeros((CHUNK, 1), F32)
+    for k, out in enumerate((own_out, send1, send2, send3)):
+        rows = block_of(index_ref, k, width)
+        grad_out[rows, :] += dot_tn(normed[k], d_in)
+        d_part = d_normed_ref[:, k * width : (k + 1) * width] + dot_nn(d_in, w_ref[:, rows])
+        out[...] = d_part.astype(out.dtype)
+        scaled_hat = hats[k] * gain_ref[k : k + 1]
+        row_dot = row_dot + jnp.sum(d_part * scaled_hat, axis=1, keepdims=True)
+    sums_out[0] = column_of_sums((row_dot,), 8)
+
+
+def final_kernel(
+    x0, x1, x2, x3, gain_ref, own_ref, r1, r2, r3, q0, q1, q2, q3, cot_ref, grad_out, gain_out
+):
+    @pl.when(pl.program_id(0) == 0)
+    def _():
+        gain_out[...] = jnp.zeros(gain_out.shape, F32)
+
+    blocks = [ref[...].astype(F32) for ref in (x0, x1, x2, x3)]
+    inverse = inverse_rms(blocks)
+    hat = blocks[0] * inverse
+    sums = q0[0] + q1[0] + q2[0] + q3[0]
+    sums = jnp.transpose(jnp.concatenate([sums, jnp.zeros((LANES - 8, CHUNK), F32)], axis=0))
+    mean = sums[:, 0:1] / (len(blocks) * hat.shape[1])
+    d_own = own_ref[...] + r1[...].astype(F32) + r2[...].astype(F32) + r3[...].astype(F32)
+    gain_out[0:1, :] += jnp.sum(d_own * hat, axis=0, keepdims=True)
+    d_hat = d_own * gain_ref[0:1]
+    grad_out[...] = cot_ref[...].astype(F32) + inverse * (d_hat - hat * mean)
+
+
+def rows_spec(width, flip=None):
+    if flip is None:
+        return pl.BlockSpec((CHUNK, width), lambda c: (c, 0))
+    return pl.BlockSpec((CHUNK, width), lambda c: (flip - 1 - c, 0))
+
+
+def before_spec(width, count):
+    ratio = CHUNK // 8
+    return pl.BlockSpec((8, width), lambda c: (jnp.maximum((count - 1 - c) * ratio - 1, 0), 0))
+
+
+def sums_spec(flip=None):
+    if flip is None:
+        return pl.BlockSpec((1, 8, CHUNK), lambda c: (c, 0, 0))
+    return pl.BlockSpec((1, 8, CHUNK), lambda c: (flip - 1 - c, 0, 0))
+
+
+def whole_spec(shape):
+    return pl.BlockSpec(shape, lambda c: (0,) * len(shape))
+
+
+SCALARS = pl.BlockSpec(memory_space=pltpu.SMEM)
+
+
+def call(kernel, name, chunks, in_specs, outs, scratch, flops, nbytes):
+    return pl.pallas_call(
+        kernel,
+        name=name,
+        grid=(chunks,),
+        in_specs=in_specs,
+        out_specs=[spec for spec, _, _ in outs],
+        out_shape=[jax.ShapeDtypeStruct(shape, kind) for _, shape, kind in outs],
+        scratch_shapes=scratch,
+        compiler_params=pltpu.CompilerParams(
+            dimension_semantics=("arbitrary",), vmem_limit_bytes=VMEM_LIMIT
+        ),
+        cost_estimate=pl.CostEstimate(flops=flops, bytes_accessed=nbytes, transcendentals=0),
+    )
+
+
+def swap(value, distance):
+    count = lax.axis_size("head")
+    return lax.ppermute(value, "head", [(i, i ^ distance) for i in range(count)])
+
+
+def shift(value, axis, distance):
+    count = lax.axis_size(axis)
+    return lax.ppermute(value, axis, [(i, (i + distance) % count) for i in range(count)])
+
+
+def pick(stack, position):
+    return lax.dynamic_index_in_dim(stack, position, 0, keepdims=False)
+
+
+def gather_small(value, me):
+    stack = jnp.stack([value] + [swap(value, k) for k in range(1, 4)])
+    return [pick(stack, jnp.bitwise_xor(me, j)) for j in range(4)]
+
+
+def to_sequences(value, z):
+    shards = lax.axis_size("seq")
+    each = value.shape[0] // shards
+    local = value.shape[1]
+    result = []
+    for s in range(each):
+        pieces = [pick(value, z * each + s)]
+        for k in range(1, shards):
+            pieces.append(shift(pick(value, lax.rem(z + k, shards) * each + s), "seq", k))
+        ordered = jnp.concatenate(pieces[::-1] * 2, axis=0)
+        start = (shards - 1 - z) * local
+        result.append(lax.dynamic_slice_in_dim(ordered, start, shards * local, 0))
+    return result
+
+
+def to_tokens(sequences, z):
+    shards = lax.axis_size("seq")
+    local = sequences[0].shape[0] // shards
+    result = []
+    for value in sequences:
+        parts = value.reshape(shards, local, value.shape[1])
+        pieces = [pick(parts, z)]
+        for k in range(1, shards):
+            pieces.append(shift(pick(parts, lax.rem(z + k, shards)), "seq", k))
+        ordered = jnp.stack(pieces[::-1] * 2)
+        result.append(lax.dynamic_slice_in_dim(ordered, shards - 1 - z, shards, 0))
+    joined = jnp.stack(result, axis=1)
+    return joined.reshape(shards * len(sequences), local, joined.shape[-1])
+
+
+def gather_features(own):
+    half = own.shape[0] // 2
+    by_x, by_y = swap(own, 1), swap(own, 2)
+    far = jnp.concatenate([swap(by_x[:half], 2), swap(by_y[half:], 1)], axis=0)
+    return [own, by_x, by_y, far]
+
+
+def line_sum(value, parts):
+    if lax.axis_size("seq") != 4:
+        return lax.psum(value, "seq")
+    z = lax.axis_index("seq")
+    inside = (z == 1) | (z == 2)
+    size = value.shape[0] // parts
+    result = []
+    for i in range(parts):
+        piece = value[i * size : (i + 1) * size]
+        joined = piece + lax.ppermute(piece, "seq", [(0, 1), (3, 2)])
+        joined = joined + lax.ppermute(joined, "seq", [(1, 2), (2, 1)])
+        result.append(jnp.where(inside, joined, lax.ppermute(joined, "seq", [(1, 0), (2, 3)])))
+    return jnp.concatenate(result, axis=0)
+
+
+def core_sum(value, parts):
+    if lax.axis_size("dp") != 2:
+        return line_sum(lax.psum(value, "dp"), parts)
+    core = lax.axis_index("dp")
+    half = value.shape[0] // 2
+    keep = lax.dynamic_slice_in_dim(value, core * half, half, 0)
+    give = lax.dynamic_slice_in_dim(value, (1 - core) * half, half, 0)
+    mine = line_sum(keep + shift(give, "dp", 1), parts)
+    other = shift(mine, "dp", 1)
+    ordered = jnp.concatenate([other, mine, other], axis=0)
+    return lax.dynamic_slice_in_dim(ordered, (1 - core) * half, 2 * half, 0)
+
+
+def on_device(
+    hidden_in, norm_gain, w_z, w_x, w_bc, w_dt, conv_x, conv_x_bias, conv_bc, conv_bc_bias,
+    dt_bias, a_log, skip, gate_gain, w_out, out_grad,
+):
+    shards = lax.axis_size("seq")
+    z, me = lax.axis_index("seq"), lax.axis_index("head")
+    length = hidden_in.shape[1] * shards
+    part_width = hidden_in.shape[2]
+    full_width = w_z.shape[0]
+    inner = w_x.shape[1]
+    heads = dt_bias.shape[0]
+    bc_here = w_bc.shape[1]
+    each = hidden_in.shape[0] // shards
+    chunks = length // CHUNK
+    conv_width = inner + 2 * STATE
+    tail_width = conv_width + LANES
+    index = jnp.bitwise_xor(me, jnp.arange(4, dtype=jnp.int32))
+
+    tokens = [gather_features(part) for part in to_sequences(hidden_in, z)]
+
+    packed = jnp.concatenate([w_bc, norm_gain.reshape(-1, bc_here)], axis=0)
+    packed = gather_small(packed, me)
+    w_bc_all = jnp.concatenate([part[:full_width] for part in packed], axis=1)
+    gain_all = jnp.stack([part[full_width:].reshape(-1) for part in packed]).astype(F32)
+    gain_here = jnp.stack([pick(gain_all, index[k]) for k in range(4)])
+    taps_bc_own = jnp.concatenate([conv_bc, conv_bc_bias[None], jnp.zeros((3, bc_here), F32)])
+    taps_bc = jnp.concatenate(gather_small(taps_bc_own, me), axis=1)
+    taps_x = jnp.concatenate([conv_x, conv_x_bias[None], jnp.zeros((3, inner), F32)])
+    taps = jnp.concatenate([taps_x, taps_bc], axis=1)
+    w_dt_wide = jnp.pad(w_dt, ((0, 0), (0, LANES - heads)))
+    w_all = jnp.concatenate([w_z, w_x, w_bc_all, w_dt_wide], axis=1)
+    w_back = jnp.concatenate([w_z, w_x, w_dt_wide], axis=1).T
+    w_bc_back = w_bc.T
+    w_out_back = w_out.T
+    dt_params = jnp.pad(jnp.stack([dt_bias, a_log]), ((0, 6), (0, LANES - heads)))
+    skip_wide = jnp.repeat(skip, HEAD_DIM)[None]
+    gate_wide = gate_gain[None]
+    owner = jnp.arange(inner) // HEAD_DIM
+    spread = (jnp.arange(LANES)[:, None] == owner[None, :]).astype(BF)
+    collect = (owner[:, None] == jnp.arange(LANES)[None, :]).astype(BF)
+    order = jnp.arange(CHUNK)
+    lower = (order[:, None] >= order[None, :]).astype(BF)
+    upper = (order[:, None] <= order[None, :]).astype(BF)
+
+    x_specs = [rows_spec(part_width)] * 4
+    x_flipped = [rows_spec(part_width, chunks)] * 4
+    gain_spec = whole_spec((4, part_width))
+    rows_inner = rows_spec(inner)
+
+    forward = call(
+        forward_kernel,
+        "forward_scan",
+        chunks,
+        [SCALARS] + x_specs + [
+            whole_spec(w_all.shape), gain_spec, whole_spec(taps.shape), whole_spec((8, LANES)),
+            whole_spec((1, inner)), whole_spec(spread.shape), whole_spec(lower.shape),
+        ],
+        [
+            (rows_inner, (length, inner), F32),
+            (rows_spec(tail_width), (length, tail_width), F32),
+            (rows_inner, (length, inner), F32),
+            (pl.BlockSpec((None, inner, STATE), lambda c: (c, 0, 0)), (chunks, inner, STATE), F32),
+        ],
+        [pltpu.VMEM((CHUNK + 8, conv_width), F32), pltpu.VMEM((inner, STATE), F32)],
+        8 * 10**9, 2 * 10**7,
+    )
+    ahead = [
+        forward(index, *x, w_all, gain_here, taps, dt_params, skip_wide, spread, lower)
+        for x in tokens
+    ]
+    cotangents = [gather_features(part) for part in to_sequences(out_grad, z)]
+
+    score = call(
+        score_kernel,
+        "gate_sums",
+        chunks,
+        [SCALARS] + x_specs + [
+            whole_spec(w_out_back.shape), rows_inner, rows_inner, whole_spec((1, inner)),
+        ],
+        [(rows_inner, (length, inner), F32), (sums_spec(), (chunks, 8, CHUNK), F32)],
+        [],
+        2 * 10**9, 10**7,
+    )
+    scored = []
+    for (gate, _, ssd, _), g in zip(ahead, cotangents):
+        d_scaled, sums = score(index, *g, w_out_back, ssd, gate, gate_wide)
+        scored.append((d_scaled, [sums] + [swap(sums, k) for k in range(1, 4)]))
+
+    flipped = rows_spec(inner, chunks)
+    backward = call(
+        functools.partial(backward_kernel, inner * lax.axis_size("head")),
+        "backward_scan",
+        chunks,
+        [SCALARS] + [sums_spec(chunks)] * 4 + [
+            flipped, flipped, flipped, rows_spec(tail_width, chunks),
+            before_spec(tail_width, chunks),
+            pl.BlockSpec((None, inner, STATE), lambda c: (chunks - 1 - c, 0, 0)),
+            whole_spec((1, inner)), whole_spec(taps.shape), whole_spec((8, LANES)),
+            whole_spec((1, inner)), whole_spec(spread.shape), whole_spec(collect.shape),
+            whole_spec(lower.shape), whole_spec(upper.shape),
+        ],
+        [
+            (flipped, (length, inner), BF),
+            (flipped, (length, inner), BF),
+            (flipped, (length, inner), BF),
+            (rows_spec(LANES, chunks), (length, LANES), BF),
+            (rows_spec(2 * STATE, chunks), (length, 2 * STATE), F32),
+            (whole_spec((8, inner)), (8, inner), F32),
+            (whole_spec((8, LANES)), (8, LANES), F32),
+        ],
+        [
+            pltpu.VMEM((CHUNK + 8, conv_width), F32),
+            pltpu.VMEM((CHUNK + 8, inner), F32),
+            pltpu.VMEM((inner, STATE), F32),
+        ],
+        12 * 10**9, 2 * 10**7,
+    )
+    weigh = call(
+        weight_kernel,
+        "weight_sums",
+        chunks,
+        [SCALARS] + x_specs + [
+            gain_spec, whole_spec(w_back.shape), rows_inner, rows_inner, rows_spec(LANES),
+        ],
+        [
+            (rows_spec(full_width), (length, full_width), F32),
+            (whole_spec((full_width, 2 * inner)), (full_width, 2 * inner), F32),
+            (whole_spec((full_width, LANES)), (full_width, LANES), F32),
+        ],
+        [],
+        9 * 10**9, 2 * 10**7,
+    )
+    mix = call(
+        mixed_kernel,
+        "input_sums",
+        chunks,
+        [SCALARS] + x_flipped + [gain_spec, whole_spec(w_bc_back.shape)]
+        + [rows_spec(bc_here, chunks)] * 5
+        + [before_spec(bc_here, chunks), whole_spec((8, bc_here)), rows_spec(full_width, chunks)],
+        [
+            (rows_spec(part_width, chunks), (length, part_width), F32),
+            (rows_spec(part_width, chunks), (length, part_width), BF),
+            (rows_spec(part_width, chunks), (length, part_width), BF),
+            (rows_spec(part_width, chunks), (length, part_width), BF),
+            (sums_spec(chunks), (chunks, 8, CHUNK), F32),
+            (whole_spec((full_width, bc_here)), (full_width, bc_here), F32),
+            (whole_spec((8, bc_here)), (8, bc_here), F32),
+        ],
+        [pltpu.VMEM((CHUNK + 8, bc_here), F32), pltpu.VMEM((CHUNK + 8, bc_here), F32)],
+        10**9, 2 * 10**7,
+    )
+    finish = call(
+        final_kernel,
+        "input_gradient",
+        chunks,
+        x_specs + [gain_spec] + [rows_spec(part_width)] * 4 + [sums_spec()] * 4
+        + [rows_spec(part_width)],
+        [
+            (rows_spec(part_width), (length, part_width), F32),
+            (whole_spec((8, part_width)), (8, part_width), F32),
+        ],
+        [],
+        10**8, 10**7,
+    )
+
+    largest = jnp.max(jnp.abs(w_out.astype(F32)))
+    largest = functools.reduce(jnp.maximum, gather_small(largest[None], me))
+    out_scale = 16.0 / jnp.maximum(largest[0], 1e-30)
+    w_out_parts = [
+        lax.dynamic_slice_in_dim(w_out, index[k] * part_width, part_width, 1) for k in range(4)
+    ]
+
+    totals = None
+    block_parts, grad_parts = [], []
+    for s in range(each):
+        x, g = tokens[s], cotangents[s]
+        gate, conv, ssd, states = ahead[s]
+        d_scaled, sums = scored[s]
+        scaled, d_gate, d_x, d_dt, d_bc, wide, dt_sums = backward(
+            index, *sums, ssd, gate, d_scaled, conv, conv, states, gate_wide, taps, dt_params,
+            skip_wide, spread, collect, lower, upper,
+        )
+        d_bc_parts = [
+            lax.dynamic_slice_in_dim(d_bc, index[k] * bc_here, bc_here, 1) for k in range(4)
+        ]
+        d_bc_parts = [d_bc_parts[0]] + [swap(d_bc_parts[k], k) for k in range(1, 4)]
+
+        out_parts = [jnp.dot(scaled, part, preferred_element_type=F32) for part in w_out_parts]
+        received = [
+            swap((out_parts[k] * out_scale).astype(jnp.float16), k) for k in range(1, 4)
+        ]
+        block = x[0].astype(F32) + out_parts[0]
+        block = block + sum(part.astype(F32) for part in received) / out_scale
+        block_parts.append(block.astype(BF))
+        g_w_out = jnp.stack(
+            [
+                lax.dot_general(scaled, part, (((0,), (0,)), ((), ())), preferred_element_type=F32)
+                for part in g
+            ]
+        )
+
+        d_normed, g_wide, g_dt = weigh(index, *x, gain_here, w_back, d_gate, d_x, d_dt)
+        conv_own = lax.dynamic_slice_in_dim(conv, inner + me * bc_here, bc_here, 1)
+        own, send1, send2, send3, dots, g_bc, taps_sums = mix(
+            index, *x, gain_here, w_bc_back, *d_bc_parts, conv_own, conv_own, taps_bc_own, d_normed
+        )
+        dots = [dots] + [swap(dots, k) for k in range(1, 4)]
+        grad, gain_sums = finish(
+            *x, gain_here, own, swap(send1, 1), swap(send2, 2), swap(send3, 3), *dots, g[0]
+        )
+        grad_parts.append(grad)
+        now = (g_w_out, g_wide, g_dt[:, :heads], g_bc, wide, dt_sums, taps_sums, gain_sums[0:1])
+        totals = now if totals is None else jax.tree.map(jnp.add, totals, now)
+
+    g_w_out, g_wide, g_dt, g_bc, wide, dt_sums, taps_sums, gain_sums = totals
+    g_w_out = core_sum(g_w_out.reshape(4 * inner, part_width), 2).reshape(4, inner, part_width)
+    g_wide = core_sum(g_wide, 4)
+    g_rest = core_sum(jnp.concatenate([g_bc, g_dt], axis=1), 1)
+    wide, dt_sums, taps_sums, gain_sums = lax.psum(
+        (wide, dt_sums, taps_sums, gain_sums), ("seq", "dp")
+    )
+    g_w_out = jnp.concatenate([pick(g_w_out, index[j]) for j in range(4)], axis=1)
+    return (
+        to_tokens(block_parts, z),
+        to_tokens(grad_parts, z),
+        gain_sums[0],
+        g_wide[:, :inner],
+        g_wide[:, inner:],
+        g_rest[:, :bc_here],
+        g_rest[:, bc_here:],
+        wide[0:4],
+        wide[4],
+        taps_sums[0:4],
+        taps_sums[4],
+        dt_sums[1, :heads],
+        dt_sums[0, :heads],
+        wide[6].reshape(heads, HEAD_DIM).sum(axis=1),
+        wide[5],
+        g_w_out,
+    )
+
+
+def fits(mesh, seqs, length):
+    shards = mesh.shape["seq"]
+    local_seqs = seqs // mesh.shape["dp"]
+    return mesh.shape["head"] == 4 and local_seqs % shards == 0 and length % CHUNK == 0
+
+
 def solution(mesh):
     in_specs = (
         P("dp", "seq", "head"),
@@ -319,6 +1098,12 @@
         P("head"),
         P("head", None),
     )
-    return jax.shard_map(
-        on_device, mesh=mesh, in_specs=in_specs, out_specs=out_specs, check_vma=False
-    )
+
+    def run(*args):
+        seqs, length, _ = args[0].shape
+        body = on_device if fits(mesh, seqs, length) else on_device_general
+        return jax.shard_map(
+            body, mesh=mesh, in_specs=in_specs, out_specs=out_specs, check_vma=False
+        )(*args)
+
+    return run

time: 1020 us -> 747 us (0.73)
  waiting for transfers between devices: 540 us -> 271 us
  Pallas kernels: 0 us -> 150 us
  starting transfers between devices: 5.26 us -> 141 us
  matrix products: 139 us -> 25.8 us
  other arithmetic: 106 us -> 40.6 us
  blocking collectives: 82.3 us -> 26.5 us
  local copies, waits for them, and re-layouts: 121 us -> 67.2 us
    all_gather x5 -> x0, waiting for transfers between devices: 303 us -> none  [the longest x2 243 us: prefix(): pieces = jax.tree.map(lambda part: lax.all_gather(part, axis), value)]
    ppermute x2 -> x106, waiting for transfers between devices: 0.01 us -> 271 us  [the longest x30 81.7 us: shift(): lax.ppermute(value, axis, [(i, (i + distance) % count) for i in range(cou...]
    pallas_call x0 -> x12, Pallas kernels: none -> 150 us  [the longest x2 54.9 us: on_device(): backward(index, *sums, ssd, gate, d_scaled, conv, conv, states, gate_wide...]
    ppermute x2 -> x106, starting transfers between devices: 4.68 us -> 141 us  [the longest x55 69.5 us: swap(): lax.ppermute(value, 'head', [(i, i ^ distance) for i in range(count)])]
    reduce_scatter x3 -> x0, waiting for transfers between devices: 123 us -> none  [the longest x1 77.6 us: on_device(): lax.psum_scatter(lax.dot_general(w_cat, d_proj, (((1,), (1,)), ((), ())),...]
    dot_general x18 -> x16, matrix products: 139 us -> 25.8 us  [the longest x8 15.4 us: on_device(): lax.dot_general(scaled, part, (((0,), (0,)), ((), ())), preferred_element...]
    psum x1 -> x0, waiting for transfers between devices: 113 us -> none  [on_device(): lax.psum((g_norm_gain, g_w_cat, g_kernel, g_kernel_bias, g_dt_bias, g_a_l...]
    reduce_sum x10 -> x1, other arithmetic: 46.2 us -> 0.63 us  [on_device(): wide[6].reshape(heads, HEAD_DIM).sum(axis=1)]
  transfers between devices with their start and end apart: 11 -> 106, of which waited for: 8 -> 34; matrix products, arithmetic and copies ran while one was open for 21% -> 14% of each run, Pallas kernels for 0% -> 17%
where the time goes in v1:
time: 747 us; the launch traced here: 741 us
  waiting for transfers between devices  271 us (36%)
  Pallas kernels  150 us (20%)
  starting transfers between devices  141 us (19%)
  local copies, waits for them, and re-layouts  67.2 us (9%)
  other arithmetic  40.6 us (5%)
  blocking collectives  26.5 us (4%)
  matrix products  25.8 us (3%)
  between operations  18.8 us (3%)
    ppermute x30, waiting for transfers between devices, shift(): lax.ppermute(value, axis, [(i, (i + distance) % count) for i in range(cou...  81.7 us
    ppermute x55, starting transfers between devices, swap(): lax.ppermute(value, 'head', [(i, i ^ distance) for i in range(count)])  69.5 us
    ppermute x7, waiting for transfers between devices, line_sum(): lax.ppermute(joined, 'seq', [(1, 0), (2, 3)])  69.4 us
    ppermute x55, waiting for transfers between devices, swap(): lax.ppermute(value, 'head', [(i, i ^ distance) for i in range(count)])  66.4 us
    pallas_call x2, Pallas kernels, on_device(): backward(index, *sums, ssd, gate, d_scaled, conv, conv, states, gate_wide...  54.9 us
    ppermute x7, waiting for transfers between devices, line_sum(): joined = piece + lax.ppermute(piece, 'seq', [(0, 1), (3, 2)])  53.4 us
    ppermute x30, starting transfers between devices, shift(): lax.ppermute(value, axis, [(i, (i + distance) % count) for i in range(cou...  44.4 us
    pallas_call x2, Pallas kernels, on_device(): forward(index, *x, w_all, gain_here, taps, dt_params, skip_wide, spread,...  32.8 us
  transfers between devices with their start and end apart: 106, of which 34 were waited for; matrix products, arithmetic and copies ran while one was open for 14% of the time, Pallas kernels for 17%

profile of v1, /device:TPU:0, one launch (start us, length us, event | category | flops | bytes accessed | tf_op | source)
XLA Modules:
  0.0 740.7 jit_solution(13484981246583190548)
XLA Ops:
  2.8 3.9 collective-permute-start.25
  65.2 5.1 collective-permute-start.5
  70.4 3.8 collective-permute-done.5
  75.5 5.3 collective-permute-done
  80.8 4.1 collective-permute-start.33
  87.0 6.6 collective-permute-done.35
  99.6 3.8 collective-permute-start.34
  109.5 5.9 collective-permute-start.10
  121.8 17.6 %collective-permute-done.16 = bf16[1028,64]{1,0:T(8,128)(2,1)S(1)} collective-permute-done((bf16[1028,64]{1,0:T(8,128)(2,1)}, bf16[1028,64]{1,0:T(8,128)(2,1)S(1)}, u32[]{:S(2)}, u32[]{:S(2)}) %collective-permute-start.16) | collective-permute-done | bytes 131616 | tf_op jit(solution)/shard_map/ppermute | solution.py:734
  156.2 5.9 concatenate.70.w_ref
  172.5 16.4 %forward_scan.3 = (f32[1024,512]{1,0:T(8,128)}, f32[1024,896]{1,0:T(8,128)}, f32[1024,512]{1,0:T(8,128)}, f32[4,512,128]{2,1,0:T(8,128)}) custom-call(s32[4]{0:T(128)} %copy-done.67, bf16[1024,256]{1,0:T(8,128)(2,1)} %copy-done.4, bf16[1024,256]{1,0:T(8,128)(2,1)} %copy-done.17, bf16[1024,256]{1,0:T(8,128)(2,1)} %collective-permute-done.43.x2, ...), custom_call_target="tpu_custom_call" | custom-call | flops 8000000000 | bytes 20000000 | tf_op jit(solution)/shard_map/forward_scan/pallas_call | solution.py:883
  190.9 6.1 gate_sums.3
  201.5 16.4 %forward_scan.2 = (f32[1024,512]{1,0:T(8,128)}, f32[1024,896]{1,0:T(8,128)}, f32[1024,512]{1,0:T(8,128)}, f32[4,512,128]{2,1,0:T(8,128)}) custom-call(s32[4]{0:T(128)} %copy-done.67, bf16[1024,256]{1,0:T(8,128)(2,1)} %copy-done.3, bf16[1024,256]{1,0:T(8,128)(2,1)} %copy-done.15, bf16[1024,256]{1,0:T(8,128)(2,1)} %copy-done.14, bf16[1024,256]{1,0:T(8,128)(2,1)} %copy-done.20, ...), custom_call_target="tpu_custom_call" | custom-call | flops 8000000000 | bytes 20000000 | tf_op jit(solution)/shard_map/forward_scan/pallas_call | solution.py:883
  218.8 6.1 gate_sums.2
  233.3 27.4 %backward_scan.3 = (bf16[1024,512]{1,0:T(8,128)(2,1)}, bf16[1024,512]{1,0:T(8,128)(2,1)}, bf16[1024,512]{1,0:T(8,128)(2,1)}, bf16[1024,128]{1,0:T(8,128)(2,1)}, ...) custom-call(s32[4]{0:T(128)} %copy-done.67, f32[4,8,256]{2,1,0:T(8,128)} %get-tuple-element.75.q0, ...), custom_call_target="tpu_custom_call" | custom-call | flops 12000000000 | bytes 20000000 | tf_op jit(solution)/shard_map/backward_scan/pallas_call | solution.py:994
  265.4 27.6 %backward_scan.2 = (bf16[1024,512]{1,0:T(8,128)(2,1)}, bf16[1024,512]{1,0:T(8,128)(2,1)}, bf16[1024,512]{1,0:T(8,128)(2,1)}, bf16[1024,128]{1,0:T(8,128)(2,1)}, ...) custom-call(s32[4]{0:T(128)} %copy-done.67, f32[4,8,256]{2,1,0:T(8,128)} %get-tuple-element.68.q0, ...), custom_call_target="tpu_custom_call" | custom-call | flops 12000000000 | bytes 20000000 | tf_op jit(solution)/shard_map/backward_scan/pallas_call | solution.py:994
  319.1 12.7 %weight_sums.3 = (f32[1024,1024]{1,0:T(8,128)}, f32[1024,1024]{1,0:T(8,128)}, f32[1024,128]{1,0:T(8,128)}) custom-call(s32[4]{0:T(128)} %copy-done.67, bf16[1024,256]{1,0:T(8,128)(2,1)} %copy-done.4, bf16[1024,256]{1,0:T(8,128)(2,1)} %copy-done.17, bf16[1024,256]{1,0:T(8,128)(2,1)} %collective-permute-done.43.x2, bf16[1024,256]{1,0:T(8,128)(2,1)} %copy-done.19, ...), custom_call_target="tpu_custom_call" | custom-call | flops 8999999488 | bytes 20000000 | tf_op jit(solution)/shard_map/weight_sums/pallas_call | solution.py:1017
  331.9 12.6 %weight_sums.2 = (f32[1024,1024]{1,0:T(8,128)}, f32[1024,1024]{1,0:T(8,128)}, f32[1024,128]{1,0:T(8,128)}) custom-call(s32[4]{0:T(128)} %copy-done.67, bf16[1024,256]{1,0:T(8,128)(2,1)} %copy-done.3, bf16[1024,256]{1,0:T(8,128)(2,1)} %copy-done.15, bf16[1024,256]{1,0:T(8,128)(2,1)} %copy-done.14, bf16[1024,256]{1,0:T(8,128)(2,1)} %copy-done.20, ...), custom_call_target="tpu_custom_call" | custom-call | flops 8999999488 | bytes 20000000 | tf_op jit(solution)/shard_map/weight_sums/pallas_call | solution.py:1017
  356.6 7.4 input_sums.3
  367.3 7.4 input_sums.2
  386.1 19.4 %collective-permute-done.27 = f16[1024,256]{1,0:T(8,128)(2,1)S(1)} collective-permute-done((f16[1024,256]{1,0:T(8,128)(2,1)S(1)}, f16[1024,256]{1,0:T(8,128)(2,1)S(1)}, u32[]{:S(2)}, u32[]{:S(2)}) %collective-permute-start.27) | collective-permute-done | bytes 524320 | tf_op jit(solution)/shard_map/ppermute | solution.py:734
  408.6 4.9 collective-permute-done.94
  414.9 4.3 collective-permute-start.29
  422.8 5.9 collective-permute-done.53
  430.7 7.0 collective-permute-done.54
  437.7 5.9 collective-permute-done.30
  444.0 6.4 collective-permute-done.31
  454.6 9.7 %collective-permute-done.63.q3 = f32[4,8,256]{2,1,0:T(8,128)S(1)} collective-permute-done((f32[4,8,256]{2,1,0:T(8,128)S(1)}, f32[4,8,256]{2,1,0:T(8,128)S(1)}, u32[]{:S(2)}, u32[]{:S(2)}) %collective-permute-start.63) | collective-permute-done | bytes 32800 | tf_op jit(solution)/shard_map/ppermute | solution.py:734
  469.1 8.4 %collective-permute-done.71.r2 = bf16[1024,256]{1,0:T(8,128)(2,1)S(1)} collective-permute-done((bf16[1024,256]{1,0:T(8,128)(2,1)S(1)}, bf16[1024,256]{1,0:T(8,128)(2,1)S(1)}, u32[]{:S(2)}, u32[]{:S(2)}) %collective-permute-start.71) | collective-permute-done | bytes 524320 | tf_op jit(solution)/shard_map/ppermute | solution.py:734
  481.2 5.0 input_gradient.3
  486.1 7.6 %collective-permute-done.62.q2 = f32[4,8,256]{2,1,0:T(8,128)S(1)} collective-permute-done((f32[4,8,256]{2,1,0:T(8,128)S(1)}, f32[4,8,256]{2,1,0:T(8,128)S(1)}, u32[]{:S(2)}, u32[]{:S(2)}) %collective-permute-start.62) | collective-permute-done | bytes 32800 | tf_op jit(solution)/shard_map/ppermute | solution.py:734
  496.6 5.1 input_gradient.2
  502.4 26.5 %all-reduce.2 = (f32[256]{0:T(256)}, f32[8,512]{1,0:T(8,128)S(1)}, f32[8,64]{1,0:T(8,128)S(1)}, f32[8,128]{1,0:T(8,128)S(1)}) all-reduce(f32[256]{0:T(256)S(1)} %bitcast.239, f32[8,512]{1,0:T(8,128)S(1)} %add.416, f32[8,64]{1,0:T(8,128)S(1)} %add.417, f32[8,128]{1,0:T(8,128)S(1)} %add.418), channel_id=1, replica_groups=mesh['seq'=4,'dp'=2,'head'=4] {'seq','dp'}, use_global_device_ids=true, to_apply=%region_1.2 | all-reduce | flops 5888 | bytes 47104 | tf_op jit(solution)/shard_map/psum | solution.py:1034
  531.1 3.8 collective-permute-start.76
  543.6 11.1 %collective-permute-done.77 = f32[256,256]{1,0:T(8,128)} collective-permute-done((f32[256,256]{1,0:T(8,128)}, f32[256,256]{1,0:T(8,128)}, u32[]{:S(2)}, u32[]{:S(2)}) %collective-permute-start.77) | collective-permute-done | bytes 262176 | tf_op jit(solution)/shard_map/ppermute | solution.py:739
  569.3 4.5 collective-permute-done.99
  573.8 4.4 collective-permute-start.83
  578.2 6.8 collective-permute-done.102
  587.6 8.6 %collective-permute-done.80 = f32[128,1024]{1,0:T(8,128)S(1)} collective-permute-done((f32[128,1024]{1,0:T(8,128)S(1)}, f32[128,1024]{1,0:T(8,128)S(1)}, u32[]{:S(2)}, u32[]{:S(2)}) %collective-permute-start.80) | collective-permute-done | bytes 524320 | tf_op jit(solution)/shard_map/ppermute | solution.py:797
  598.9 8.6 %collective-permute-done.89 = f32[128,1024]{1,0:T(8,128)S(1)} collective-permute-done((f32[128,1024]{1,0:T(8,128)S(1)}, f32[128,1024]{1,0:T(8,128)S(1)}, u32[]{:S(2)}, u32[]{:S(2)}) %collective-permute-start.89) | collective-permute-done | bytes 524320 | tf_op jit(solution)/shard_map/ppermute | solution.py:797
  609.2 9.6 %collective-permute-done.86 = f32[128,1024]{1,0:T(8,128)S(1)} collective-permute-done((f32[128,1024]{1,0:T(8,128)S(1)}, f32[128,1024]{1,0:T(8,128)S(1)}, u32[]{:S(2)}, u32[]{:S(2)}) %collective-permute-start.86) | collective-permute-done | bytes 524320 | tf_op jit(solution)/shard_map/ppermute | solution.py:797
  619.4 10.5 %collective-permute-done.83 = f32[128,1024]{1,0:T(8,128)S(1)} collective-permute-done((f32[128,1024]{1,0:T(8,128)S(1)}, f32[128,1024]{1,0:T(8,128)S(1)}, u32[]{:S(2)}, u32[]{:S(2)}) %collective-permute-start.83) | collective-permute-done | bytes 524320 | tf_op jit(solution)/shard_map/ppermute | solution.py:797
  631.1 15.1 %collective-permute-done.64 = f32[256,256]{1,0:T(8,128)S(1)} collective-permute-done((f32[256,256]{1,0:T(8,128)S(1)}, f32[256,256]{1,0:T(8,128)S(1)}, u32[]{:S(2)}, u32[]{:S(2)}) %collective-permute-start.64) | collective-permute-done | bytes 262176 | tf_op jit(solution)/shard_map/ppermute | solution.py:739
  653.6 10.0 %collective-permute-done.101 = f32[512,256]{1,0:T(8,128)S(1)} collective-permute-done((f32[512,256]{1,0:T(8,128)S(1)}, f32[512,256]{1,0:T(8,128)S(1)}, u32[]{:S(2)}, u32[]{:S(2)}) %collective-permute-start.101) | collective-permute-done | bytes 524320 | tf_op jit(solution)/shard_map/ppermute | solution.py:799
  667.9 16.6 %collective-permute-done.82 = f32[128,1024]{1,0:T(8,128)S(1)} collective-permute-done((f32[128,1024]{1,0:T(8,128)S(1)}, f32[128,1024]{1,0:T(8,128)S(1)}, u32[]{:S(2)}, u32[]{:S(2)}) %collective-permute-start.82) | collective-permute-done | bytes 524320 | tf_op jit(solution)/shard_map/ppermute | solution.py:799
  684.6 23.6 %collective-permute-done.85 = f32[128,1024]{1,0:T(8,128)S(1)} collective-permute-done((f32[128,1024]{1,0:T(8,128)S(1)}, f32[128,1024]{1,0:T(8,128)S(1)}, u32[]{:S(2)}, u32[]{:S(2)}) %collective-permute-start.85) | collective-permute-done | bytes 524320 | tf_op jit(solution)/shard_map/ppermute | solution.py:799
  708.3 11.2 %collective-permute-done.88 = f32[128,1024]{1,0:T(8,128)S(1)} collective-permute-done((f32[128,1024]{1,0:T(8,128)S(1)}, f32[128,1024]{1,0:T(8,128)S(1)}, u32[]{:S(2)}, u32[]{:S(2)}) %collective-permute-start.88) | collective-permute-done | bytes 524320 | tf_op jit(solution)/shard_map/ppermute | solution.py:799
  719.5 8.0 %collective-permute-done.91 = f32[128,1024]{1,0:T(8,128)S(1)} collective-permute-done((f32[128,1024]{1,0:T(8,128)S(1)}, f32[128,1024]{1,0:T(8,128)S(1)}, u32[]{:S(2)}, u32[]{:S(2)}) %collective-permute-start.91) | collective-permute-done | bytes 524320 | tf_op jit(solution)/shard_map/ppermute | solution.py:799
  (574 shorter events, 251.6 us)
Async XLA Ops:
  2.8 42.7 %collective-permute-start.25 = (f32[1]{0:T(128)}, f32[1]{0:T(128)}, u32[]{:S(2)}, u32[]{:S(2)}) collective-permute-start(f32[1]{0:T(128)} %bitcast.35), channel_id=1, source_target_pairs={{0,3},{1,2},{2,1},{3,0},{4,7},{5,6},{6,5},{7,4},{8,11},{9,10},{10,... | collective-permute-start | bytes 20 | tf_op jit(solution)/shard_map/ppermute | solution.py:734
  6.7 38.9 %collective-permute-start.24 = (f32[1]{0:T(128)}, f32[1]{0:T(128)}, u32[]{:S(2)}, u32[]{:S(2)}) collective-permute-start(f32[1]{0:T(128)} %bitcast.35), channel_id=1, source_target_pairs={{0,2},{1,3},{2,0},{3,1},{4,6},{5,7},{6,4},{7,5},{8,10},{9,11},{10,... | collective-permute-start | bytes 20 | tf_op jit(solution)/shard_map/ppermute | solution.py:734
  7.2 40.4 %collective-permute-start.23 = (f32[1]{0:T(128)}, f32[1]{0:T(128)}, u32[]{:S(2)}, u32[]{:S(2)}) collective-permute-start(f32[1]{0:T(128)} %bitcast.35), channel_id=1, source_target_pairs={{0,1},{1,0},{2,3},{3,2},{4,5},{5,4},{6,7},{7,6},{8,9},{9,8},{10,11... | collective-permute-start | bytes 20 | tf_op jit(solution)/shard_map/ppermute | solution.py:734
  8.7 46.2 %collective-permute-start.19 = (f32[8,64]{1,0:T(8,128)S(1)}, f32[8,64]{1,0:T(8,128)}, u32[]{:S(2)}, u32[]{:S(2)}) collective-permute-start(f32[8,64]{1,0:T(8,128)S(1)} %get-tuple-element.230.taps_ref), channel_id=1, source_target_pairs={{0,3},{1,2},{2,1},{3,0},{4,7},{5,6},{6,5},{7,4},{8,11},{9,10},{10,... | collective-permute-start | bytes 6152 | tf_op jit(solution)/shard_map/ppermute | solution.py:734
  11.6 45.0 %collective-permute-start.18 = (f32[8,64]{1,0:T(8,128)S(1)}, f32[8,64]{1,0:T(8,128)}, u32[]{:S(2)}, u32[]{:S(2)}) collective-permute-start(f32[8,64]{1,0:T(8,128)S(1)} %get-tuple-element.230.taps_ref), channel_id=1, source_target_pairs={{0,2},{1,3},{2,0},{3,1},{4,6},{5,7},{6,4},{7,5},{8,10},{9,11},{10,... | collective-permute-start | bytes 6152 | tf_op jit(solution)/shard_map/ppermute | solution.py:734
  45.6 70.9 %collective-permute-start.15 = (bf16[1028,64]{1,0:T(8,128)(2,1)}, bf16[1028,64]{1,0:T(8,128)(2,1)S(1)}, u32[]{:S(2)}, u32[]{:S(2)}) collective-permute-start(bf16[1028,64]{1,0:T(8,128)(2,1)} %get-tuple-element.215), channel_id=1, source_target_pairs={{0,2},{1,3},{2,0},{3,1},{4,6},{5,7},{6,4},{7,5},{8,10},{9,11},{10,... | collective-permute-start | bytes 394760 | tf_op jit(solution)/shard_map/ppermute | solution.py:734
  47.6 72.3 %collective-permute-start.14 = (bf16[1028,64]{1,0:T(8,128)(2,1)}, bf16[1028,64]{1,0:T(8,128)(2,1)}, u32[]{:S(2)}, u32[]{:S(2)}) collective-permute-start(bf16[1028,64]{1,0:T(8,128)(2,1)} %get-tuple-element.215), channel_id=1, source_target_pairs={{0,1},{1,0},{2,3},{3,2},{4,5},{5,4},{6,7},{7,6},{8,9},{9,8},{10,11... | collective-permute-start | bytes 394760 | tf_op jit(solution)/shard_map/ppermute | solution.py:734
  55.0 31.8 %collective-permute-start.2 = (bf16[256,256]{1,0:T(8,128)(2,1)S(1)}, bf16[256,256]{1,0:T(8,128)(2,1)S(1)}, u32[]{:S(2)}, u32[]{:S(2)}) collective-permute-start(bf16[256,256]{1,0:T(8,128)(2,1)S(1)} %copy-done.55), channel_id=1, source_target_pairs={{0,8},{8,16},{16,24},{24,0},{1,9},{9,17},{17,25},{25,1},{2,10},{10... | collective-permute-start | bytes 393224 | tf_op jit(solution)/shard_map/ppermute | solution.py:739
  108.9 32.5 %collective-permute-start.11 = (bf16[1024,256]{1,0:T(8,128)(2,1)S(1)}, bf16[1024,256]{1,0:T(8,128)(2,1)S(1)}, u32[]{:S(2)}, u32[]{:S(2)}) collective-permute-start(bf16[1024,256]{1,0:T(8,128)(2,1)S(1)} %constant_dynamic-slice_fusion.32.x0), channel_id=1, source_target_pairs={{0,2},{1,3},{2,0},{3,1},{4,6},{5,7},{6,4},{7,5},{8,10},{9,11},{10,... | collective-permute-start | bytes 1572872 | tf_op jit(solution)/shard_map/ppermute | solution.py:734
  109.5 34.8 %collective-permute-start.10 = (bf16[1024,256]{1,0:T(8,128)(2,1)S(1)}, bf16[1024,256]{1,0:T(8,128)(2,1)S(1)}, u32[]{:S(2)}, u32[]{:S(2)}) collective-permute-start(bf16[1024,256]{1,0:T(8,128)(2,1)S(1)} %constant_dynamic-slice_fusion.32.x0), channel_id=1, source_target_pairs={{0,1},{1,0},{2,3},{3,2},{4,5},{5,4},{6,7},{7,6},{8,9},{9,8},{10,11... | collective-permute-start | bytes 1572872 | tf_op jit(solution)/shard_map/ppermute | solution.py:734
  163.7 36.9 %collective-permute-start.13 = (bf16[512,256]{1,0:T(8,128)(2,1)S(1)}, bf16[512,256]{1,0:T(8,128)(2,1)S(1)}, u32[]{:S(2)}, u32[]{:S(2)}) collective-permute-start(bf16[512,256]{1,0:T(8,128)(2,1)S(1)} %slice.207), channel_id=1, source_target_pairs={{0,1},{1,0},{2,3},{3,2},{4,5},{5,4},{6,7},{7,6},{8,9},{9,8},{10,11... | collective-permute-start | bytes 786440 | tf_op jit(solution)/shard_map/ppermute | solution.py:734
  164.9 34.0 %collective-permute-start.12 = (bf16[512,256]{1,0:T(8,128)(2,1)S(1)}, bf16[512,256]{1,0:T(8,128)(2,1)S(1)}, u32[]{:S(2)}, u32[]{:S(2)}) collective-permute-start(bf16[512,256]{1,0:T(8,128)(2,1)S(1)} %slice.206), channel_id=1, source_target_pairs={{0,2},{1,3},{2,0},{3,1},{4,6},{5,7},{6,4},{7,5},{8,10},{9,11},{10,... | collective-permute-start | bytes 786440 | tf_op jit(solution)/shard_map/ppermute | solution.py:734
  167.5 50.5 %collective-permute-start.9 = (bf16[512,256]{1,0:T(8,128)(2,1)S(1)}, bf16[512,256]{1,0:T(8,128)(2,1)S(1)}, u32[]{:S(2)}, u32[]{:S(2)}) collective-permute-start(bf16[512,256]{1,0:T(8,128)(2,1)S(1)} %slice.205), channel_id=1, source_target_pairs={{0,1},{1,0},{2,3},{3,2},{4,5},{5,4},{6,7},{7,6},{8,9},{9,8},{10,11... | collective-permute-start | bytes 786440 | tf_op jit(solution)/shard_map/ppermute | solution.py:734
  188.9 29.0 %collective-permute-start.8 = (bf16[512,256]{1,0:T(8,128)(2,1)S(1)}, bf16[512,256]{1,0:T(8,128)(2,1)S(1)}, u32[]{:S(2)}, u32[]{:S(2)}) collective-permute-start(bf16[512,256]{1,0:T(8,128)(2,1)S(1)} %slice.204), channel_id=1, source_target_pairs={{0,2},{1,3},{2,0},{3,1},{4,6},{5,7},{6,4},{7,5},{8,10},{9,11},{10,... | collective-permute-start | bytes 786440 | tf_op jit(solution)/shard_map/ppermute | solution.py:734
  197.0 35.6 %collective-permute-start.48 = (f32[4,8,256]{2,1,0:T(8,128)}, f32[4,8,256]{2,1,0:T(8,128)S(1)}, u32[]{:S(2)}, u32[]{:S(2)}) collective-permute-start(f32[4,8,256]{2,1,0:T(8,128)} %get-tuple-element.75.q0), channel_id=1, source_target_pairs={{0,3},{1,2},{2,1},{3,0},{4,7},{5,6},{6,5},{7,4},{8,11},{9,10},{10,... | collective-permute-start | bytes 98312 | tf_op jit(solution)/shard_map/ppermute | solution.py:734
  198.9 33.8 %collective-permute-start.47 = (f32[4,8,256]{2,1,0:T(8,128)}, f32[4,8,256]{2,1,0:T(8,128)S(1)}, u32[]{:S(2)}, u32[]{:S(2)}) collective-permute-start(f32[4,8,256]{2,1,0:T(8,128)} %get-tuple-element.75.q0), channel_id=1, source_target_pairs={{0,2},{1,3},{2,0},{3,1},{4,6},{5,7},{6,4},{7,5},{8,10},{9,11},{10,... | collective-permute-start | bytes 98312 | tf_op jit(solution)/shard_map/ppermute | solution.py:734
  200.6 32.1 %collective-permute-start.46 = (f32[4,8,256]{2,1,0:T(8,128)}, f32[4,8,256]{2,1,0:T(8,128)S(1)}, u32[]{:S(2)}, u32[]{:S(2)}) collective-permute-start(f32[4,8,256]{2,1,0:T(8,128)} %get-tuple-element.75.q0), channel_id=1, source_target_pairs={{0,1},{1,0},{2,3},{3,2},{4,5},{5,4},{6,7},{7,6},{8,9},{9,8},{10,11... | collective-permute-start | bytes 98312 | tf_op jit(solution)/shard_map/ppermute | solution.py:734
  224.9 39.9 %collective-permute-start.22 = (f32[4,8,256]{2,1,0:T(8,128)}, f32[4,8,256]{2,1,0:T(8,128)S(1)}, u32[]{:S(2)}, u32[]{:S(2)}) collective-permute-start(f32[4,8,256]{2,1,0:T(8,128)} %get-tuple-element.68.q0), channel_id=1, source_target_pairs={{0,3},{1,2},{2,1},{3,0},{4,7},{5,6},{6,5},{7,4},{8,11},{9,10},{10,... | collective-permute-start | bytes 98312 | tf_op jit(solution)/shard_map/ppermute | solution.py:734
  226.8 38.0 %collective-permute-start.21 = (f32[4,8,256]{2,1,0:T(8,128)}, f32[4,8,256]{2,1,0:T(8,128)S(1)}, u32[]{:S(2)}, u32[]{:S(2)}) collective-permute-start(f32[4,8,256]{2,1,0:T(8,128)} %get-tuple-element.68.q0), channel_id=1, source_target_pairs={{0,2},{1,3},{2,0},{3,1},{4,6},{5,7},{6,4},{7,5},{8,10},{9,11},{10,... | collective-permute-start | bytes 98312 | tf_op jit(solution)/shard_map/ppermute | solution.py:734
  232.5 32.3 %collective-permute-start.20 = (f32[4,8,256]{2,1,0:T(8,128)S(1)}, f32[4,8,256]{2,1,0:T(8,128)S(1)}, u32[]{:S(2)}, u32[]{:S(2)}) collective-permute-start(f32[4,8,256]{2,1,0:T(8,128)S(1)} %copy-done.86), channel_id=1, source_target_pairs={{0,1},{1,0},{2,3},{3,2},{4,5},{5,4},{6,7},{7,6},{8,9},{9,8},{10,11... | collective-permute-start | bytes 98312 | tf_op jit(solution)/shard_map/ppermute | solution.py:734
  310.2 42.7 %collective-permute-start.69 = (f32[1024,64]{1,0:T(8,128)S(1)}, f32[1024,64]{1,0:T(8,128)S(1)}, u32[]{:S(2)}, u32[]{:S(2)}) collective-permute-start(f32[1024,64]{1,0:T(8,128)S(1)} %get-tuple-element.188), channel_id=1, source_target_pairs={{0,3},{1,2},{2,1},{3,0},{4,7},{5,6},{6,5},{7,4},{8,11},{9,10},{10,... | collective-permute-start | bytes 786440 | tf_op jit(solution)/shard_map/ppermute | solution.py:734
  312.0 42.2 %collective-permute-start.68 = (f32[1024,64]{1,0:T(8,128)}, f32[1024,64]{1,0:T(8,128)}, u32[]{:S(2)}, u32[]{:S(2)}) collective-permute-start(f32[1024,64]{1,0:T(8,128)} %get-tuple-element.189), channel_id=1, source_target_pairs={{0,2},{1,3},{2,0},{3,1},{4,6},{5,7},{6,4},{7,5},{8,10},{9,11},{10,... | collective-permute-start | bytes 786440 | tf_op jit(solution)/shard_map/ppermute | solution.py:734
  313.7 42.6 %collective-permute-start.67 = (f32[1024,64]{1,0:T(8,128)}, f32[1024,64]{1,0:T(8,128)}, u32[]{:S(2)}, u32[]{:S(2)}) collective-permute-start(f32[1024,64]{1,0:T(8,128)} %get-tuple-element.190), channel_id=1, source_target_pairs={{0,1},{1,0},{2,3},{3,2},{4,5},{5,4},{6,7},{7,6},{8,9},{9,8},{10,11... | collective-permute-start | bytes 786440 | tf_op jit(solution)/shard_map/ppermute | solution.py:734
  315.6 48.3 %collective-permute-start.57 = (f32[1024,64]{1,0:T(8,128)}, f32[1024,64]{1,0:T(8,128)}, u32[]{:S(2)}, u32[]{:S(2)}) collective-permute-start(f32[1024,64]{1,0:T(8,128)} %get-tuple-element.181), channel_id=1, source_target_pairs={{0,3},{1,2},{2,1},{3,0},{4,7},{5,6},{6,5},{7,4},{8,11},{9,10},{10,... | collective-permute-start | bytes 786440 | tf_op jit(solution)/shard_map/ppermute | solution.py:734
  317.4 47.9 %collective-permute-start.56 = (f32[1024,64]{1,0:T(8,128)}, f32[1024,64]{1,0:T(8,128)}, u32[]{:S(2)}, u32[]{:S(2)}) collective-permute-start(f32[1024,64]{1,0:T(8,128)} %get-tuple-element.182), channel_id=1, source_target_pairs={{0,2},{1,3},{2,0},{3,1},{4,6},{5,7},{6,4},{7,5},{8,10},{9,11},{10,... | collective-permute-start | bytes 786440 | tf_op jit(solution)/shard_map/ppermute | solution.py:734
  380.7 70.1 %collective-permute-start.75 = (f32[4,8,256]{2,1,0:T(8,128)S(1)}, f32[4,8,256]{2,1,0:T(8,128)S(1)}, u32[]{:S(2)}, u32[]{:S(2)}) collective-permute-start(f32[4,8,256]{2,1,0:T(8,128)S(1)} %copy-done.60), channel_id=1, source_target_pairs={{0,3},{1,2},{2,1},{3,0},{4,7},{5,6},{6,5},{7,4},{8,11},{9,10},{10,... | collective-permute-start | bytes 98312 | tf_op jit(solution)/shard_map/ppermute | solution.py:734
  382.4 69.7 %collective-permute-start.74 = (f32[4,8,256]{2,1,0:T(8,128)S(1)}, f32[4,8,256]{2,1,0:T(8,128)S(1)}, u32[]{:S(2)}, u32[]{:S(2)}) collective-permute-start(f32[4,8,256]{2,1,0:T(8,128)S(1)} %copy-done.60), channel_id=1, source_target_pairs={{0,2},{1,3},{2,0},{3,1},{4,6},{5,7},{6,4},{7,5},{8,10},{9,11},{10,... | collective-permute-start | bytes 98312 | tf_op jit(solution)/shard_map/ppermute | solution.py:734
  386.0 67.9 %collective-permute-start.73 = (f32[4,8,256]{2,1,0:T(8,128)S(1)}, f32[4,8,256]{2,1,0:T(8,128)S(1)}, u32[]{:S(2)}, u32[]{:S(2)}) collective-permute-start(f32[4,8,256]{2,1,0:T(8,128)S(1)} %copy-done.60), channel_id=1, source_target_pairs={{0,1},{1,0},{2,3},{3,2},{4,5},{5,4},{6,7},{7,6},{8,9},{9,8},{10,11... | collective-permute-start | bytes 98312 | tf_op jit(solution)/shard_map/ppermute | solution.py:734
  413.5 54.0 %collective-permute-start.70 = (bf16[1024,256]{1,0:T(8,128)(2,1)S(1)}, bf16[1024,256]{1,0:T(8,128)(2,1)S(1)}, u32[]{:S(2)}, u32[]{:S(2)}) collective-permute-start(bf16[1024,256]{1,0:T(8,128)(2,1)S(1)} %copy-done.82), channel_id=1, source_target_pairs={{0,1},{1,0},{2,3},{3,2},{4,5},{5,4},{6,7},{7,6},{8,9},{9,8},{10,11... | collective-permute-start | bytes 1572872 | tf_op jit(solution)/shard_map/ppermute | solution.py:734
  450.8 28.4 %collective-permute-start.72 = (bf16[1024,256]{1,0:T(8,128)(2,1)S(1)}, bf16[1024,256]{1,0:T(8,128)(2,1)S(1)}, u32[]{:S(2)}, u32[]{:S(2)}) collective-permute-start(bf16[1024,256]{1,0:T(8,128)(2,1)S(1)} %copy-done.80), channel_id=1, source_target_pairs={{0,3},{1,2},{2,1},{3,0},{4,7},{5,6},{6,5},{7,4},{8,11},{9,10},{10,... | collective-permute-start | bytes 1572872 | tf_op jit(solution)/shard_map/ppermute | solution.py:734
  464.3 30.0 %collective-permute-start.58 = (bf16[1024,256]{1,0:T(8,128)(2,1)}, bf16[1024,256]{1,0:T(8,128)(2,1)S(1)}, u32[]{:S(2)}, u32[]{:S(2)}) collective-permute-start(bf16[1024,256]{1,0:T(8,128)(2,1)} %get-tuple-element.86), channel_id=1, source_target_pairs={{0,1},{1,0},{2,3},{3,2},{4,5},{5,4},{6,7},{7,6},{8,9},{9,8},{10,11... | collective-permute-start | bytes 1572872 | tf_op jit(solution)/shard_map/ppermute | solution.py:734
  465.5 30.1 %collective-permute-start.59 = (bf16[1024,256]{1,0:T(8,128)(2,1)}, bf16[1024,256]{1,0:T(8,128)(2,1)S(1)}, u32[]{:S(2)}, u32[]{:S(2)}) collective-permute-start(bf16[1024,256]{1,0:T(8,128)(2,1)} %get-tuple-element.87), channel_id=1, source_target_pairs={{0,2},{1,3},{2,0},{3,1},{4,6},{5,7},{6,4},{7,5},{8,10},{9,11},{10,... | collective-permute-start | bytes 1572872 | tf_op jit(solution)/shard_map/ppermute | solution.py:734
  493.8 64.9 %collective-permute-start.98 = (f32[1024,256]{1,0:T(8,128)}, f32[1024,256]{1,0:T(8,128)}, u32[]{:S(2)}, u32[]{:S(2)}) collective-permute-start(f32[1024,256]{1,0:T(8,128)} %constant_dynamic-slice_fusion), channel_id=1, source_target_pairs={{0,4},{4,0},{1,5},{5,1},{2,6},{6,2},{3,7},{7,3},{8,12},{12,8},{9,1... | collective-permute-start | bytes 3145736 | tf_op jit(solution)/shard_map/ppermute | solution.py:739
  493.8 69.1 %collective-permute-start.79 = (f32[512,1024]{1,0:T(8,128)}, f32[512,1024]{1,0:T(8,128)}, u32[]{:S(2)}, u32[]{:S(2)}) collective-permute-start(f32[512,1024]{1,0:T(8,128)} %constant_dynamic-slice_fusion.2), channel_id=1, source_target_pairs={{0,4},{4,0},{1,5},{5,1},{2,6},{6,2},{3,7},{7,3},{8,12},{12,8},{9,1... | collective-permute-start | bytes 6291464 | tf_op jit(solution)/shard_map/ppermute | solution.py:739
  494.3 41.7 %collective-permute-start.96 = (f32[512,72]{1,0:T(8,128)}, f32[512,72]{1,0:T(8,128)}, u32[]{:S(2)}, u32[]{:S(2)}) collective-permute-start(f32[512,72]{1,0:T(8,128)} %add.415), channel_id=1, source_target_pairs={{8,0},{16,24},{9,1},{17,25},{10,2},{18,26},{11,3},{19,27},{12,4},{... | collective-permute-start | bytes 442376 | tf_op jit(solution)/shard_map/ppermute | solution.py:799
  565.2 31.1 %collective-permute-start.80 = (f32[128,1024]{1,0:T(8,128)S(1)}, f32[128,1024]{1,0:T(8,128)S(1)}, u32[]{:S(2)}, u32[]{:S(2)}) collective-permute-start(f32[128,1024]{1,0:T(8,128)S(1)} %get-tuple-element.162), channel_id=1, source_target_pairs={{0,8},{24,16},{1,9},{25,17},{2,10},{26,18},{3,11},{27,19},{4,12},{... | collective-permute-start | bytes 1572872 | tf_op jit(solution)/shard_map/ppermute | solution.py:797
  566.6 40.8 %collective-permute-start.89 = (f32[128,1024]{1,0:T(8,128)S(1)}, f32[128,1024]{1,0:T(8,128)S(1)}, u32[]{:S(2)}, u32[]{:S(2)}) collective-permute-start(f32[128,1024]{1,0:T(8,128)S(1)} %get-tuple-element.163), channel_id=1, source_target_pairs={{0,8},{24,16},{1,9},{25,17},{2,10},{26,18},{3,11},{27,19},{4,12},{... | collective-permute-start | bytes 1572872 | tf_op jit(solution)/shard_map/ppermute | solution.py:797
  568.0 50.8 %collective-permute-start.86 = (f32[128,1024]{1,0:T(8,128)S(1)}, f32[128,1024]{1,0:T(8,128)S(1)}, u32[]{:S(2)}, u32[]{:S(2)}) collective-permute-start(f32[128,1024]{1,0:T(8,128)S(1)} %get-tuple-element.164), channel_id=1, source_target_pairs={{0,8},{24,16},{1,9},{25,17},{2,10},{26,18},{3,11},{27,19},{4,12},{... | collective-permute-start | bytes 1572872 | tf_op jit(solution)/shard_map/ppermute | solution.py:797
  573.8 56.2 %collective-permute-start.83 = (f32[128,1024]{1,0:T(8,128)S(1)}, f32[128,1024]{1,0:T(8,128)S(1)}, u32[]{:S(2)}, u32[]{:S(2)}) collective-permute-start(f32[128,1024]{1,0:T(8,128)S(1)} %get-tuple-element.165), channel_id=1, source_target_pairs={{0,8},{24,16},{1,9},{25,17},{2,10},{26,18},{3,11},{27,19},{4,12},{... | collective-permute-start | bytes 1572872 | tf_op jit(solution)/shard_map/ppermute | solution.py:797
  585.0 64.2 %collective-permute-start.66 = (f32[256,256]{1,0:T(8,128)S(1)}, f32[256,256]{1,0:T(8,128)S(1)}, u32[]{:S(2)}, u32[]{:S(2)}) collective-permute-start(f32[256,256]{1,0:T(8,128)S(1)} %copy-done.46), channel_id=1, source_target_pairs={{0,8},{8,16},{16,24},{24,0},{1,9},{9,17},{17,25},{25,1},{2,10},{10... | collective-permute-start | bytes 786440 | tf_op jit(solution)/shard_map/ppermute | solution.py:739
  596.3 50.7 %collective-permute-start.65 = (f32[256,256]{1,0:T(8,128)S(1)}, f32[256,256]{1,0:T(8,128)S(1)}, u32[]{:S(2)}, u32[]{:S(2)}) collective-permute-start(f32[256,256]{1,0:T(8,128)S(1)} %copy-done.47), channel_id=1, source_target_pairs={{0,16},{8,24},{16,0},{24,8},{1,17},{9,25},{17,1},{25,9},{2,18},{10... | collective-permute-start | bytes 786440 | tf_op jit(solution)/shard_map/ppermute | solution.py:739
  607.5 38.7 %collective-permute-start.64 = (f32[256,256]{1,0:T(8,128)S(1)}, f32[256,256]{1,0:T(8,128)S(1)}, u32[]{:S(2)}, u32[]{:S(2)}) collective-permute-start(f32[256,256]{1,0:T(8,128)S(1)} %copy-done.48), channel_id=1, source_target_pairs={{0,24},{8,0},{16,8},{24,16},{1,25},{9,1},{17,9},{25,17},{2,26},{10... | collective-permute-start | bytes 786440 | tf_op jit(solution)/shard_map/ppermute | solution.py:739
  618.7 28.2 %collective-permute-start.100 = (f32[512,256]{1,0:T(8,128)S(1)}, f32[512,256]{1,0:T(8,128)S(1)}, u32[]{:S(2)}, u32[]{:S(2)}) collective-permute-start(f32[512,256]{1,0:T(8,128)S(1)} %get-tuple-element.174), channel_id=1, source_target_pairs={{8,16},{16,8},{9,17},{17,9},{10,18},{18,10},{11,19},{19,11},{12,20... | collective-permute-start | bytes 1572872 | tf_op jit(solution)/shard_map/ppermute | solution.py:798
  650.7 33.8 %collective-permute-start.82 = (f32[128,1024]{1,0:T(8,128)S(1)}, f32[128,1024]{1,0:T(8,128)S(1)}, u32[]{:S(2)}, u32[]{:S(2)}) collective-permute-start(f32[128,1024]{1,0:T(8,128)S(1)} %add.403), channel_id=1, source_target_pairs={{8,0},{16,24},{9,1},{17,25},{10,2},{18,26},{11,3},{19,27},{12,4},{... | collective-permute-start | bytes 1572872 | tf_op jit(solution)/shard_map/ppermute | solution.py:799
  652.2 75.8 %collective-permute-start.104 = (f32[512,256]{1,0:T(8,128)S(1)}, f32[512,256]{1,0:T(8,128)S(1)}, u32[]{:S(2)}, u32[]{:S(2)}) collective-permute-start(f32[512,256]{1,0:T(8,128)S(1)} %add.427), channel_id=1, source_target_pairs={{8,0},{16,24},{9,1},{17,25},{10,2},{18,26},{11,3},{19,27},{12,4},{... | collective-permute-start | bytes 1572872 | tf_op jit(solution)/shard_map/ppermute | solution.py:799
  663.5 44.7 %collective-permute-start.85 = (f32[128,1024]{1,0:T(8,128)S(1)}, f32[128,1024]{1,0:T(8,128)S(1)}, u32[]{:S(2)}, u32[]{:S(2)}) collective-permute-start(f32[128,1024]{1,0:T(8,128)S(1)} %add.405), channel_id=1, source_target_pairs={{8,0},{16,24},{9,1},{17,25},{10,2},{18,26},{11,3},{19,27},{12,4},{... | collective-permute-start | bytes 1572872 | tf_op jit(solution)/shard_map/ppermute | solution.py:799
  665.0 54.5 %collective-permute-start.88 = (f32[128,1024]{1,0:T(8,128)S(1)}, f32[128,1024]{1,0:T(8,128)S(1)}, u32[]{:S(2)}, u32[]{:S(2)}) collective-permute-start(f32[128,1024]{1,0:T(8,128)S(1)} %add.407), channel_id=1, source_target_pairs={{8,0},{16,24},{9,1},{17,25},{10,2},{18,26},{11,3},{19,27},{12,4},{... | collective-permute-start | bytes 1572872 | tf_op jit(solution)/shard_map/ppermute | solution.py:799
  666.4 61.2 %collective-permute-start.91 = (f32[128,1024]{1,0:T(8,128)S(1)}, f32[128,1024]{1,0:T(8,128)S(1)}, u32[]{:S(2)}, u32[]{:S(2)}) collective-permute-start(f32[128,1024]{1,0:T(8,128)S(1)} %add.409), channel_id=1, source_target_pairs={{8,0},{16,24},{9,1},{17,25},{10,2},{18,26},{11,3},{19,27},{12,4},{... | collective-permute-start | bytes 1572872 | tf_op jit(solution)/shard_map/ppermute | solution.py:799
  (151 other events, 2053.2 us)

commit v2 on v1

--- a/solution.py
+++ b/solution.py
@@ -1,6 +1,7 @@
 import functools
 import jax
 import jax.numpy as jnp
+import numpy as np
 from jax import lax
 from jax.experimental import pallas as pl
 from jax.experimental.pallas import tpu as pltpu
@@ -356,8 +357,8 @@
 
 
 def forward_kernel(
-    index_ref, x0, x1, x2, x3, w_ref, gain_ref, taps_ref, dt_ref, skip_ref, spread_ref, lower_ref,
-    gate_out, conv_out, ssd_out, state_out, extended, state,
+    index_ref, x0, x1, x2, x3, w_z_ref, w_x_ref, w_rest_ref, gain_ref, taps_ref, dt_ref, skip_ref,
+    spread_ref, lower_ref, gate_out, conv_out, ssd_out, state_out, extended, state,
 ):
     inner = skip_ref.shape[1]
     heads = inner // HEAD_DIM
@@ -370,13 +371,17 @@
 
     x_refs = (x0, x1, x2, x3)
     _, _, normed = normed_blocks(x_refs, gain_ref)
-    projected = sum(
-        dot_nn(part, w_ref[block_of(index_ref, k, part.shape[1]), :])
-        for k, part in enumerate(normed)
-    )
-    gate_out[...] = projected[:, :inner]
-    conv_out[...] = projected[:, inner:]
-    conv_in = projected[:, inner : inner + conv_width]
+    parts = [block_of(index_ref, k, part.shape[1]) for k, part in enumerate(normed)]
+    gate_out[...] = sum(dot_nn(part, w_z_ref[rows, :]) for part, rows in zip(normed, parts))
+    projected = jnp.concatenate(
+        [
+            sum(dot_nn(part, ref[rows, :]) for part, rows in zip(normed, parts))
+            for ref in (w_x_ref, w_rest_ref)
+        ],
+        axis=1,
+    )
+    conv_out[...] = projected
+    conv_in = projected[:, :conv_width]
     extended[8 : 8 + CHUNK, :] = conv_in
     pre_act = taps_ref[4:5, :] + taps_ref[3:4, :] * conv_in
     for k in range(3):
@@ -387,7 +392,7 @@
     b_rows = act[:, inner : inner + STATE]
     c_rows = act[:, inner + STATE :]
 
-    _, step, _, step_log = step_values(projected[:, inner + conv_width :], dt_ref)
+    _, step, _, step_log = step_values(projected[:, conv_width:], dt_ref)
     cumulative = sum(dot_nn(lower_ref[...], part) for part in split3(step_log))
     cum_t = jnp.transpose(cumulative)
     step_t = jnp.transpose(step)
@@ -604,29 +609,33 @@
 
 
 def weight_kernel(
-    index_ref, x0, x1, x2, x3, gain_ref, w_ref, d_gate_ref, d_x_ref, d_dt_ref,
-    d_normed_out, wide_out, dt_out,
+    index_ref, x0, x1, x2, x3, g0, g1, g2, g3, gain_ref, w_ref, scaled_ref, d_gate_ref, d_x_ref,
+    d_dt_ref, *rest,
 ):
+    *sums_so_far, d_normed_out, wide_out, dt_out, out_out = rest
+
     @pl.when(pl.program_id(0) == 0)
     def _():
-        wide_out[...] = jnp.zeros(wide_out.shape, F32)
-        dt_out[...] = jnp.zeros(dt_out.shape, F32)
+        for i, ref in enumerate((wide_out, dt_out, out_out)):
+            ref[...] = sums_so_far[i][...] if sums_so_far else jnp.zeros(ref.shape, F32)
 
     _, _, normed = normed_blocks((x0, x1, x2, x3), gain_ref)
     d_wide = jnp.concatenate([d_gate_ref[...], d_x_ref[...]], axis=1)
     d_dt = d_dt_ref[...]
     d_all = jnp.concatenate([d_wide, d_dt], axis=1)
+    scaled = scaled_ref[...]
     width = normed[0].shape[1]
-    for k, part in enumerate(normed):
+    for k, (part, cot) in enumerate(zip(normed, (g0, g1, g2, g3))):
         rows = block_of(index_ref, k, width)
         wide_out[rows, :] += dot_tn(part, d_wide)
         dt_out[rows, :] += dot_tn(part, d_dt)
+        out_out[:, k * width : (k + 1) * width] += dot_tn(scaled, cot[...])
         d_normed_out[:, k * width : (k + 1) * width] = dot_nn(d_all, w_ref[:, rows])
 
 
 def mixed_kernel(
-    index_ref, x0, x1, x2, x3, gain_ref, w_ref, r0, r1, r2, r3, conv_ref, before_ref, taps_ref,
-    d_normed_ref, own_out, send1, send2, send3, sums_out, grad_out, taps_out, extended, d_pre,
+    index_ref, x0, x1, x2, x3, gain_ref, w_ref, d_act_ref, conv_ref, before_ref, taps_ref,
+    d_normed_ref, own_out, send1, send2, send3, grad_out, taps_out, extended, d_pre,
 ):
     step_at = pl.program_id(0)
     chunk_at = pl.num_programs(0) - 1 - step_at
@@ -644,8 +653,7 @@
     pre_act = taps_ref[4:5, :] + taps_ref[3:4, :] * conv_in
     for k in range(3):
         pre_act = pre_act + taps_ref[k : k + 1, :] * extended[5 + k : 5 + k + CHUNK, :]
-    d_act = r0[...] + r1[...] + r2[...] + r3[...]
-    d_pre_now = d_act * silu_slope(pre_act, sigmoid(pre_act))
+    d_pre_now = d_act_ref[...] * silu_slope(pre_act, sigmoid(pre_act))
     d_pre[0:CHUNK, :] = d_pre_now
     taps_out[4:5, :] += jnp.sum(d_pre_now, axis=0, keepdims=True)
     taps_out[3:4, :] += jnp.sum(d_pre_now * conv_in, axis=0, keepdims=True)
@@ -660,19 +668,28 @@
     _, hats, normed = normed_blocks((x0, x1, x2, x3), gain_ref)
     width = normed[0].shape[1]
     row_dot = jnp.zeros((CHUNK, 1), F32)
-    for k, out in enumerate((own_out, send1, send2, send3)):
+    sends = (own_out, send1, send2, send3)
+    for k, out in enumerate(sends):
         rows = block_of(index_ref, k, width)
         grad_out[rows, :] += dot_tn(normed[k], d_in)
         d_part = d_normed_ref[:, k * width : (k + 1) * width] + dot_nn(d_in, w_ref[:, rows])
-        out[...] = d_part.astype(out.dtype)
+        out[0, 0:CHUNK, :] = d_part.astype(out.dtype)
         scaled_hat = hats[k] * gain_ref[k : k + 1]
         row_dot = row_dot + jnp.sum(d_part * scaled_hat, axis=1, keepdims=True)
-    sums_out[0] = column_of_sums((row_dot,), 8)
-
-
-def final_kernel(
-    x0, x1, x2, x3, gain_ref, own_ref, r1, r2, r3, q0, q1, q2, q3, cot_ref, grad_out, gain_out
-):
+    dots = column_of_sums((row_dot,), 8)
+    own_out[0, CHUNK : CHUNK + 8, :] = dots
+    high, low = split2(dots)
+    first = lax.broadcasted_iota(jnp.int32, (8, CHUNK), 0) == 0
+    low = jnp.where(first, low.astype(F32), 0.0)
+    low = jnp.concatenate([low[0:1], low[0:1], jnp.zeros((6, CHUNK), F32)], axis=0)
+    high = high.astype(F32)
+    both = jnp.where(first, high, low)
+    both = jnp.concatenate([both, jnp.zeros((8, CHUNK), F32)], axis=0).astype(BF)
+    for out in sends[1:]:
+        out[0, CHUNK : CHUNK + 16, :] = both
+
+
+def final_kernel(x0, x1, x2, x3, gain_ref, own_ref, r1, r2, r3, cot_ref, grad_out, gain_out):
     @pl.when(pl.program_id(0) == 0)
     def _():
         gain_out[...] = jnp.zeros(gain_out.shape, F32)
@@ -680,13 +697,18 @@
     blocks = [ref[...].astype(F32) for ref in (x0, x1, x2, x3)]
     inverse = inverse_rms(blocks)
     hat = blocks[0] * inverse
-    sums = q0[0] + q1[0] + q2[0] + q3[0]
+    received = [ref[0].astype(F32) for ref in (r1, r2, r3)]
+    total = received[0] + received[1] + received[2]
+    sums = own_ref[0, CHUNK : CHUNK + 8, :] + total[CHUNK : CHUNK + 8, :]
     sums = jnp.transpose(jnp.concatenate([sums, jnp.zeros((LANES - 8, CHUNK), F32)], axis=0))
-    mean = sums[:, 0:1] / (len(blocks) * hat.shape[1])
-    d_own = own_ref[...] + r1[...].astype(F32) + r2[...].astype(F32) + r3[...].astype(F32)
+    mean = (sums[:, 0:1] + sums[:, 1:2]) / (len(blocks) * hat.shape[1])
+    d_own = own_ref[0, 0:CHUNK, :] + total[0:CHUNK]
     gain_out[0:1, :] += jnp.sum(d_own * hat, axis=0, keepdims=True)
     d_hat = d_own * gain_ref[0:1]
-    grad_out[...] = cot_ref[...].astype(F32) + inverse * (d_hat - hat * mean)
+    grad = cot_ref[...].astype(F32) + inverse * (d_hat - hat * mean)
+    grad_out[...] = grad
+    top = jnp.max(jnp.abs(grad), axis=0, keepdims=True)
+    gain_out[1:2, :] = jnp.maximum(gain_out[1:2, :], top)
 
 
 def rows_spec(width, flip=None):
@@ -704,6 +726,12 @@
     if flip is None:
         return pl.BlockSpec((1, 8, CHUNK), lambda c: (c, 0, 0))
     return pl.BlockSpec((1, 8, CHUNK), lambda c: (flip - 1 - c, 0, 0))
+
+
+def part_spec(more, width, flip=None):
+    if flip is None:
+        return pl.BlockSpec((1, CHUNK + more, width), lambda c: (c, 0, 0))
+    return pl.BlockSpec((1, CHUNK + more, width), lambda c: (flip - 1 - c, 0, 0))
 
 
 def whole_spec(shape):
@@ -743,74 +771,80 @@
     return lax.dynamic_index_in_dim(stack, position, 0, keepdims=False)
 
 
-def gather_small(value, me):
-    stack = jnp.stack([value] + [swap(value, k) for k in range(1, 4)])
-    return [pick(stack, jnp.bitwise_xor(me, j)) for j in range(4)]
+def after(value, *earlier):
+    return lax.optimization_barrier((value, earlier))[0]
+
+
+def exchange(parts, z):
+    shards = lax.axis_size("seq")
+    pieces = [pick(parts, z)]
+    for k in range(1, shards):
+        pieces.append(shift(pick(parts, lax.rem(z + k, shards)), "seq", k))
+    return pieces
+
+
+def in_order(pieces, z, axis):
+    size = pieces[0].shape[axis]
+    count = len(pieces)
+    ordered = jnp.concatenate(pieces[::-1] * 2, axis=axis)
+    return lax.dynamic_slice_in_dim(ordered, (count - 1 - z) * size, count * size, axis)
 
 
 def to_sequences(value, z):
     shards = lax.axis_size("seq")
-    each = value.shape[0] // shards
-    local = value.shape[1]
-    result = []
-    for s in range(each):
-        pieces = [pick(value, z * each + s)]
-        for k in range(1, shards):
-            pieces.append(shift(pick(value, lax.rem(z + k, shards) * each + s), "seq", k))
-        ordered = jnp.concatenate(pieces[::-1] * 2, axis=0)
-        start = (shards - 1 - z) * local
-        result.append(lax.dynamic_slice_in_dim(ordered, start, shards * local, 0))
-    return result
-
-
-def to_tokens(sequences, z):
+    parts = value.reshape((shards, -1) + value.shape[1:])
+    return in_order(exchange(parts, z), z, 1)
+
+
+def to_tokens(value, z, top=None):
     shards = lax.axis_size("seq")
-    local = sequences[0].shape[0] // shards
-    result = []
-    for value in sequences:
-        parts = value.reshape(shards, local, value.shape[1])
-        pieces = [pick(parts, z)]
-        for k in range(1, shards):
-            pieces.append(shift(pick(parts, lax.rem(z + k, shards)), "seq", k))
-        ordered = jnp.stack(pieces[::-1] * 2)
-        result.append(lax.dynamic_slice_in_dim(ordered, shards - 1 - z, shards, 0))
-    joined = jnp.stack(result, axis=1)
-    return joined.reshape(shards * len(sequences), local, joined.shape[-1])
-
-
-def gather_features(own):
-    half = own.shape[0] // 2
-    by_x, by_y = swap(own, 1), swap(own, 2)
-    far = jnp.concatenate([swap(by_x[:half], 2), swap(by_y[half:], 1)], axis=0)
-    return [own, by_x, by_y, far]
-
-
-def line_sum(value, parts):
-    if lax.axis_size("seq") != 4:
-        return lax.psum(value, "seq")
-    z = lax.axis_index("seq")
-    inside = (z == 1) | (z == 2)
-    size = value.shape[0] // parts
-    result = []
-    for i in range(parts):
-        piece = value[i * size : (i + 1) * size]
-        joined = piece + lax.ppermute(piece, "seq", [(0, 1), (3, 2)])
-        joined = joined + lax.ppermute(joined, "seq", [(1, 2), (2, 1)])
-        result.append(jnp.where(inside, joined, lax.ppermute(joined, "seq", [(1, 0), (2, 3)])))
-    return jnp.concatenate(result, axis=0)
-
-
-def core_sum(value, parts):
-    if lax.axis_size("dp") != 2:
-        return line_sum(lax.psum(value, "dp"), parts)
-    core = lax.axis_index("dp")
-    half = value.shape[0] // 2
-    keep = lax.dynamic_slice_in_dim(value, core * half, half, 0)
-    give = lax.dynamic_slice_in_dim(value, (1 - core) * half, half, 0)
-    mine = line_sum(keep + shift(give, "dp", 1), parts)
-    other = shift(mine, "dp", 1)
-    ordered = jnp.concatenate([other, mine, other], axis=0)
-    return lax.dynamic_slice_in_dim(ordered, (1 - core) * half, 2 * half, 0)
+    parts = value.reshape(shards, value.shape[0] // shards, value.shape[1])
+    if top is None:
+        return in_order([piece[None] for piece in exchange(parts, z)], z, 0)
+    power = exponent_of(top)
+    pieces = [pick(parts, z)]
+    for k in range(1, shards):
+        payload = to_half(pick(parts, lax.rem(z + k, shards)), power)
+        pieces.append(from_half(shift(payload, "seq", k))[0])
+    return in_order([piece[None] for piece in pieces], z, 0)
+
+
+def joined_tokens(parts):
+    joined = jnp.stack(parts, axis=1)
+    return joined.reshape((-1,) + joined.shape[2:])
+
+
+def far_features(by_x, by_y):
+    half = by_x.shape[0] // 2
+    return jnp.concatenate([swap(by_x[:half], 2), swap(by_y[half:], 1)], axis=0)
+
+
+HALF_TOP = 8.0
+
+
+def exponent_of(top):
+    return jnp.ceil(jnp.log2(jnp.maximum(top, 1e-30)))
+
+
+def to_half(value, exponent):
+    body = (value * jnp.exp2(HALF_TOP - exponent)).astype(jnp.float16)
+    mark = jnp.full((16, value.shape[1]), exponent, F32).astype(jnp.float16)
+    return jnp.concatenate([body, mark], axis=0)
+
+
+def from_half(payload):
+    exponent = payload[-1, 0].astype(F32)
+    return payload[:-16].astype(F32) * jnp.exp2(exponent - HALF_TOP), exponent
+
+
+def butterfly_sum(value):
+    for axis in ("dp", "seq"):
+        distance = 1
+        while distance < lax.axis_size(axis):
+            pairs = [(i, i ^ distance) for i in range(lax.axis_size(axis))]
+            value = value + lax.ppermute(value, axis, pairs)
+            distance *= 2
+    return value
 
 
 def on_device(
@@ -831,34 +865,70 @@
     tail_width = conv_width + LANES
     index = jnp.bitwise_xor(me, jnp.arange(4, dtype=jnp.int32))
 
-    tokens = [gather_features(part) for part in to_sequences(hidden_in, z)]
-
-    packed = jnp.concatenate([w_bc, norm_gain.reshape(-1, bc_here)], axis=0)
-    packed = gather_small(packed, me)
-    w_bc_all = jnp.concatenate([part[:full_width] for part in packed], axis=1)
-    gain_all = jnp.stack([part[full_width:].reshape(-1) for part in packed]).astype(F32)
-    gain_here = jnp.stack([pick(gain_all, index[k]) for k in range(4)])
+    hidden = to_sequences(hidden_in, z)
+
+    largest = jnp.max(jnp.abs(w_out.astype(F32)))
+    packed = jnp.concatenate(
+        [
+            w_bc.astype(F32),
+            norm_gain.astype(F32).reshape(-1, bc_here),
+            conv_bc,
+            conv_bc_bias[None],
+            jnp.full((1, bc_here), largest),
+        ],
+        axis=0,
+    )
+    packed = lax.all_gather(packed, "head")
+    w_dt, w_bc, w_out = after((w_dt, w_bc, w_out), hidden)
+    gain_end = full_width + part_width // bc_here
+    w_bc_all = jnp.concatenate([packed[j, :full_width] for j in range(4)], axis=1).astype(BF)
+    gain_all = packed[:, full_width:gain_end].reshape(4, part_width)
+    gain_here = jnp.concatenate(
+        [lax.dynamic_slice_in_dim(gain_all, index[k], 1, 0) for k in range(4)], axis=0
+    )
     taps_bc_own = jnp.concatenate([conv_bc, conv_bc_bias[None], jnp.zeros((3, bc_here), F32)])
-    taps_bc = jnp.concatenate(gather_small(taps_bc_own, me), axis=1)
-    taps_x = jnp.concatenate([conv_x, conv_x_bias[None], jnp.zeros((3, inner), F32)])
-    taps = jnp.concatenate([taps_x, taps_bc], axis=1)
+    taps_bc = jnp.concatenate([packed[j, gain_end : gain_end + 5] for j in range(4)], axis=1)
+    out_scale = 16.0 / jnp.maximum(jnp.max(packed[:, gain_end + 5, 0]), 1e-30)
+    taps_x = jnp.concatenate([conv_x, conv_x_bias[None]])
+    taps = jnp.pad(jnp.concatenate([taps_x, taps_bc], axis=1), ((0, 3), (0, 0)))
     w_dt_wide = jnp.pad(w_dt, ((0, 0), (0, LANES - heads)))
-    w_all = jnp.concatenate([w_z, w_x, w_bc_all, w_dt_wide], axis=1)
+    w_rest = jnp.concatenate([w_bc_all, w_dt_wide], axis=1)
     w_back = jnp.concatenate([w_z, w_x, w_dt_wide], axis=1).T
     w_bc_back = w_bc.T
     w_out_back = w_out.T
+    w_out_parts = [
+        lax.dynamic_slice_in_dim(w_out, index[k] * part_width, part_width, 1) for k in range(4)
+    ]
     dt_params = jnp.pad(jnp.stack([dt_bias, a_log]), ((0, 6), (0, LANES - heads)))
     skip_wide = jnp.repeat(skip, HEAD_DIM)[None]
     gate_wide = gate_gain[None]
-    owner = jnp.arange(inner) // HEAD_DIM
-    spread = (jnp.arange(LANES)[:, None] == owner[None, :]).astype(BF)
-    collect = (owner[:, None] == jnp.arange(LANES)[None, :]).astype(BF)
-    order = jnp.arange(CHUNK)
-    lower = (order[:, None] >= order[None, :]).astype(BF)
-    upper = (order[:, None] <= order[None, :]).astype(BF)
+    owner = np.arange(inner) // HEAD_DIM
+    spread = jnp.asarray(np.arange(LANES)[:, None] == owner[None, :], BF)
+    collect = jnp.asarray(owner[:, None] == np.arange(LANES)[None, :], BF)
+    order = np.arange(CHUNK)
+    lower = jnp.asarray(order[:, None] >= order[None, :], BF)
+    upper = jnp.asarray(order[:, None] <= order[None, :], BF)
+
+    tokens = []
+    near = [swap(hidden[0], 1), swap(hidden[0], 2)]
+    pieces = exchange(after(out_grad, near).reshape((shards, each) + out_grad.shape[1:]), z)
+    near, gain_here, w_rest, taps, w_out_back, w_back = after(
+        (near, gain_here, w_rest, taps, w_out_back, w_back), hidden
+    )
+    near = after(near, gain_here, w_rest, taps, w_out_back, w_back)
+    for s in range(each):
+        own = hidden[s]
+        if s:
+            own = after(own, near)
+            near = [swap(own, 1), swap(own, 2)]
+        tokens.append([own] + near + [far_features(*near)])
+    straight = jnp.arange(4, dtype=jnp.int32)
 
     x_specs = [rows_spec(part_width)] * 4
     x_flipped = [rows_spec(part_width, chunks)] * 4
+    g_specs = [
+        pl.BlockSpec((None, CHUNK, part_width), lambda c, k=k: (k, c, 0)) for k in range(4)
+    ]
     gain_spec = whole_spec((4, part_width))
     rows_inner = rows_spec(inner)
 
@@ -867,7 +937,8 @@
         "forward_scan",
         chunks,
         [SCALARS] + x_specs + [
-            whole_spec(w_all.shape), gain_spec, whole_spec(taps.shape), whole_spec((8, LANES)),
+            whole_spec(w_z.shape), whole_spec(w_x.shape), whole_spec(w_rest.shape), gain_spec,
+            whole_spec(taps.shape), whole_spec((8, LANES)),
             whole_spec((1, inner)), whole_spec(spread.shape), whole_spec(lower.shape),
         ],
         [
@@ -877,30 +948,27 @@
             (pl.BlockSpec((None, inner, STATE), lambda c: (c, 0, 0)), (chunks, inner, STATE), F32),
         ],
         [pltpu.VMEM((CHUNK + 8, conv_width), F32), pltpu.VMEM((inner, STATE), F32)],
-        8 * 10**9, 2 * 10**7,
+        10**9, 10**7,
     )
     ahead = [
-        forward(index, *x, w_all, gain_here, taps, dt_params, skip_wide, spread, lower)
+        forward(index, *x, w_z, w_x, w_rest, gain_here, taps, dt_params, skip_wide, spread, lower)
         for x in tokens
     ]
-    cotangents = [gather_features(part) for part in to_sequences(out_grad, z)]
+    own_cot = in_order(after(pieces, ahead[0][0], tokens[-1][1]), z, 1)
+    own_cot = [own_cot[s] for s in range(each)]
+    cotangents = [lax.all_gather(own, "head") for own in own_cot]
 
     score = call(
         score_kernel,
         "gate_sums",
         chunks,
-        [SCALARS] + x_specs + [
+        [SCALARS] + g_specs + [
             whole_spec(w_out_back.shape), rows_inner, rows_inner, whole_spec((1, inner)),
         ],
         [(rows_inner, (length, inner), F32), (sums_spec(), (chunks, 8, CHUNK), F32)],
         [],
-        2 * 10**9, 10**7,
-    )
-    scored = []
-    for (gate, _, ssd, _), g in zip(ahead, cotangents):
-        d_scaled, sums = score(index, *g, w_out_back, ssd, gate, gate_wide)
-        scored.append((d_scaled, [sums] + [swap(sums, k) for k in range(1, 4)]))
-
+        10**9, 10**6,
+    )
     flipped = rows_spec(inner, chunks)
     backward = call(
         functools.partial(backward_kernel, inner * lax.axis_size("head")),
@@ -928,121 +996,152 @@
             pltpu.VMEM((CHUNK + 8, inner), F32),
             pltpu.VMEM((inner, STATE), F32),
         ],
-        12 * 10**9, 2 * 10**7,
-    )
-    weigh = call(
-        weight_kernel,
-        "weight_sums",
-        chunks,
-        [SCALARS] + x_specs + [
-            gain_spec, whole_spec(w_back.shape), rows_inner, rows_inner, rows_spec(LANES),
-        ],
-        [
-            (rows_spec(full_width), (length, full_width), F32),
-            (whole_spec((full_width, 2 * inner)), (full_width, 2 * inner), F32),
-            (whole_spec((full_width, LANES)), (full_width, LANES), F32),
-        ],
-        [],
-        9 * 10**9, 2 * 10**7,
-    )
+        2 * 10**9, 10**7,
+    )
+    sum_shapes = [(full_width, 2 * inner), (full_width, LANES), (inner, full_width)]
+
+    def weigh(*args):
+        return call(
+            weight_kernel,
+            "weight_sums",
+            chunks,
+            [SCALARS] + x_specs + g_specs + [
+                gain_spec, whole_spec(w_back.shape), rows_inner, rows_inner, rows_inner,
+                rows_spec(LANES),
+            ] + [whole_spec(shape) for shape in sum_shapes[: len(args) - 15]],
+            [(rows_spec(full_width), (length, full_width), F32)]
+            + [(whole_spec(shape), shape, F32) for shape in sum_shapes],
+            [],
+            2 * 10**9, 10**7,
+        )(*args)
+
     mix = call(
         mixed_kernel,
         "input_sums",
         chunks,
         [SCALARS] + x_flipped + [gain_spec, whole_spec(w_bc_back.shape)]
-        + [rows_spec(bc_here, chunks)] * 5
+        + [rows_spec(bc_here, chunks)] * 2
         + [before_spec(bc_here, chunks), whole_spec((8, bc_here)), rows_spec(full_width, chunks)],
         [
-            (rows_spec(part_width, chunks), (length, part_width), F32),
-            (rows_spec(part_width, chunks), (length, part_width), BF),
-            (rows_spec(part_width, chunks), (length, part_width), BF),
-            (rows_spec(part_width, chunks), (length, part_width), BF),
-            (sums_spec(chunks), (chunks, 8, CHUNK), F32),
+            (part_spec(8, part_width, chunks), (chunks, CHUNK + 8, part_width), F32),
+            (part_spec(16, part_width, chunks), (chunks, CHUNK + 16, part_width), BF),
+            (part_spec(16, part_width, chunks), (chunks, CHUNK + 16, part_width), BF),
+            (part_spec(16, part_width, chunks), (chunks, CHUNK + 16, part_width), BF),
             (whole_spec((full_width, bc_here)), (full_width, bc_here), F32),
             (whole_spec((8, bc_here)), (8, bc_here), F32),
         ],
         [pltpu.VMEM((CHUNK + 8, bc_here), F32), pltpu.VMEM((CHUNK + 8, bc_here), F32)],
-        10**9, 2 * 10**7,
+        10**9, 10**7,
     )
     finish = call(
         final_kernel,
         "input_gradient",
         chunks,
-        x_specs + [gain_spec] + [rows_spec(part_width)] * 4 + [sums_spec()] * 4
+        x_specs + [gain_spec, part_spec(8, part_width)] + [part_spec(16, part_width)] * 3
         + [rows_spec(part_width)],
         [
             (rows_spec(part_width), (length, part_width), F32),
             (whole_spec((8, part_width)), (8, part_width), F32),
         ],
         [],
-        10**8, 10**7,
-    )
-
-    largest = jnp.max(jnp.abs(w_out.astype(F32)))
-    largest = functools.reduce(jnp.maximum, gather_small(largest[None], me))
-    out_scale = 16.0 / jnp.maximum(largest[0], 1e-30)
-    w_out_parts = [
-        lax.dynamic_slice_in_dim(w_out, index[k] * part_width, part_width, 1) for k in range(4)
-    ]
-
-    totals = None
-    block_parts, grad_parts = [], []
+        10**8, 10**6,
+    )
+
+    def scores_of(s, cotangent):
+        gate, _, ssd, _ = ahead[s]
+        d_scaled, sums = score(straight, *[cotangent] * 4, w_out_back, ssd, gate, gate_wide)
+        return d_scaled, [sums] + [swap(sums, k) for k in range(1, 4)]
+
+    behind, d_bc_all, blocks, outward = [], [], [], []
     for s in range(each):
-        x, g = tokens[s], cotangents[s]
         gate, conv, ssd, states = ahead[s]
-        d_scaled, sums = scored[s]
-        scaled, d_gate, d_x, d_dt, d_bc, wide, dt_sums = backward(
-            index, *sums, ssd, gate, d_scaled, conv, conv, states, gate_wide, taps, dt_params,
-            skip_wide, spread, collect, lower, upper,
+        cotangent = after(cotangents[s], behind[-1][0]) if behind else cotangents[s]
+        d_scaled, sums = scores_of(s, cotangent)
+        if behind:
+            sums = after(sums, outward[-1])
+        behind.append(
+            backward(
+                index, *sums, ssd, gate, d_scaled, conv, conv, states, gate_wide, taps, dt_params,
+                skip_wide, spread, collect, lower, upper,
+            )
         )
-        d_bc_parts = [
+        d_bc = behind[s][4]
+        power = exponent_of(jnp.max(jnp.abs(d_bc)))
+        parts = [
             lax.dynamic_slice_in_dim(d_bc, index[k] * bc_here, bc_here, 1) for k in range(4)
         ]
-        d_bc_parts = [d_bc_parts[0]] + [swap(d_bc_parts[k], k) for k in range(1, 4)]
-
+        sent = [
+            swap(to_half(jnp.concatenate([p[: length // 2], p[length // 2 :]], axis=1), power), k)
+            for k, p in enumerate(parts)
+            if k
+        ]
+        total = sum(from_half(part)[0] for part in sent)
+        total = jnp.concatenate([total[:, :bc_here], total[:, bc_here:]], axis=0)
+        d_bc_all.append(parts[0] + total)
+
+        scaled = behind[s][0]
         out_parts = [jnp.dot(scaled, part, preferred_element_type=F32) for part in w_out_parts]
-        received = [
-            swap((out_parts[k] * out_scale).astype(jnp.float16), k) for k in range(1, 4)
-        ]
-        block = x[0].astype(F32) + out_parts[0]
-        block = block + sum(part.astype(F32) for part in received) / out_scale
-        block_parts.append(block.astype(BF))
-        g_w_out = jnp.stack(
-            [
-                lax.dot_general(scaled, part, (((0,), (0,)), ((), ())), preferred_element_type=F32)
-                for part in g
-            ]
+        outward.append([(out_parts[k] * out_scale).astype(jnp.float16) for k in range(1, 4)])
+        received = [swap(part, k + 1) for k, part in enumerate(after(outward[s], sent))]
+        block = tokens[s][0].astype(F32) + out_parts[0]
+        blocks.append((block + sum(part.astype(F32) for part in received) / out_scale).astype(BF))
+
+    g_sums, mixed = [], []
+    sent_blocks = [to_tokens(block, z) for block in blocks]
+    for s in range(each):
+        scaled, d_gate, d_x, d_dt, _, _, _ = behind[s]
+        if s == 0:
+            d_dt = after(d_dt, outward, blocks[:-1])
+        else:
+            d_dt = after(d_dt, mixed[-1][0])
+        d_normed, *g_sums = weigh(
+            index, *tokens[s], *[cotangents[s]] * 4, gain_here, w_back, scaled, d_gate, d_x, d_dt,
+            *g_sums,
         )
-
-        d_normed, g_wide, g_dt = weigh(index, *x, gain_here, w_back, d_gate, d_x, d_dt)
-        conv_own = lax.dynamic_slice_in_dim(conv, inner + me * bc_here, bc_here, 1)
-        own, send1, send2, send3, dots, g_bc, taps_sums = mix(
-            index, *x, gain_here, w_bc_back, *d_bc_parts, conv_own, conv_own, taps_bc_own, d_normed
+        if s + 1 == each:
+            d_normed = after(d_normed, sent_blocks[:-1], blocks[-1])
+        conv_own = lax.dynamic_slice_in_dim(ahead[s][1], inner + me * bc_here, bc_here, 1)
+        own, send1, send2, send3, g_bc, taps_sums = mix(
+            index, *tokens[s], gain_here, w_bc_back, d_bc_all[s], conv_own, conv_own, taps_bc_own,
+            d_normed,
         )
-        dots = [dots] + [swap(dots, k) for k in range(1, 4)]
-        grad, gain_sums = finish(
-            *x, gain_here, own, swap(send1, 1), swap(send2, 2), swap(send3, 3), *dots, g[0]
-        )
-        grad_parts.append(grad)
-        now = (g_w_out, g_wide, g_dt[:, :heads], g_bc, wide, dt_sums, taps_sums, gain_sums[0:1])
-        totals = now if totals is None else jax.tree.map(jnp.add, totals, now)
-
-    g_w_out, g_wide, g_dt, g_bc, wide, dt_sums, taps_sums, gain_sums = totals
-    g_w_out = core_sum(g_w_out.reshape(4 * inner, part_width), 2).reshape(4, inner, part_width)
-    g_wide = core_sum(g_wide, 4)
-    g_rest = core_sum(jnp.concatenate([g_bc, g_dt], axis=1), 1)
-    wide, dt_sums, taps_sums, gain_sums = lax.psum(
-        (wide, dt_sums, taps_sums, gain_sums), ("seq", "dp")
-    )
-    g_w_out = jnp.concatenate([pick(g_w_out, index[j]) for j in range(4)], axis=1)
+        mixed.append((own, (swap(send1, 1), swap(send2, 2), swap(send3, 3)), g_bc, taps_sums))
+    g_wide, g_dt, g_w_out = g_sums
+    g_wide, g_w_out = lax.psum((g_wide, g_w_out), ("seq", "dp"))
+    wide = sum(part[5] for part in behind)
+    dt_sums = sum(part[6] for part in behind)
+
+    grads, gain_sums = [], []
+    for s in range(each):
+        own, sends, _, _ = mixed[s]
+        own = after(own, mixed[-1][0])
+        grad, gain_sum = finish(*tokens[s], gain_here, own, *sends, own_cot[s])
+        gain_sums.append(gain_sum[0:1])
+        grads.append(to_tokens(grad, z, jnp.max(gain_sum[1])))
+    g_bc = sum(part[2] for part in mixed)
+    taps_sums = sum(part[3] for part in mixed)
+    gain_sums = sum(gain_sums)
+    late = [
+        part.reshape(-1, LANES)
+        for part in (g_bc, g_dt[:, :heads], wide, dt_sums, taps_sums, gain_sums)
+    ]
+    ends = np.cumsum([0] + [part.shape[0] for part in late])
+    late = butterfly_sum(jnp.concatenate(late, axis=0))
+    late = [late[ends[i] : ends[i + 1]] for i in range(len(ends) - 1)]
+    g_bc, g_dt, wide, dt_sums, taps_sums, gain_sums = late
+    g_bc = g_bc.reshape(full_width, bc_here)
+    g_dt = g_dt.reshape(full_width, heads)
+    wide = wide.reshape(8, inner)
+    taps_sums = taps_sums.reshape(8, bc_here)
+    gain_sums = gain_sums.reshape(1, part_width)
     return (
-        to_tokens(block_parts, z),
-        to_tokens(grad_parts, z),
+        joined_tokens(sent_blocks),
+        joined_tokens(grads),
         gain_sums[0],
         g_wide[:, :inner],
         g_wide[:, inner:],
-        g_rest[:, :bc_here],
-        g_rest[:, bc_here:],
+        g_bc,
+        g_dt,
         wide[0:4],
         wide[4],
         taps_sums[0:4],
@@ -1058,7 +1157,8 @@
 def fits(mesh, seqs, length):
     shards = mesh.shape["seq"]
     local_seqs = seqs // mesh.shape["dp"]
-    return mesh.shape["head"] == 4 and local_seqs % shards == 0 and length % CHUNK == 0
+    doubling = all(mesh.shape[axis] & (mesh.shape[axis] - 1) == 0 for axis in ("seq", "dp"))
+    return doubling and mesh.shape["head"] == 4 and local_seqs % shards == 0 and length % CHUNK == 0
 
 
 def solution(mesh):

time: 747 us -> 531 us (0.71)
  waiting for transfers between devices: 271 us -> 123 us
  starting transfers between devices: 141 us -> 65.2 us
  blocking collectives: 26.5 us -> 0 us
  between operations: 18.8 us -> 40.4 us
  local copies, waits for them, and re-layouts: 67.2 us -> 85.4 us
  matrix products: 25.8 us -> 14.6 us
  Pallas kernels: 150 us -> 158 us
    ppermute x21 -> x3, waiting for transfers between devices: 123 us -> 34 us  [butterfly_sum(): value = value + lax.ppermute(value, axis, pairs)]
    ppermute x30 -> x18, waiting for transfers between devices: 81.7 us -> 33.2 us  [shift(): lax.ppermute(value, axis, [(i, (i + distance) % count) for i in range(cou...]
    ppermute x55 -> x32, waiting for transfers between devices: 66.4 us -> 28.7 us  [swap(): lax.ppermute(value, 'head', [(i, i ^ distance) for i in range(count)])]
    ppermute x55 -> x32, starting transfers between devices: 69.5 us -> 39.1 us  [swap(): lax.ppermute(value, 'head', [(i, i ^ distance) for i in range(count)])]
    psum x1 -> x0, blocking collectives: 26.5 us -> none  [on_device(): lax.psum((wide, dt_sums, taps_sums, gain_sums), ('seq', 'dp'))]
    ppermute x21 -> x3, starting transfers between devices: 26.6 us -> 0.18 us  [butterfly_sum(): value = value + lax.ppermute(value, axis, pairs)]
    psum x0 -> x1, waiting for transfers between devices: none -> 26 us  [on_device(): g_wide, g_w_out = lax.psum((g_wide, g_w_out), ('seq', 'dp'))]
    ppermute x30 -> x18, starting transfers between devices: 44.4 us -> 25.5 us  [shift(): lax.ppermute(value, axis, [(i, (i + distance) % count) for i in range(cou...]
  transfers between devices with their start and end apart: 106 -> 57, of which waited for: 34 -> 14; matrix products, arithmetic and copies ran while one was open for 14% -> 21% of each run, Pallas kernels for 17% -> 29%
where the time goes in v2:
time: 531 us; the launch traced here: 523 us
  Pallas kernels  158 us (30%)
  waiting for transfers between devices  123 us (23%)
  local copies, waits for them, and re-layouts  85.4 us (16%)
  starting transfers between devices  65.2 us (12%)
  between operations  40.4 us (8%)
  other arithmetic  36.4 us (7%)
  matrix products  14.6 us (3%)
    pallas_call x2, Pallas kernels, on_device(): backward(index, *sums, ssd, gate, d_scaled, conv, conv, states, gate_wide...  54.7 us
    ppermute x32, starting transfers between devices, swap(): lax.ppermute(value, 'head', [(i, i ^ distance) for i in range(count)])  39.1 us
    ppermute x3, waiting for transfers between devices, butterfly_sum(): value = value + lax.ppermute(value, axis, pairs)  34 us
    ppermute x18, waiting for transfers between devices, shift(): lax.ppermute(value, axis, [(i, (i + distance) % count) for i in range(cou...  33.2 us
    pallas_call x2, Pallas kernels, on_device(): forward(index, *x, w_z, w_x, w_rest, gain_here, taps, dt_params, skip_wid...  33 us
    pallas_call x2, Pallas kernels, weigh(): call(weight_kernel, 'weight_sums', chunks, [SCALARS] + x_specs + g_specs...  32.5 us
    ppermute x32, waiting for transfers between devices, swap(): lax.ppermute(value, 'head', [(i, i ^ distance) for i in range(count)])  28.7 us
    psum x1, waiting for transfers between devices, on_device(): g_wide, g_w_out = lax.psum((g_wide, g_w_out), ('seq', 'dp'))  26 us
  transfers between devices with their start and end apart: 57, of which 14 were waited for; matrix products, arithmetic and copies ran while one was open for 21% of the time, Pallas kernels for 29%

profile of v2, /device:TPU:0, one launch (start us, length us, event | category | flops | bytes accessed | tf_op | source)
XLA Modules:
  0.0 522.5 jit_solution(8697280902035130563)
XLA Ops:
  9.8 2.0 abs_reduce_fusion
  15.1 5.0 collective-permute-start
  32.3 10.5 %collective-permute-done.1 = bf16[2,256,256]{2,1,0:T(8,128)(2,1)} collective-permute-done((bf16[2,256,256]{2,1,0:T(8,128)(2,1)}, bf16[2,256,256]{2,1,0:T(8,128)(2,1)}, u32[]{:S(2)}, u32[]{:S(2)}) %collective-permute-start.1) | collective-permute-done | bytes 262176 | tf_op jit(solution)/shard_map/ppermute | solution.py:767
  59.2 2.9 maximum_bitcast_fusion.w_ref
  68.4 2.1 dynamic-slice_bitcast_fusion.5
  70.6 1.9 collective-permute-start.6
  73.7 3.0 collective-permute-start.7
  79.4 16.5 %forward_scan.2 = (f32[1024,512]{1,0:T(8,128)}, f32[1024,896]{1,0:T(8,128)}, f32[1024,512]{1,0:T(8,128)}, f32[4,512,128]{2,1,0:T(8,128)}) custom-call(s32[4]{0:T(128)} %copy-done.36, bf16[1024,256]{1,0:T(8,128)(2,1)} %copy-done, bf16[1024,256]{1,0:T(8,128)(2,1)} %copy-done.4, bf16[1024,256]{1,0:T(8,128)(2,1)} %copy-done.5, bf16[1024,256]{1,0:T(8,128)(2,1)} %copy-done.8, ...), custom_call_target="tpu_custom_call" | custom-call | flops 1000000000 | bytes 10000000 | tf_op jit(solution)/shard_map/forward_scan/pallas_call | solution.py:954
  108.7 10.5 %collective-permute-done.23.x2 = bf16[1024,256]{1,0:T(8,128)(2,1)S(1)} collective-permute-done((bf16[1024,256]{1,0:T(8,128)(2,1)S(1)}, bf16[1024,256]{1,0:T(8,128)(2,1)S(1)}, u32[]{:S(2)}, u32[]{:S(2)}) %collective-permute-start.23) | collective-permute-done | bytes 524320 | tf_op jit(solution)/shard_map/ppermute | solution.py:762
  121.9 2.2 constant_dynamic-slice_fusion.3.conv_ref.before_ref
  124.2 3.2 collective-permute-done.25
  128.2 16.5 %forward_scan.3 = (f32[1024,512]{1,0:T(8,128)}, f32[1024,896]{1,0:T(8,128)}, f32[1024,512]{1,0:T(8,128)}, f32[4,512,128]{2,1,0:T(8,128)}) custom-call(s32[4]{0:T(128)} %copy-done.36, bf16[1024,256]{1,0:T(8,128)(2,1)} %copy-done.2, bf16[1024,256]{1,0:T(8,128)(2,1)} %copy-done.6, bf16[1024,256]{1,0:T(8,128)(2,1)} %copy-done.7, bf16[1024,256]{1,0:T(8,128)(2,1)} %copy-done.9, ...), custom_call_target="tpu_custom_call" | custom-call | flops 1000000000 | bytes 10000000 | tf_op jit(solution)/shard_map/forward_scan/pallas_call | solution.py:954
  145.3 6.3 %gate_sums.2 = (f32[1024,512]{1,0:T(8,128)}, f32[4,8,256]{2,1,0:T(8,128)}) custom-call(s32[4]{0:T(128)} %iota.9.index_ref, bf16[4,1024,256]{2,1,0:T(8,128)(2,1)} %all-gather.6.cloned.1.call-done.g0.g1.g2.g3, bf16[4,1024,256]{2,1,0:T(8,128)(2,1)} %all-gather.6.cloned.1.call-done.g0.g1.g2.g3, bf16[4,1024,256]{2,1,0:T(8,128)(2,1)} %all-gather.6.cloned.1.call-done.g0.g1.g2.g3, ...), custom_call_target="tpu_custom_call" | custom-call | flops 1000000000 | bytes 1000000 | tf_op jit(solution)/shard_map/gate_sums/pallas_call | solution.py:1052
  152.7 2.4 collective-permute-start.13
  155.1 2.1 constant_dynamic-slice_fusion.2.conv_ref.before_ref
  158.3 27.4 %backward_scan.2 = (bf16[1024,512]{1,0:T(8,128)(2,1)}, bf16[1024,512]{1,0:T(8,128)(2,1)}, bf16[1024,512]{1,0:T(8,128)(2,1)}, bf16[1024,128]{1,0:T(8,128)(2,1)}, ...) custom-call(s32[4]{0:T(128)} %copy-done.36, f32[4,8,256]{2,1,0:T(8,128)} %get-tuple-element.119.q0, ...), custom_call_target="tpu_custom_call" | custom-call | flops 2000000000 | bytes 10000000 | tf_op jit(solution)/shard_map/backward_scan/pallas_call | solution.py:1063
  186.3 6.7 %gate_sums.3 = (f32[1024,512]{1,0:T(8,128)}, f32[4,8,256]{2,1,0:T(8,128)}) custom-call(s32[4]{0:T(128)} %iota.10.index_ref, bf16[4,1024,256]{2,1,0:T(8,128)(2,1)} %all-gather.8.cloned.1.call-done.g0.g1.g2.g3, bf16[4,1024,256]{2,1,0:T(8,128)(2,1)} %all-gather.8.cloned.1.call-done.g0.g1.g2.g3, bf16[4,1024,256]{2,1,0:T(8,128)(2,1)} %all-gather.8.cloned.1.call-done.g0.g1.g2.g3, ...), custom_call_target="tpu_custom_call" | custom-call | flops 1000000000 | bytes 1000000 | tf_op jit(solution)/shard_map/gate_sums/pallas_call | solution.py:1052
  193.8 2.0 collective-permute-start.27
  204.0 2.0 collective-permute-start.15
  209.8 27.3 %backward_scan.3 = (bf16[1024,512]{1,0:T(8,128)(2,1)}, bf16[1024,512]{1,0:T(8,128)(2,1)}, bf16[1024,512]{1,0:T(8,128)(2,1)}, bf16[1024,128]{1,0:T(8,128)(2,1)}, ...) custom-call(s32[4]{0:T(128)} %copy-done.36, f32[4,8,256]{2,1,0:T(8,128)} %get-tuple-element.132.q0, ...), custom_call_target="tpu_custom_call" | custom-call | flops 2000000000 | bytes 10000000 | tf_op jit(solution)/shard_map/backward_scan/pallas_call | solution.py:1063
  237.2 2.6 fusion.5
  239.7 2.5 fusion.6
  249.5 2.0 collective-permute-start.30
  253.3 2.5 fusion.7
  256.6 2.1 collective-permute-start.19
  268.0 2.1 collective-permute-start.34
  278.7 6.7 %collective-permute-done.18 = f16[1024,256]{1,0:T(8,128)(2,1)S(1)} collective-permute-done((f16[1024,256]{1,0:T(8,128)(2,1)}, f16[1024,256]{1,0:T(8,128)(2,1)S(1)}, u32[]{:S(2)}, u32[]{:S(2)}) %collective-permute-start.18) | collective-permute-done | bytes 524320 | tf_op jit(solution)/shard_map/ppermute | solution.py:762
  288.7 15.2 %weight_sums.2 = (f32[1024,1024]{1,0:T(8,128)}, f32[1024,1024]{1,0:T(8,128)}, f32[1024,128]{1,0:T(8,128)}, f32[512,1024]{1,0:T(8,128)}) custom-call(s32[4]{0:T(128)} %copy-done.36, bf16[1024,256]{1,0:T(8,128)(2,1)} %copy-done, bf16[1024,256]{1,0:T(8,128)(2,1)} %copy-done.4, bf16[1024,256]{1,0:T(8,128)(2,1)} %copy-done.5, bf16[1024,256]{1,0:T(8,128)(2,1)} %copy-done.8, ...), custom_call_target="tpu_custom_call" | custom-call | flops 2000000000 | bytes 10000000 | tf_op jit(solution)/shard_map/weight_sums/pallas_call | solution.py:1004
  303.9 7.3 %input_sums.2 = (f32[4,264,256]{2,1,0:T(8,128)}, bf16[4,272,256]{2,1,0:T(8,128)(2,1)}, bf16[4,272,256]{2,1,0:T(8,128)(2,1)}, bf16[4,272,256]{2,1,0:T(8,128)(2,1)}, f32[1024,64]{1,0:T(8,128)}, /*index=5*/f32[8,64]{1,0:T(8,128)}) custom-call(s32[4]{0:T(128)} %copy-done.36, bf16[1024,256]{1,0:T(8,128)(2,1)} %copy-done, bf16[1024,256]{1,0:T(8,128)(2,1)} %copy-done.4, ...), custom_call_target="tpu_custom_call" | custom-call | flops 1000000000 | bytes 10000000 | tf_op jit(solution)/shard_map/input_sums/pallas_call | solution.py:1104
  311.2 17.3 %weight_sums.3 = (f32[1024,1024]{1,0:T(8,128)}, f32[1024,1024]{1,0:T(8,128)}, f32[1024,128]{1,0:T(8,128)}, f32[512,1024]{1,0:T(8,128)}) custom-call(s32[4]{0:T(128)} %copy-done.36, bf16[1024,256]{1,0:T(8,128)(2,1)} %copy-done.2, bf16[1024,256]{1,0:T(8,128)(2,1)} %copy-done.6, bf16[1024,256]{1,0:T(8,128)(2,1)} %copy-done.7, bf16[1024,256]{1,0:T(8,128)(2,1)} %copy-done.9, ...), custom_call_target="tpu_custom_call" | custom-call | flops 2000000000 | bytes 10000000 | tf_op jit(solution)/shard_map/weight_sums/pallas_call | solution.py:1004
  328.5 1.9 reshape.200
  332.7 1.8 fusion.4
  337.0 3.8 collective-permute-start.35
  342.0 7.4 %input_sums.3 = (f32[4,264,256]{2,1,0:T(8,128)}, bf16[4,272,256]{2,1,0:T(8,128)(2,1)}, bf16[4,272,256]{2,1,0:T(8,128)(2,1)}, bf16[4,272,256]{2,1,0:T(8,128)(2,1)}, f32[1024,64]{1,0:T(8,128)}, /*index=5*/f32[8,64]{1,0:T(8,128)}) custom-call(s32[4]{0:T(128)} %copy-done.36, bf16[1024,256]{1,0:T(8,128)(2,1)} %copy-done.2, bf16[1024,256]{1,0:T(8,128)(2,1)} %copy-done.6, ...), custom_call_target="tpu_custom_call" | custom-call | flops 1000000000 | bytes 10000000 | tf_op jit(solution)/shard_map/input_sums/pallas_call | solution.py:1104
  354.4 7.3 %collective-permute-done.37 = bf16[256,256]{1,0:T(8,128)(2,1)S(1)} collective-permute-done((bf16[256,256]{1,0:T(8,128)(2,1)S(1)}, bf16[256,256]{1,0:T(8,128)(2,1)S(1)}, u32[]{:S(2)}, u32[]{:S(2)}) %collective-permute-start.37) | collective-permute-done | bytes 131104 | tf_op jit(solution)/shard_map/ppermute | solution.py:767
  362.6 2.5 collective-permute-start.46
  366.1 5.0 input_gradient.2
  371.1 7.7 %collective-permute-done.45.r2 = bf16[4,272,256]{2,1,0:T(8,128)(2,1)S(1)} collective-permute-done((bf16[4,272,256]{2,1,0:T(8,128)(2,1)}, bf16[4,272,256]{2,1,0:T(8,128)(2,1)S(1)}, u32[]{:S(2)}, u32[]{:S(2)}) %collective-permute-start.45) | collective-permute-done | bytes 557088 | tf_op jit(solution)/shard_map/ppermute | solution.py:762
  379.8 5.1 input_gradient.3
  384.9 1.9 slice_add_fusion
  395.6 2.0 collective-permute-start.49
  404.3 2.2 concatenate.146
  408.3 3.2 collective-permute-done.48
  417.6 10.3 %collective-permute-done.42 = f16[272,256]{1,0:T(8,128)(2,1)} collective-permute-done((f16[272,256]{1,0:T(8,128)(2,1)}, f16[272,256]{1,0:T(8,128)(2,1)}, u32[]{:S(2)}, u32[]{:S(2)}) %collective-permute-start.42) | collective-permute-done | bytes 139296 | tf_op jit(solution)/shard_map/ppermute | solution.py:767
  441.4 15.2 %collective-permute-done.51 = f32[622,128]{1,0:T(8,128)S(1)} collective-permute-done((f32[622,128]{1,0:T(8,128)S(1)}, f32[622,128]{1,0:T(8,128)S(1)}, u32[]{:S(2)}, u32[]{:S(2)}) %collective-permute-start.51) | collective-permute-done | bytes 318496 | tf_op jit(solution)/shard_map/ppermute | solution.py:845
  458.3 18.9 %collective-permute-done.52 = f32[622,128]{1,0:T(8,128)S(1)} collective-permute-done((f32[622,128]{1,0:T(8,128)S(1)}, f32[622,128]{1,0:T(8,128)S(1)}, u32[]{:S(2)}, u32[]{:S(2)}) %collective-permute-start.52) | collective-permute-done | bytes 318496 | tf_op jit(solution)/shard_map/ppermute | solution.py:845
  483.6 26.0 %all-reduce.18.cloned.1.call-done = (f32[1024,1024]{1,0:T(8,128)}, f32[512,1024]{1,0:T(8,128)}) async-done(((f32[1024,1024]{1,0:T(8,128)}, f32[512,1024]{1,0:T(8,128)}), (f32[1024,1024]{1,0:T(8,128)}, f32[512,1024]{1,0:T(8,128)})) %all-reduce.18.cloned.1.call-update) | async-done | bytes 6291472 | tf_op jit(solution)/shard_map/psum | solution.py:1110
  509.6 4.8 fusion.41
  (391 shorter events, 142.5 us)
Async XLA Ops:
  7.2 45.1 %all-gather.10.cloned.1.call-start = ((), (), s32[]{:S(2)}) async-start(), calls=%async_computation.2 | async-start | bytes 1474560 | tf_op jit(solution)/shard_map/all_gather | solution.py:881
  14.1 130.6 %all-gather.6.cloned.1.call-start = ((), (), s32[]{:S(2)}) async-start(), calls=%async_computation | async-start | bytes 2621440 | tf_op jit(solution)/shard_map/all_gather | solution.py:959
  15.1 17.1 %collective-permute-start = (bf16[2,256,256]{2,1,0:T(8,128)(2,1)}, bf16[2,256,256]{2,1,0:T(8,128)(2,1)S(1)}, u32[]{:S(2)}, u32[]{:S(2)}) collective-permute-start(bf16[2,256,256]{2,1,0:T(8,128)(2,1)} %get-tuple-element.252), channel_id=1, source_target_pairs={{0,24},{8,0},{16,8},{24,16},{1,25},{9,1},{17,9},{25,17},{2,26},{10... | collective-permute-start | bytes 786440 | tf_op jit(solution)/shard_map/ppermute | solution.py:767
  20.2 22.6 %collective-permute-start.1 = (bf16[2,256,256]{2,1,0:T(8,128)(2,1)}, bf16[2,256,256]{2,1,0:T(8,128)(2,1)}, u32[]{:S(2)}, u32[]{:S(2)}) collective-permute-start(bf16[2,256,256]{2,1,0:T(8,128)(2,1)} %get-tuple-element.251), channel_id=1, source_target_pairs={{0,16},{8,24},{16,0},{24,8},{1,17},{9,25},{17,1},{25,9},{2,18},{10... | collective-permute-start | bytes 786440 | tf_op jit(solution)/shard_map/ppermute | solution.py:767
  20.2 23.6 %collective-permute-start.2 = (bf16[2,256,256]{2,1,0:T(8,128)(2,1)}, bf16[2,256,256]{2,1,0:T(8,128)(2,1)}, u32[]{:S(2)}, u32[]{:S(2)}) collective-permute-start(bf16[2,256,256]{2,1,0:T(8,128)(2,1)} %get-tuple-element.250), channel_id=1, source_target_pairs={{0,8},{8,16},{16,24},{24,0},{1,9},{9,17},{17,25},{25,1},{2,10},{10... | collective-permute-start | bytes 786440 | tf_op jit(solution)/shard_map/ppermute | solution.py:767
  47.9 14.1 %collective-permute-start.3 = (bf16[1024,256]{1,0:T(8,128)(2,1)S(1)}, bf16[1024,256]{1,0:T(8,128)(2,1)S(1)}, u32[]{:S(2)}, u32[]{:S(2)}) collective-permute-start(bf16[1024,256]{1,0:T(8,128)(2,1)S(1)} %get-tuple-element.223.x0), channel_id=1, source_target_pairs={{0,1},{1,0},{2,3},{3,2},{4,5},{5,4},{6,7},{7,6},{8,9},{9,8},{10,11... | collective-permute-start | bytes 1572872 | tf_op jit(solution)/shard_map/ppermute | solution.py:762
  49.5 12.5 %collective-permute-start.4 = (bf16[1024,256]{1,0:T(8,128)(2,1)S(1)}, bf16[1024,256]{1,0:T(8,128)(2,1)S(1)}, u32[]{:S(2)}, u32[]{:S(2)}) collective-permute-start(bf16[1024,256]{1,0:T(8,128)(2,1)S(1)} %get-tuple-element.223.x0), channel_id=1, source_target_pairs={{0,2},{1,3},{2,0},{3,1},{4,6},{5,7},{6,4},{7,5},{8,10},{9,11},{10,... | collective-permute-start | bytes 1572872 | tf_op jit(solution)/shard_map/ppermute | solution.py:762
  65.0 12.7 %collective-permute-start.9 = (bf16[512,256]{1,0:T(8,128)(2,1)}, bf16[512,256]{1,0:T(8,128)(2,1)}, u32[]{:S(2)}, u32[]{:S(2)}) collective-permute-start(bf16[512,256]{1,0:T(8,128)(2,1)} %slice.294), channel_id=1, source_target_pairs={{0,1},{1,0},{2,3},{3,2},{4,5},{5,4},{6,7},{7,6},{8,9},{9,8},{10,11... | collective-permute-start | bytes 786440 | tf_op jit(solution)/shard_map/ppermute | solution.py:762
  65.5 30.4 %collective-permute-start.10 = (bf16[1024,256]{1,0:T(8,128)(2,1)S(1)}, bf16[1024,256]{1,0:T(8,128)(2,1)S(1)}, u32[]{:S(2)}, u32[]{:S(2)}) collective-permute-start(bf16[1024,256]{1,0:T(8,128)(2,1)S(1)} %get-tuple-element.113.x0), channel_id=1, source_target_pairs={{0,1},{1,0},{2,3},{3,2},{4,5},{5,4},{6,7},{7,6},{8,9},{9,8},{10,11... | collective-permute-start | bytes 1572872 | tf_op jit(solution)/shard_map/ppermute | solution.py:762
  70.5 25.5 %collective-permute-start.5 = (bf16[2,256,256]{2,1,0:T(8,128)(2,1)}, bf16[2,256,256]{2,1,0:T(8,128)(2,1)S(1)}, u32[]{:S(2)}, u32[]{:S(2)}) collective-permute-start(bf16[2,256,256]{2,1,0:T(8,128)(2,1)} %get-tuple-element.248), channel_id=1, source_target_pairs={{0,8},{8,16},{16,24},{24,0},{1,9},{9,17},{17,25},{25,1},{2,10},{10... | collective-permute-start | bytes 786440 | tf_op jit(solution)/shard_map/ppermute | solution.py:767
  70.6 25.3 %collective-permute-start.6 = (bf16[2,256,256]{2,1,0:T(8,128)(2,1)}, bf16[2,256,256]{2,1,0:T(8,128)(2,1)}, u32[]{:S(2)}, u32[]{:S(2)}) collective-permute-start(bf16[2,256,256]{2,1,0:T(8,128)(2,1)} %get-tuple-element.247), channel_id=1, source_target_pairs={{0,16},{8,24},{16,0},{24,8},{1,17},{9,25},{17,1},{25,9},{2,18},{10... | collective-permute-start | bytes 786440 | tf_op jit(solution)/shard_map/ppermute | solution.py:767
  73.7 22.2 %collective-permute-start.7 = (bf16[2,256,256]{2,1,0:T(8,128)(2,1)}, bf16[2,256,256]{2,1,0:T(8,128)(2,1)S(1)}, u32[]{:S(2)}, u32[]{:S(2)}) collective-permute-start(bf16[2,256,256]{2,1,0:T(8,128)(2,1)} %get-tuple-element.246), channel_id=1, source_target_pairs={{0,24},{8,0},{16,8},{24,16},{1,25},{9,1},{17,9},{25,17},{2,26},{10... | collective-permute-start | bytes 786440 | tf_op jit(solution)/shard_map/ppermute | solution.py:767
  99.4 86.3 %all-gather.8.cloned.1.call-start = ((), (), s32[]{:S(2)}) async-start(), calls=%async_computation.1 | async-start | bytes 2621440 | tf_op jit(solution)/shard_map/all_gather | solution.py:959
  100.1 409.5 %all-reduce.18.cloned.1.call-start = ((), (), s32[]{:S(2)}) async-start(), calls=%async_computation.3 | async-start | bytes 12582912 | tf_op jit(solution)/shard_map/psum | solution.py:1110
  100.5 18.7 %collective-permute-start.23 = (bf16[1024,256]{1,0:T(8,128)(2,1)S(1)}, bf16[1024,256]{1,0:T(8,128)(2,1)S(1)}, u32[]{:S(2)}, u32[]{:S(2)}) collective-permute-start(bf16[1024,256]{1,0:T(8,128)(2,1)S(1)} %get-tuple-element.113.x0), channel_id=1, source_target_pairs={{0,2},{1,3},{2,0},{3,1},{4,6},{5,7},{6,4},{7,5},{8,10},{9,11},{10,... | collective-permute-start | bytes 1572872 | tf_op jit(solution)/shard_map/ppermute | solution.py:762
  101.2 23.0 %collective-permute-start.24 = (bf16[512,256]{1,0:T(8,128)(2,1)S(1)}, bf16[512,256]{1,0:T(8,128)(2,1)S(1)}, u32[]{:S(2)}, u32[]{:S(2)}) collective-permute-start(bf16[512,256]{1,0:T(8,128)(2,1)S(1)} %slice.372), channel_id=1, source_target_pairs={{0,2},{1,3},{2,0},{3,1},{4,6},{5,7},{6,4},{7,5},{8,10},{9,11},{10,... | collective-permute-start | bytes 786440 | tf_op jit(solution)/shard_map/ppermute | solution.py:762
  193.0 15.4 %collective-permute-start.26 = (f32[4,8,256]{2,1,0:T(8,128)}, f32[4,8,256]{2,1,0:T(8,128)S(1)}, u32[]{:S(2)}, u32[]{:S(2)}) collective-permute-start(f32[4,8,256]{2,1,0:T(8,128)} %get-tuple-element.132.q0), channel_id=1, source_target_pairs={{0,1},{1,0},{2,3},{3,2},{4,5},{5,4},{6,7},{7,6},{8,9},{9,8},{10,11... | collective-permute-start | bytes 98312 | tf_op jit(solution)/shard_map/ppermute | solution.py:762
  193.8 15.4 %collective-permute-start.27 = (f32[4,8,256]{2,1,0:T(8,128)}, f32[4,8,256]{2,1,0:T(8,128)S(1)}, u32[]{:S(2)}, u32[]{:S(2)}) collective-permute-start(f32[4,8,256]{2,1,0:T(8,128)} %get-tuple-element.132.q0), channel_id=1, source_target_pairs={{0,2},{1,3},{2,0},{3,1},{4,6},{5,7},{6,4},{7,5},{8,10},{9,11},{10,... | collective-permute-start | bytes 98312 | tf_op jit(solution)/shard_map/ppermute | solution.py:762
  195.8 13.4 %collective-permute-start.28 = (f32[4,8,256]{2,1,0:T(8,128)}, f32[4,8,256]{2,1,0:T(8,128)S(1)}, u32[]{:S(2)}, u32[]{:S(2)}) collective-permute-start(f32[4,8,256]{2,1,0:T(8,128)} %get-tuple-element.132.q0), channel_id=1, source_target_pairs={{0,3},{1,2},{2,1},{3,0},{4,7},{5,6},{6,5},{7,4},{8,11},{9,10},{10,... | collective-permute-start | bytes 98312 | tf_op jit(solution)/shard_map/ppermute | solution.py:762
  202.5 53.3 %collective-permute-start.14 = (f16[528,128]{1,0:T(8,128)(2,1)S(1)}, f16[528,128]{1,0:T(8,128)(2,1)}, u32[]{:S(2)}, u32[]{:S(2)}) collective-permute-start(f16[528,128]{1,0:T(8,128)(2,1)S(1)} %concatenate.121), channel_id=1, source_target_pairs={{0,1},{1,0},{2,3},{3,2},{4,5},{5,4},{6,7},{7,6},{8,9},{9,8},{10,11... | collective-permute-start | bytes 405512 | tf_op jit(solution)/shard_map/ppermute | solution.py:762
  204.0 52.6 %collective-permute-start.15 = (f16[528,128]{1,0:T(8,128)(2,1)}, f16[528,128]{1,0:T(8,128)(2,1)}, u32[]{:S(2)}, u32[]{:S(2)}) collective-permute-start(f16[528,128]{1,0:T(8,128)(2,1)} %concatenate.123), channel_id=1, source_target_pairs={{0,2},{1,3},{2,0},{3,1},{4,6},{5,7},{6,4},{7,5},{8,10},{9,11},{10,... | collective-permute-start | bytes 405512 | tf_op jit(solution)/shard_map/ppermute | solution.py:762
  208.3 48.3 %collective-permute-start.16 = (f16[528,128]{1,0:T(8,128)(2,1)}, f16[528,128]{1,0:T(8,128)(2,1)}, u32[]{:S(2)}, u32[]{:S(2)}) collective-permute-start(f16[528,128]{1,0:T(8,128)(2,1)} %concatenate.125), channel_id=1, source_target_pairs={{0,3},{1,2},{2,1},{3,0},{4,7},{5,6},{6,5},{7,4},{8,11},{9,10},{10,... | collective-permute-start | bytes 405512 | tf_op jit(solution)/shard_map/ppermute | solution.py:762
  247.0 19.7 %collective-permute-start.29 = (f16[528,128]{1,0:T(8,128)(2,1)}, f16[528,128]{1,0:T(8,128)(2,1)}, u32[]{:S(2)}, u32[]{:S(2)}) collective-permute-start(f16[528,128]{1,0:T(8,128)(2,1)} %concatenate.129), channel_id=1, source_target_pairs={{0,1},{1,0},{2,3},{3,2},{4,5},{5,4},{6,7},{7,6},{8,9},{9,8},{10,11... | collective-permute-start | bytes 405512 | tf_op jit(solution)/shard_map/ppermute | solution.py:762
  249.5 18.5 %collective-permute-start.30 = (f16[528,128]{1,0:T(8,128)(2,1)}, f16[528,128]{1,0:T(8,128)(2,1)}, u32[]{:S(2)}, u32[]{:S(2)}) collective-permute-start(f16[528,128]{1,0:T(8,128)(2,1)} %concatenate.131), channel_id=1, source_target_pairs={{0,2},{1,3},{2,0},{3,1},{4,6},{5,7},{6,4},{7,5},{8,10},{9,11},{10,... | collective-permute-start | bytes 405512 | tf_op jit(solution)/shard_map/ppermute | solution.py:762
  255.8 12.3 %collective-permute-start.31 = (f16[528,128]{1,0:T(8,128)(2,1)S(1)}, f16[528,128]{1,0:T(8,128)(2,1)S(1)}, u32[]{:S(2)}, u32[]{:S(2)}) collective-permute-start(f16[528,128]{1,0:T(8,128)(2,1)S(1)} %concatenate.133), channel_id=1, source_target_pairs={{0,3},{1,2},{2,1},{3,0},{4,7},{5,6},{6,5},{7,4},{8,11},{9,10},{10,... | collective-permute-start | bytes 405512 | tf_op jit(solution)/shard_map/ppermute | solution.py:762
  256.6 20.7 %collective-permute-start.19 = (f16[1024,256]{1,0:T(8,128)(2,1)}, f16[1024,256]{1,0:T(8,128)(2,1)S(1)}, u32[]{:S(2)}, u32[]{:S(2)}) collective-permute-start(f16[1024,256]{1,0:T(8,128)(2,1)} %fusion.3), channel_id=1, source_target_pairs={{0,3},{1,2},{2,1},{3,0},{4,7},{5,6},{6,5},{7,4},{8,11},{9,10},{10,... | collective-permute-start | bytes 1572872 | tf_op jit(solution)/shard_map/ppermute | solution.py:762
  258.7 26.7 %collective-permute-start.18 = (f16[1024,256]{1,0:T(8,128)(2,1)}, f16[1024,256]{1,0:T(8,128)(2,1)S(1)}, u32[]{:S(2)}, u32[]{:S(2)}) collective-permute-start(f16[1024,256]{1,0:T(8,128)(2,1)} %fusion.2), channel_id=1, source_target_pairs={{0,2},{1,3},{2,0},{3,1},{4,6},{5,7},{6,4},{7,5},{8,10},{9,11},{10,... | collective-permute-start | bytes 1572872 | tf_op jit(solution)/shard_map/ppermute | solution.py:762
  266.6 18.7 %collective-permute-start.17 = (f16[1024,256]{1,0:T(8,128)(2,1)S(1)}, f16[1024,256]{1,0:T(8,128)(2,1)S(1)}, u32[]{:S(2)}, u32[]{:S(2)}) collective-permute-start(f16[1024,256]{1,0:T(8,128)(2,1)S(1)} %copy-done.57), channel_id=1, source_target_pairs={{0,1},{1,0},{2,3},{3,2},{4,5},{5,4},{6,7},{7,6},{8,9},{9,8},{10,11... | collective-permute-start | bytes 1572872 | tf_op jit(solution)/shard_map/ppermute | solution.py:762
  268.0 62.4 %collective-permute-start.34 = (f16[1024,256]{1,0:T(8,128)(2,1)}, f16[1024,256]{1,0:T(8,128)(2,1)}, u32[]{:S(2)}, u32[]{:S(2)}) collective-permute-start(f16[1024,256]{1,0:T(8,128)(2,1)} %fusion.7), channel_id=1, source_target_pairs={{0,3},{1,2},{2,1},{3,0},{4,7},{5,6},{6,5},{7,4},{8,11},{9,10},{10,... | collective-permute-start | bytes 1572872 | tf_op jit(solution)/shard_map/ppermute | solution.py:762
  270.1 60.6 %collective-permute-start.33 = (f16[1024,256]{1,0:T(8,128)(2,1)}, f16[1024,256]{1,0:T(8,128)(2,1)}, u32[]{:S(2)}, u32[]{:S(2)}) collective-permute-start(f16[1024,256]{1,0:T(8,128)(2,1)} %fusion.6), channel_id=1, source_target_pairs={{0,2},{1,3},{2,0},{3,1},{4,6},{5,7},{6,4},{7,5},{8,10},{9,11},{10,... | collective-permute-start | bytes 1572872 | tf_op jit(solution)/shard_map/ppermute | solution.py:762
  277.3 54.5 %collective-permute-start.32 = (f16[1024,256]{1,0:T(8,128)(2,1)}, f16[1024,256]{1,0:T(8,128)(2,1)}, u32[]{:S(2)}, u32[]{:S(2)}) collective-permute-start(f16[1024,256]{1,0:T(8,128)(2,1)} %fusion.5), channel_id=1, source_target_pairs={{0,1},{1,0},{2,3},{3,2},{4,5},{5,4},{6,7},{7,6},{8,9},{9,8},{10,11... | collective-permute-start | bytes 1572872 | tf_op jit(solution)/shard_map/ppermute | solution.py:762
  286.5 48.9 %collective-permute-start.20 = (bf16[256,256]{1,0:T(8,128)(2,1)}, bf16[256,256]{1,0:T(8,128)(2,1)S(1)}, u32[]{:S(2)}, u32[]{:S(2)}) collective-permute-start(bf16[256,256]{1,0:T(8,128)(2,1)} %get-tuple-element.255), channel_id=1, source_target_pairs={{0,24},{8,0},{16,8},{24,16},{1,25},{9,1},{17,9},{25,17},{2,26},{10... | collective-permute-start | bytes 393224 | tf_op jit(solution)/shard_map/ppermute | solution.py:767
  287.0 50.0 %collective-permute-start.21 = (bf16[256,256]{1,0:T(8,128)(2,1)}, bf16[256,256]{1,0:T(8,128)(2,1)S(1)}, u32[]{:S(2)}, u32[]{:S(2)}) collective-permute-start(bf16[256,256]{1,0:T(8,128)(2,1)} %get-tuple-element.254), channel_id=1, source_target_pairs={{0,16},{8,24},{16,0},{24,8},{1,17},{9,25},{17,1},{25,9},{2,18},{10... | collective-permute-start | bytes 393224 | tf_op jit(solution)/shard_map/ppermute | solution.py:767
  330.7 31.8 %collective-permute-start.38 = (bf16[4,272,256]{2,1,0:T(8,128)(2,1)}, bf16[4,272,256]{2,1,0:T(8,128)(2,1)}, u32[]{:S(2)}, u32[]{:S(2)}) collective-permute-start(bf16[4,272,256]{2,1,0:T(8,128)(2,1)} %get-tuple-element.162), channel_id=1, source_target_pairs={{0,1},{1,0},{2,3},{3,2},{4,5},{5,4},{6,7},{7,6},{8,9},{9,8},{10,11... | collective-permute-start | bytes 1671176 | tf_op jit(solution)/shard_map/ppermute | solution.py:762
  331.8 33.3 %collective-permute-start.39 = (bf16[4,272,256]{2,1,0:T(8,128)(2,1)}, bf16[4,272,256]{2,1,0:T(8,128)(2,1)}, u32[]{:S(2)}, u32[]{:S(2)}) collective-permute-start(bf16[4,272,256]{2,1,0:T(8,128)(2,1)} %get-tuple-element.163), channel_id=1, source_target_pairs={{0,2},{1,3},{2,0},{3,1},{4,6},{5,7},{6,4},{7,5},{8,10},{9,11},{10,... | collective-permute-start | bytes 1671176 | tf_op jit(solution)/shard_map/ppermute | solution.py:762
  335.4 29.8 %collective-permute-start.40 = (bf16[4,272,256]{2,1,0:T(8,128)(2,1)}, bf16[4,272,256]{2,1,0:T(8,128)(2,1)S(1)}, u32[]{:S(2)}, u32[]{:S(2)}) collective-permute-start(bf16[4,272,256]{2,1,0:T(8,128)(2,1)} %get-tuple-element.164), channel_id=1, source_target_pairs={{0,3},{1,2},{2,1},{3,0},{4,7},{5,6},{6,5},{7,4},{8,11},{9,10},{10,... | collective-permute-start | bytes 1671176 | tf_op jit(solution)/shard_map/ppermute | solution.py:762
  337.0 15.0 %collective-permute-start.35 = (bf16[256,256]{1,0:T(8,128)(2,1)S(1)}, bf16[256,256]{1,0:T(8,128)(2,1)S(1)}, u32[]{:S(2)}, u32[]{:S(2)}) collective-permute-start(bf16[256,256]{1,0:T(8,128)(2,1)S(1)} %get-tuple-element.258), channel_id=1, source_target_pairs={{0,24},{8,0},{16,8},{24,16},{1,25},{9,1},{17,9},{25,17},{2,26},{10... | collective-permute-start | bytes 393224 | tf_op jit(solution)/shard_map/ppermute | solution.py:767
  352.9 18.2 %collective-permute-start.44 = (bf16[4,272,256]{2,1,0:T(8,128)(2,1)}, bf16[4,272,256]{2,1,0:T(8,128)(2,1)S(1)}, u32[]{:S(2)}, u32[]{:S(2)}) collective-permute-start(bf16[4,272,256]{2,1,0:T(8,128)(2,1)} %get-tuple-element.168), channel_id=1, source_target_pairs={{0,1},{1,0},{2,3},{3,2},{4,5},{5,4},{6,7},{7,6},{8,9},{9,8},{10,11... | collective-permute-start | bytes 1671176 | tf_op jit(solution)/shard_map/ppermute | solution.py:762
  361.7 17.0 %collective-permute-start.45 = (bf16[4,272,256]{2,1,0:T(8,128)(2,1)}, bf16[4,272,256]{2,1,0:T(8,128)(2,1)S(1)}, u32[]{:S(2)}, u32[]{:S(2)}) collective-permute-start(bf16[4,272,256]{2,1,0:T(8,128)(2,1)} %get-tuple-element.169), channel_id=1, source_target_pairs={{0,2},{1,3},{2,0},{3,1},{4,6},{5,7},{6,4},{7,5},{8,10},{9,11},{10,... | collective-permute-start | bytes 1671176 | tf_op jit(solution)/shard_map/ppermute | solution.py:762
  362.6 16.2 %collective-permute-start.46 = (bf16[4,272,256]{2,1,0:T(8,128)(2,1)}, bf16[4,272,256]{2,1,0:T(8,128)(2,1)S(1)}, u32[]{:S(2)}, u32[]{:S(2)}) collective-permute-start(bf16[4,272,256]{2,1,0:T(8,128)(2,1)} %get-tuple-element.170), channel_id=1, source_target_pairs={{0,3},{1,2},{2,1},{3,0},{4,7},{5,6},{6,5},{7,4},{8,11},{9,10},{10,... | collective-permute-start | bytes 1671176 | tf_op jit(solution)/shard_map/ppermute | solution.py:762
  394.1 17.4 %collective-permute-start.48 = (f16[272,256]{1,0:T(8,128)(2,1)}, f16[272,256]{1,0:T(8,128)(2,1)S(1)}, u32[]{:S(2)}, u32[]{:S(2)}) collective-permute-start(f16[272,256]{1,0:T(8,128)(2,1)} %concatenate.143), channel_id=1, source_target_pairs={{0,16},{8,24},{16,0},{24,8},{1,17},{9,25},{17,1},{25,9},{2,18},{10... | collective-permute-start | bytes 417800 | tf_op jit(solution)/shard_map/ppermute | solution.py:767
  395.6 18.3 %collective-permute-start.49 = (f16[272,256]{1,0:T(8,128)(2,1)}, f16[272,256]{1,0:T(8,128)(2,1)}, u32[]{:S(2)}, u32[]{:S(2)}) collective-permute-start(f16[272,256]{1,0:T(8,128)(2,1)} %concatenate.144), channel_id=1, source_target_pairs={{0,8},{8,16},{16,24},{24,0},{1,9},{9,17},{17,25},{25,1},{2,10},{10... | collective-permute-start | bytes 417800 | tf_op jit(solution)/shard_map/ppermute | solution.py:767
  398.3 17.5 %collective-permute-start.41 = (f16[272,256]{1,0:T(8,128)(2,1)}, f16[272,256]{1,0:T(8,128)(2,1)}, u32[]{:S(2)}, u32[]{:S(2)}) collective-permute-start(f16[272,256]{1,0:T(8,128)(2,1)} %concatenate.138), channel_id=1, source_target_pairs={{0,24},{8,0},{16,8},{24,16},{1,25},{9,1},{17,9},{25,17},{2,26},{10... | collective-permute-start | bytes 417800 | tf_op jit(solution)/shard_map/ppermute | solution.py:767
  400.8 27.1 %collective-permute-start.42 = (f16[272,256]{1,0:T(8,128)(2,1)}, f16[272,256]{1,0:T(8,128)(2,1)}, u32[]{:S(2)}, u32[]{:S(2)}) collective-permute-start(f16[272,256]{1,0:T(8,128)(2,1)} %concatenate.139), channel_id=1, source_target_pairs={{0,16},{8,24},{16,0},{24,8},{1,17},{9,25},{17,1},{25,9},{2,18},{10... | collective-permute-start | bytes 417800 | tf_op jit(solution)/shard_map/ppermute | solution.py:767
  402.5 27.3 %collective-permute-start.43 = (f16[272,256]{1,0:T(8,128)(2,1)}, f16[272,256]{1,0:T(8,128)(2,1)}, u32[]{:S(2)}, u32[]{:S(2)}) collective-permute-start(f16[272,256]{1,0:T(8,128)(2,1)} %concatenate.140), channel_id=1, source_target_pairs={{0,8},{8,16},{16,24},{24,0},{1,9},{9,17},{17,25},{25,1},{2,10},{10... | collective-permute-start | bytes 417800 | tf_op jit(solution)/shard_map/ppermute | solution.py:767
  411.5 28.7 %collective-permute-start.50 = (f32[622,128]{1,0:T(8,128)S(1)}, f32[622,128]{1,0:T(8,128)S(1)}, u32[]{:S(2)}, u32[]{:S(2)}) collective-permute-start(f32[622,128]{1,0:T(8,128)S(1)} %concatenate.146), channel_id=1, source_target_pairs={{0,4},{4,0},{1,5},{5,1},{2,6},{6,2},{3,7},{7,3},{8,12},{12,8},{9,1... | collective-permute-start | bytes 955400 | tf_op jit(solution)/shard_map/ppermute | solution.py:845
  440.3 16.3 %collective-permute-start.51 = (f32[622,128]{1,0:T(8,128)S(1)}, f32[622,128]{1,0:T(8,128)S(1)}, u32[]{:S(2)}, u32[]{:S(2)}) collective-permute-start(f32[622,128]{1,0:T(8,128)S(1)} %add.286), channel_id=1, source_target_pairs={{0,8},{8,0},{16,24},{24,16},{1,9},{9,1},{17,25},{25,17},{2,10},{10... | collective-permute-start | bytes 955400 | tf_op jit(solution)/shard_map/ppermute | solution.py:845
  456.6 20.6 %collective-permute-start.52 = (f32[622,128]{1,0:T(8,128)S(1)}, f32[622,128]{1,0:T(8,128)S(1)}, u32[]{:S(2)}, u32[]{:S(2)}) collective-permute-start(f32[622,128]{1,0:T(8,128)S(1)} %add.287), channel_id=1, source_target_pairs={{0,16},{8,24},{16,0},{24,8},{1,17},{9,25},{17,1},{25,9},{2,18},{10... | collective-permute-start | bytes 955400 | tf_op jit(solution)/shard_map/ppermute | solution.py:845
  (67 other events, 544.0 us)
Sparse Core Ops, SparseCore 0:
  14.3 30.4 all-gather.9
  99.5 37.6 all-gather.5
  139.0 35.0 all-gather.7
  330.5 179.0 all-reduce.17

commit v3 on v2

--- a/solution.py
+++ b/solution.py
@@ -612,11 +612,11 @@
     index_ref, x0, x1, x2, x3, g0, g1, g2, g3, gain_ref, w_ref, scaled_ref, d_gate_ref, d_x_ref,
     d_dt_ref, *rest,
 ):
-    *sums_so_far, d_normed_out, wide_out, dt_out, out_out = rest
+    *sums_so_far, d_normed_out, total_out, dt_out = rest
 
     @pl.when(pl.program_id(0) == 0)
     def _():
-        for i, ref in enumerate((wide_out, dt_out, out_out)):
+        for i, ref in enumerate((total_out, dt_out)):
             ref[...] = sums_so_far[i][...] if sums_so_far else jnp.zeros(ref.shape, F32)
 
     _, _, normed = normed_blocks((x0, x1, x2, x3), gain_ref)
@@ -627,9 +627,10 @@
     width = normed[0].shape[1]
     for k, (part, cot) in enumerate(zip(normed, (g0, g1, g2, g3))):
         rows = block_of(index_ref, k, width)
-        wide_out[rows, :] += dot_tn(part, d_wide)
+        total_out[rows, :] += dot_tn(part, d_wide)
         dt_out[rows, :] += dot_tn(part, d_dt)
-        out_out[:, k * width : (k + 1) * width] += dot_tn(scaled, cot[...])
+        columns = slice(k * width, (k + 1) * width)
+        total_out[4 * width :, columns] += dot_tn(scaled, cot[...])
         d_normed_out[:, k * width : (k + 1) * width] = dot_nn(d_all, w_ref[:, rows])
 
 
@@ -911,7 +912,7 @@
 
     tokens = []
     near = [swap(hidden[0], 1), swap(hidden[0], 2)]
-    pieces = exchange(after(out_grad, near).reshape((shards, each) + out_grad.shape[1:]), z)
+    pieces = exchange(after(out_grad, hidden).reshape((shards, each) + out_grad.shape[1:]), z)
     near, gain_here, w_rest, taps, w_out_back, w_back = after(
         (near, gain_here, w_rest, taps, w_out_back, w_back), hidden
     )
@@ -919,7 +920,7 @@
     for s in range(each):
         own = hidden[s]
         if s:
-            own = after(own, near)
+            own = after(own, tokens[-1][3])
             near = [swap(own, 1), swap(own, 2)]
         tokens.append([own] + near + [far_features(*near)])
     straight = jnp.arange(4, dtype=jnp.int32)
@@ -950,6 +951,7 @@
         [pltpu.VMEM((CHUNK + 8, conv_width), F32), pltpu.VMEM((inner, STATE), F32)],
         10**9, 10**7,
     )
+    tokens[0] = after(tokens[0], tokens[-1][1:3])
     ahead = [
         forward(index, *x, w_z, w_x, w_rest, gain_here, taps, dt_params, skip_wide, spread, lower)
         for x in tokens
@@ -998,7 +1000,7 @@
         ],
         2 * 10**9, 10**7,
     )
-    sum_shapes = [(full_width, 2 * inner), (full_width, LANES), (inner, full_width)]
+    sum_shapes = [(full_width + inner, full_width), (full_width, LANES)]
 
     def weigh(*args):
         return call(
@@ -1052,62 +1054,67 @@
         d_scaled, sums = score(straight, *[cotangent] * 4, w_out_back, ssd, gate, gate_wide)
         return d_scaled, [sums] + [swap(sums, k) for k in range(1, 4)]
 
-    behind, d_bc_all, blocks, outward = [], [], [], []
+    def d_bc_sends(d_bc):
+        power = exponent_of(jnp.max(jnp.abs(d_bc)))
+        parts = [
+            lax.dynamic_slice_in_dim(d_bc, index[k] * bc_here, bc_here, 1) for k in range(4)
+        ]
+        payloads = [
+            to_half(jnp.concatenate([p[: length // 2], p[length // 2 :]], axis=1), power)
+            for p in parts[1:]
+        ]
+        return parts[0], payloads
+
+    def d_bc_total(own, payloads):
+        total = sum(from_half(swap(part, k + 1))[0] for k, part in enumerate(payloads))
+        return own + jnp.concatenate([total[:, :bc_here], total[:, bc_here:]], axis=0)
+
+    behind, d_bc_all = [], []
     for s in range(each):
         gate, conv, ssd, states = ahead[s]
         cotangent = after(cotangents[s], behind[-1][0]) if behind else cotangents[s]
         d_scaled, sums = scores_of(s, cotangent)
         if behind:
-            sums = after(sums, outward[-1])
+            own, payloads = d_bc_sends(behind[-1][4])
+            sums = after(sums, payloads)
+            d_bc_all.append(d_bc_total(own, payloads))
         behind.append(
             backward(
                 index, *sums, ssd, gate, d_scaled, conv, conv, states, gate_wide, taps, dt_params,
                 skip_wide, spread, collect, lower, upper,
             )
         )
-        d_bc = behind[s][4]
-        power = exponent_of(jnp.max(jnp.abs(d_bc)))
-        parts = [
-            lax.dynamic_slice_in_dim(d_bc, index[k] * bc_here, bc_here, 1) for k in range(4)
-        ]
-        sent = [
-            swap(to_half(jnp.concatenate([p[: length // 2], p[length // 2 :]], axis=1), power), k)
-            for k, p in enumerate(parts)
-            if k
-        ]
-        total = sum(from_half(part)[0] for part in sent)
-        total = jnp.concatenate([total[:, :bc_here], total[:, bc_here:]], axis=0)
-        d_bc_all.append(parts[0] + total)
-
-        scaled = behind[s][0]
-        out_parts = [jnp.dot(scaled, part, preferred_element_type=F32) for part in w_out_parts]
-        outward.append([(out_parts[k] * out_scale).astype(jnp.float16) for k in range(1, 4)])
-        received = [swap(part, k + 1) for k, part in enumerate(after(outward[s], sent))]
-        block = tokens[s][0].astype(F32) + out_parts[0]
-        blocks.append((block + sum(part.astype(F32) for part in received) / out_scale).astype(BF))
-
-    g_sums, mixed = [], []
-    sent_blocks = [to_tokens(block, z) for block in blocks]
+
+    g_sums, mixed, d_normed_all = [], [], []
     for s in range(each):
         scaled, d_gate, d_x, d_dt, _, _, _ = behind[s]
-        if s == 0:
-            d_dt = after(d_dt, outward, blocks[:-1])
-        else:
-            d_dt = after(d_dt, mixed[-1][0])
+        d_dt = after(d_dt, behind[-1][0])
         d_normed, *g_sums = weigh(
             index, *tokens[s], *[cotangents[s]] * 4, gain_here, w_back, scaled, d_gate, d_x, d_dt,
             *g_sums,
         )
-        if s + 1 == each:
-            d_normed = after(d_normed, sent_blocks[:-1], blocks[-1])
+        d_normed_all.append(d_normed)
+    g_total, g_dt = g_sums
+    g_total_sum = lax.psum(g_total, ("seq", "dp"))
+
+    d_bc_all.append(d_bc_total(*d_bc_sends(after(behind[-1][4], g_total))))
+    for s in range(each):
+        d_normed = after(d_normed_all[s], g_total, [part[0] for part in mixed])
         conv_own = lax.dynamic_slice_in_dim(ahead[s][1], inner + me * bc_here, bc_here, 1)
         own, send1, send2, send3, g_bc, taps_sums = mix(
             index, *tokens[s], gain_here, w_bc_back, d_bc_all[s], conv_own, conv_own, taps_bc_own,
             d_normed,
         )
         mixed.append((own, (swap(send1, 1), swap(send2, 2), swap(send3, 3)), g_bc, taps_sums))
-    g_wide, g_dt, g_w_out = g_sums
-    g_wide, g_w_out = lax.psum((g_wide, g_w_out), ("seq", "dp"))
+    blocks = []
+    for s in range(each):
+        scaled = after(behind[s][0], mixed[-1][0])
+        out_parts = [jnp.dot(scaled, part, preferred_element_type=F32) for part in w_out_parts]
+        sent = [(out_parts[k] * out_scale).astype(jnp.float16) for k in range(1, 4)]
+        received = [swap(part, k + 1) for k, part in enumerate(after(sent, mixed[s][1]))]
+        block = tokens[s][0].astype(F32) + out_parts[0]
+        blocks.append((block + sum(part.astype(F32) for part in received) / out_scale).astype(BF))
+    sent_blocks = [to_tokens(block, z) for block in blocks]
     wide = sum(part[5] for part in behind)
     dt_sums = sum(part[6] for part in behind)
 
@@ -1138,8 +1145,8 @@
         joined_tokens(sent_blocks),
         joined_tokens(grads),
         gain_sums[0],
-        g_wide[:, :inner],
-        g_wide[:, inner:],
+        g_total_sum[:full_width, :inner],
+        g_total_sum[:full_width, inner:],
         g_bc,
         g_dt,
         wide[0:4],
@@ -1150,7 +1157,7 @@
         dt_sums[0, :heads],
         wide[6].reshape(heads, HEAD_DIM).sum(axis=1),
         wide[5],
-        g_w_out,
+        g_total_sum[full_width:],
     )
 
 

time: 531 us -> 502 us (0.945)
  waiting for transfers between devices: 123 us -> 93.1 us
  starting transfers between devices: 65.2 us -> 79.8 us
  local copies, waits for them, and re-layouts: 85.4 us -> 77.8 us
    psum x1, waiting for transfers between devices: 26 us -> 0.01 us  [on_device(): g_total_sum = lax.psum(g_total, ('seq', 'dp'))]
    ppermute x32, waiting for transfers between devices: 28.7 us -> 44.4 us  [swap(): lax.ppermute(value, 'head', [(i, i ^ distance) for i in range(count)])]
    ppermute x3, waiting for transfers between devices: 34 us -> 21.7 us  [butterfly_sum(): value = value + lax.ppermute(value, axis, pairs)]
    ppermute x18, starting transfers between devices: 25.5 us -> 35.8 us  [shift(): lax.ppermute(value, axis, [(i, (i + distance) % count) for i in range(cou...]
    ppermute x18, waiting for transfers between devices: 33.2 us -> 24.6 us  [shift(): lax.ppermute(value, axis, [(i, (i + distance) % count) for i in range(cou...]
    unnamed x162 -> x138, local copies, waits for them, and re-layouts: 20.8 us -> 14.7 us
    ppermute x3, starting transfers between devices: 0.18 us -> 5.58 us  [butterfly_sum(): value = value + lax.ppermute(value, axis, pairs)]
  transfers between devices with their start and end apart: 57 -> 57, of which waited for: 14 -> 16; matrix products, arithmetic and copies ran while one was open for 21% -> 21% of each run, Pallas kernels for 29% -> 31%
where the time goes in v3:
time: 502 us; the launch traced here: 494 us
  Pallas kernels  158 us (31%)
  waiting for transfers between devices  93.1 us (19%)
  starting transfers between devices  79.8 us (16%)
  local copies, waits for them, and re-layouts  77.8 us (15%)
  between operations  40.3 us (8%)
  other arithmetic  36.1 us (7%)
  matrix products  9.34 us (2%)
    pallas_call x2, Pallas kernels, on_device(): backward(index, *sums, ssd, gate, d_scaled, conv, conv, states, gate_wide...  54.3 us
    ppermute x32, waiting for transfers between devices, swap(): lax.ppermute(value, 'head', [(i, i ^ distance) for i in range(count)])  44.4 us
    ppermute x32, starting transfers between devices, swap(): lax.ppermute(value, 'head', [(i, i ^ distance) for i in range(count)])  38 us
    ppermute x18, starting transfers between devices, shift(): lax.ppermute(value, axis, [(i, (i + distance) % count) for i in range(cou...  35.8 us
    pallas_call x2, Pallas kernels, on_device(): forward(index, *x, w_z, w_x, w_rest, gain_here, taps, dt_params, skip_wid...  33.3 us
    pallas_call x2, Pallas kernels, weigh(): call(weight_kernel, 'weight_sums', chunks, [SCALARS] + x_specs + g_specs...  32.5 us
    ppermute x18, waiting for transfers between devices, shift(): lax.ppermute(value, axis, [(i, (i + distance) % count) for i in range(cou...  24.6 us
    ppermute x3, waiting for transfers between devices, butterfly_sum(): value = value + lax.ppermute(value, axis, pairs)  21.7 us
  transfers between devices with their start and end apart: 57, of which 16 were waited for; matrix products, arithmetic and copies ran while one was open for 21% of the time, Pallas kernels for 31%

profile of v3, /device:TPU:0, one launch (start us, length us, event | category | flops | bytes accessed | tf_op | source)
XLA Modules:
  0.0 494.0 jit_solution(18400300289562666452)
XLA Ops:
  7.3 2.1 abs_reduce_fusion
  12.4 1.7 concatenate.112
  15.1 3.0 collective-permute-start.2
  18.1 2.6 collective-permute-start.1
  33.1 2.2 collective-permute-done
  36.4 1.8 collective-permute-done.1
  53.6 2.9 maximum_bitcast_fusion.w_ref
  59.6 4.9 collective-permute-done.5
  68.8 6.4 %collective-permute-start.11 = (bf16[2,256,256]{2,1,0:T(8,128)(2,1)}, bf16[2,256,256]{2,1,0:T(8,128)(2,1)S(1)}, u32[]{:S(2)}, u32[]{:S(2)}) collective-permute-start(bf16[2,256,256]{2,1,0:T(8,128)(2,1)} %get-tuple-element.256), channel_id=1, source_target_pairs={{0,24},{8,0},{16,8},{24,16},{1,25},{9,1},{17,9},{25,17},{2,26},{10... | collective-permute-start | bytes 786440 | tf_op jit(solution)/shard_map/ppermute | solution.py:768
  75.2 2.4 collective-permute-start.10
  78.9 2.3 copy.74.w_rest_ref
  81.2 16.9 %forward_scan.2 = (f32[1024,512]{1,0:T(8,128)}, f32[1024,896]{1,0:T(8,128)}, f32[1024,512]{1,0:T(8,128)}, f32[4,512,128]{2,1,0:T(8,128)}) custom-call(s32[4]{0:T(128)} %copy-done.27, bf16[1024,256]{1,0:T(8,128)(2,1)} %copy-done.2, bf16[1024,256]{1,0:T(8,128)(2,1)} %copy-done.5, bf16[1024,256]{1,0:T(8,128)(2,1)} %copy-done.4, bf16[1024,256]{1,0:T(8,128)(2,1)} %copy-done.8, ...), custom_call_target="tpu_custom_call" | custom-call | flops 1000000000 | bytes 10000000 | tf_op jit(solution)/shard_map/forward_scan/pallas_call | solution.py:956
  110.0 2.1 constant_dynamic-slice_fusion.2.conv_ref.before_ref
  112.0 6.6 %collective-permute-done.16 = bf16[512,256]{1,0:T(8,128)(2,1)S(1)} collective-permute-done((bf16[512,256]{1,0:T(8,128)(2,1)S(1)}, bf16[512,256]{1,0:T(8,128)(2,1)S(1)}, u32[]{:S(2)}, u32[]{:S(2)}) %collective-permute-start.16) | collective-permute-done | bytes 262176 | tf_op jit(solution)/shard_map/ppermute | solution.py:763
  119.4 16.5 %forward_scan.3 = (f32[1024,512]{1,0:T(8,128)}, f32[1024,896]{1,0:T(8,128)}, f32[1024,512]{1,0:T(8,128)}, f32[4,512,128]{2,1,0:T(8,128)}) custom-call(s32[4]{0:T(128)} %copy-done.27, bf16[1024,256]{1,0:T(8,128)(2,1)} %copy-done, bf16[1024,256]{1,0:T(8,128)(2,1)} %copy-done.7, bf16[1024,256]{1,0:T(8,128)(2,1)} %copy-done.6, bf16[1024,256]{1,0:T(8,128)(2,1)} %copy-done.9, ...), custom_call_target="tpu_custom_call" | custom-call | flops 1000000000 | bytes 10000000 | tf_op jit(solution)/shard_map/forward_scan/pallas_call | solution.py:956
  138.1 6.1 %gate_sums.2 = (f32[1024,512]{1,0:T(8,128)}, f32[4,8,256]{2,1,0:T(8,128)}) custom-call(s32[4]{0:T(128)} %iota.9.index_ref, bf16[4,1024,256]{2,1,0:T(8,128)(2,1)} %all-gather.6.cloned.1.call-done.g0.g1.g2.g3, bf16[4,1024,256]{2,1,0:T(8,128)(2,1)} %all-gather.6.cloned.1.call-done.g0.g1.g2.g3, bf16[4,1024,256]{2,1,0:T(8,128)(2,1)} %all-gather.6.cloned.1.call-done.g0.g1.g2.g3, ...), custom_call_target="tpu_custom_call" | custom-call | flops 1000000000 | bytes 1000000 | tf_op jit(solution)/shard_map/gate_sums/pallas_call | solution.py:1054
  147.7 2.1 constant_dynamic-slice_fusion.3.conv_ref.before_ref
  149.8 1.9 collective-permute-done.12.q1
  152.3 27.1 %backward_scan.2 = (bf16[1024,512]{1,0:T(8,128)(2,1)}, bf16[1024,512]{1,0:T(8,128)(2,1)}, bf16[1024,512]{1,0:T(8,128)(2,1)}, bf16[1024,128]{1,0:T(8,128)(2,1)}, ...) custom-call(s32[4]{0:T(128)} %copy-done.27, f32[4,8,256]{2,1,0:T(8,128)} %get-tuple-element.129.q0, ...), custom_call_target="tpu_custom_call" | custom-call | flops 2000000000 | bytes 10000000 | tf_op jit(solution)/shard_map/backward_scan/pallas_call | solution.py:1082
  180.0 6.6 %gate_sums.3 = (f32[1024,512]{1,0:T(8,128)}, f32[4,8,256]{2,1,0:T(8,128)}) custom-call(s32[4]{0:T(128)} %iota.10.index_ref, bf16[4,1024,256]{2,1,0:T(8,128)(2,1)} %all-gather.8.cloned.1.call-done.g0.g1.g2.g3, bf16[4,1024,256]{2,1,0:T(8,128)(2,1)} %all-gather.8.cloned.1.call-done.g0.g1.g2.g3, bf16[4,1024,256]{2,1,0:T(8,128)(2,1)} %all-gather.8.cloned.1.call-done.g0.g1.g2.g3, ...), custom_call_target="tpu_custom_call" | custom-call | flops 1000000000 | bytes 1000000 | tf_op jit(solution)/shard_map/gate_sums/pallas_call | solution.py:1054
  198.8 27.2 %backward_scan.3 = (bf16[1024,512]{1,0:T(8,128)(2,1)}, bf16[1024,512]{1,0:T(8,128)(2,1)}, bf16[1024,512]{1,0:T(8,128)(2,1)}, bf16[1024,128]{1,0:T(8,128)(2,1)}, ...) custom-call(s32[4]{0:T(128)} %copy-done.27, f32[4,8,256]{2,1,0:T(8,128)} %get-tuple-element.140.q0, ...), custom_call_target="tpu_custom_call" | custom-call | flops 2000000000 | bytes 10000000 | tf_op jit(solution)/shard_map/backward_scan/pallas_call | solution.py:1082
  225.9 15.3 %weight_sums.2 = (f32[1024,1024]{1,0:T(8,128)}, f32[1536,1024]{1,0:T(8,128)}, f32[1024,128]{1,0:T(8,128)}) custom-call(s32[4]{0:T(128)} %copy-done.27, bf16[1024,256]{1,0:T(8,128)(2,1)} %copy-done.2, bf16[1024,256]{1,0:T(8,128)(2,1)} %copy-done.5, bf16[1024,256]{1,0:T(8,128)(2,1)} %copy-done.4, bf16[1024,256]{1,0:T(8,128)(2,1)} %copy-done.8, ...), custom_call_target="tpu_custom_call" | custom-call | flops 2000000000 | bytes 10000000 | tf_op jit(solution)/shard_map/weight_sums/pallas_call | solution.py:1006
  241.2 17.3 %weight_sums.3 = (f32[1024,1024]{1,0:T(8,128)}, f32[1536,1024]{1,0:T(8,128)}, f32[1024,128]{1,0:T(8,128)}) custom-call(s32[4]{0:T(128)} %copy-done.27, bf16[1024,256]{1,0:T(8,128)(2,1)} %copy-done, bf16[1024,256]{1,0:T(8,128)(2,1)} %copy-done.7, bf16[1024,256]{1,0:T(8,128)(2,1)} %copy-done.6, bf16[1024,256]{1,0:T(8,128)(2,1)} %copy-done.9, ...), custom_call_target="tpu_custom_call" | custom-call | flops 2000000000 | bytes 10000000 | tf_op jit(solution)/shard_map/weight_sums/pallas_call | solution.py:1006
  263.6 1.9 reshape.200
  278.0 7.3 %input_sums.2 = (f32[4,264,256]{2,1,0:T(8,128)}, bf16[4,272,256]{2,1,0:T(8,128)(2,1)}, bf16[4,272,256]{2,1,0:T(8,128)(2,1)}, bf16[4,272,256]{2,1,0:T(8,128)(2,1)}, f32[1024,64]{1,0:T(8,128)}, /*index=5*/f32[8,64]{1,0:T(8,128)}) custom-call(s32[4]{0:T(128)} %copy-done.27, bf16[1024,256]{1,0:T(8,128)(2,1)} %copy-done.2, bf16[1024,256]{1,0:T(8,128)(2,1)} %copy-done.5, ...), custom_call_target="tpu_custom_call" | custom-call | flops 1000000000 | bytes 10000000 | tf_op jit(solution)/shard_map/input_sums/pallas_call | solution.py:1104
  293.7 7.4 %input_sums.3 = (f32[4,264,256]{2,1,0:T(8,128)}, bf16[4,272,256]{2,1,0:T(8,128)(2,1)}, bf16[4,272,256]{2,1,0:T(8,128)(2,1)}, bf16[4,272,256]{2,1,0:T(8,128)(2,1)}, f32[1024,64]{1,0:T(8,128)}, /*index=5*/f32[8,64]{1,0:T(8,128)}) custom-call(s32[4]{0:T(128)} %copy-done.27, bf16[1024,256]{1,0:T(8,128)(2,1)} %copy-done, bf16[1024,256]{1,0:T(8,128)(2,1)} %copy-done.7, ...), custom_call_target="tpu_custom_call" | custom-call | flops 1000000000 | bytes 10000000 | tf_op jit(solution)/shard_map/input_sums/pallas_call | solution.py:1104
  313.1 5.0 %input_gradient.2 = (f32[1024,256]{1,0:T(8,128)}, f32[8,256]{1,0:T(8,128)}) custom-call(bf16[1024,256]{1,0:T(8,128)(2,1)} %copy-done.2, bf16[1024,256]{1,0:T(8,128)(2,1)} %copy-done.5, bf16[1024,256]{1,0:T(8,128)(2,1)} %copy-done.4, bf16[1024,256]{1,0:T(8,128)(2,1)} %copy-done.8, f32[4,256]{1,0:T(4,128)} %pad_maximum_fusion.3.gain_ref, ...), custom_call_target="tpu_custom_call" | custom-call | flops 100000000 | bytes 1000000 | tf_op jit(solution)/shard_map/input_gradient/pallas_call | solution.py:1125
  318.1 6.9 %collective-permute-done.35.r1 = bf16[4,272,256]{2,1,0:T(8,128)(2,1)} collective-permute-done((bf16[4,272,256]{2,1,0:T(8,128)(2,1)}, bf16[4,272,256]{2,1,0:T(8,128)(2,1)}, u32[]{:S(2)}, u32[]{:S(2)}) %collective-permute-start.35) | collective-permute-done | bytes 557088 | tf_op jit(solution)/shard_map/ppermute | solution.py:763
  325.1 7.0 %collective-permute-done.36.r2 = bf16[4,272,256]{2,1,0:T(8,128)(2,1)} collective-permute-done((bf16[4,272,256]{2,1,0:T(8,128)(2,1)}, bf16[4,272,256]{2,1,0:T(8,128)(2,1)}, u32[]{:S(2)}, u32[]{:S(2)}) %collective-permute-start.36) | collective-permute-done | bytes 557088 | tf_op jit(solution)/shard_map/ppermute | solution.py:763
  332.1 5.0 %input_gradient.3 = (f32[1024,256]{1,0:T(8,128)}, f32[8,256]{1,0:T(8,128)}) custom-call(bf16[1024,256]{1,0:T(8,128)(2,1)} %copy-done, bf16[1024,256]{1,0:T(8,128)(2,1)} %copy-done.7, bf16[1024,256]{1,0:T(8,128)(2,1)} %copy-done.6, bf16[1024,256]{1,0:T(8,128)(2,1)} %copy-done.9, f32[4,256]{1,0:T(4,128)} %pad_maximum_fusion.3.gain_ref, ...), custom_call_target="tpu_custom_call" | custom-call | flops 100000000 | bytes 1000000 | tf_op jit(solution)/shard_map/input_gradient/pallas_call | solution.py:1125
  337.1 1.9 slice_add_fusion
  340.5 2.3 fusion.24
  353.1 2.4 collective-permute-start.48
  361.1 2.3 concatenate.146
  370.3 1.7 collective-permute-start.31
  373.9 2.7 collective-permute-done.45
  397.9 3.5 collective-permute-start.51
  401.9 2.3 collective-permute-start.33
  404.2 15.4 %collective-permute-done.39 = f16[1024,256]{1,0:T(8,128)(2,1)S(1)} collective-permute-done((f16[1024,256]{1,0:T(8,128)(2,1)S(1)}, f16[1024,256]{1,0:T(8,128)(2,1)S(1)}, u32[]{:S(2)}, u32[]{:S(2)}) %collective-permute-start.39) | collective-permute-done | bytes 524320 | tf_op jit(solution)/shard_map/ppermute | solution.py:763
  419.7 5.2 %collective-permute-start.32 = (bf16[256,256]{1,0:T(8,128)(2,1)S(1)}, bf16[256,256]{1,0:T(8,128)(2,1)S(1)}, u32[]{:S(2)}, u32[]{:S(2)}) collective-permute-start(bf16[256,256]{1,0:T(8,128)(2,1)S(1)} %get-tuple-element.265), channel_id=1, source_target_pairs={{0,24},{8,0},{16,8},{24,16},{1,25},{9,1},{17,9},{25,17},{2,26},{10... | collective-permute-start | bytes 393224 | tf_op jit(solution)/shard_map/ppermute | solution.py:768
  425.4 7.6 %collective-permute-done.32 = bf16[256,256]{1,0:T(8,128)(2,1)S(1)} collective-permute-done((bf16[256,256]{1,0:T(8,128)(2,1)S(1)}, bf16[256,256]{1,0:T(8,128)(2,1)S(1)}, u32[]{:S(2)}, u32[]{:S(2)}) %collective-permute-start.32) | collective-permute-done | bytes 131104 | tf_op jit(solution)/shard_map/ppermute | solution.py:768
  433.0 2.7 collective-permute-start.42
  435.7 1.6 collective-permute-start.41
  437.5 2.1 collective-permute-start.52
  439.5 10.3 %collective-permute-done.41 = bf16[256,256]{1,0:T(8,128)(2,1)S(1)} collective-permute-done((bf16[256,256]{1,0:T(8,128)(2,1)S(1)}, bf16[256,256]{1,0:T(8,128)(2,1)S(1)}, u32[]{:S(2)}, u32[]{:S(2)}) %collective-permute-start.41) | collective-permute-done | bytes 131104 | tf_op jit(solution)/shard_map/ppermute | solution.py:768
  451.3 21.7 %collective-permute-done.52 = f32[622,128]{1,0:T(8,128)S(1)} collective-permute-done((f32[622,128]{1,0:T(8,128)S(1)}, f32[622,128]{1,0:T(8,128)S(1)}, u32[]{:S(2)}, u32[]{:S(2)}) %collective-permute-start.52) | collective-permute-done | bytes 318496 | tf_op jit(solution)/shard_map/ppermute | solution.py:846
  479.4 3.2 slice.419
  482.6 4.7 fusion.40
  (369 shorter events, 141.8 us)
Async XLA Ops:
  7.2 39.5 %all-gather.10.cloned.1.call-start = ((), (), s32[]{:S(2)}) async-start(), calls=%async_computation.3 | async-start | bytes 1474560 | tf_op jit(solution)/shard_map/all_gather | solution.py:882
  14.1 123.4 %all-gather.6.cloned.1.call-start = ((), (), s32[]{:S(2)}) async-start(), calls=%async_computation | async-start | bytes 2621440 | tf_op jit(solution)/shard_map/all_gather | solution.py:961
  15.1 24.0 %collective-permute-start.2 = (bf16[2,256,256]{2,1,0:T(8,128)(2,1)}, bf16[2,256,256]{2,1,0:T(8,128)(2,1)S(1)}, u32[]{:S(2)}, u32[]{:S(2)}) collective-permute-start(bf16[2,256,256]{2,1,0:T(8,128)(2,1)} %get-tuple-element.260), channel_id=1, source_target_pairs={{0,8},{8,16},{16,24},{24,0},{1,9},{9,17},{17,25},{25,1},{2,10},{10... | collective-permute-start | bytes 786440 | tf_op jit(solution)/shard_map/ppermute | solution.py:768
  18.1 20.0 %collective-permute-start.1 = (bf16[2,256,256]{2,1,0:T(8,128)(2,1)}, bf16[2,256,256]{2,1,0:T(8,128)(2,1)}, u32[]{:S(2)}, u32[]{:S(2)}) collective-permute-start(bf16[2,256,256]{2,1,0:T(8,128)(2,1)} %get-tuple-element.261), channel_id=1, source_target_pairs={{0,16},{8,24},{16,0},{24,8},{1,17},{9,25},{17,1},{25,9},{2,18},{10... | collective-permute-start | bytes 786440 | tf_op jit(solution)/shard_map/ppermute | solution.py:768
  20.7 14.6 %collective-permute-start = (bf16[2,256,256]{2,1,0:T(8,128)(2,1)}, bf16[2,256,256]{2,1,0:T(8,128)(2,1)}, u32[]{:S(2)}, u32[]{:S(2)}) collective-permute-start(bf16[2,256,256]{2,1,0:T(8,128)(2,1)} %get-tuple-element.262), channel_id=1, source_target_pairs={{0,24},{8,0},{16,8},{24,16},{1,25},{9,1},{17,9},{25,17},{2,26},{10... | collective-permute-start | bytes 786440 | tf_op jit(solution)/shard_map/ppermute | solution.py:768
  42.4 14.1 %collective-permute-start.4 = (bf16[1024,256]{1,0:T(8,128)(2,1)S(1)}, bf16[1024,256]{1,0:T(8,128)(2,1)S(1)}, u32[]{:S(2)}, u32[]{:S(2)}) collective-permute-start(bf16[1024,256]{1,0:T(8,128)(2,1)S(1)} %get-tuple-element.118.x0), channel_id=1, source_target_pairs={{0,2},{1,3},{2,0},{3,1},{4,6},{5,7},{6,4},{7,5},{8,10},{9,11},{10,... | collective-permute-start | bytes 1572872 | tf_op jit(solution)/shard_map/ppermute | solution.py:763
  43.9 13.5 %collective-permute-start.3 = (bf16[1024,256]{1,0:T(8,128)(2,1)S(1)}, bf16[1024,256]{1,0:T(8,128)(2,1)S(1)}, u32[]{:S(2)}, u32[]{:S(2)}) collective-permute-start(bf16[1024,256]{1,0:T(8,128)(2,1)S(1)} %get-tuple-element.118.x0), channel_id=1, source_target_pairs={{0,1},{1,0},{2,3},{3,2},{4,5},{5,4},{6,7},{7,6},{8,9},{9,8},{10,11... | collective-permute-start | bytes 1572872 | tf_op jit(solution)/shard_map/ppermute | solution.py:763
  64.9 16.2 %collective-permute-start.8 = (bf16[1024,256]{1,0:T(8,128)(2,1)S(1)}, bf16[1024,256]{1,0:T(8,128)(2,1)S(1)}, u32[]{:S(2)}, u32[]{:S(2)}) collective-permute-start(bf16[1024,256]{1,0:T(8,128)(2,1)S(1)} %get-tuple-element.117.x0), channel_id=1, source_target_pairs={{0,2},{1,3},{2,0},{3,1},{4,6},{5,7},{6,4},{7,5},{8,10},{9,11},{10,... | collective-permute-start | bytes 1572872 | tf_op jit(solution)/shard_map/ppermute | solution.py:763
  66.4 14.8 %collective-permute-start.7 = (bf16[1024,256]{1,0:T(8,128)(2,1)S(1)}, bf16[1024,256]{1,0:T(8,128)(2,1)S(1)}, u32[]{:S(2)}, u32[]{:S(2)}) collective-permute-start(bf16[1024,256]{1,0:T(8,128)(2,1)S(1)} %get-tuple-element.117.x0), channel_id=1, source_target_pairs={{0,1},{1,0},{2,3},{3,2},{4,5},{5,4},{6,7},{7,6},{8,9},{9,8},{10,11... | collective-permute-start | bytes 1572872 | tf_op jit(solution)/shard_map/ppermute | solution.py:763
  68.8 29.3 %collective-permute-start.11 = (bf16[2,256,256]{2,1,0:T(8,128)(2,1)}, bf16[2,256,256]{2,1,0:T(8,128)(2,1)S(1)}, u32[]{:S(2)}, u32[]{:S(2)}) collective-permute-start(bf16[2,256,256]{2,1,0:T(8,128)(2,1)} %get-tuple-element.256), channel_id=1, source_target_pairs={{0,24},{8,0},{16,8},{24,16},{1,25},{9,1},{17,9},{25,17},{2,26},{10... | collective-permute-start | bytes 786440 | tf_op jit(solution)/shard_map/ppermute | solution.py:768
  75.2 22.9 %collective-permute-start.10 = (bf16[2,256,256]{2,1,0:T(8,128)(2,1)}, bf16[2,256,256]{2,1,0:T(8,128)(2,1)S(1)}, u32[]{:S(2)}, u32[]{:S(2)}) collective-permute-start(bf16[2,256,256]{2,1,0:T(8,128)(2,1)} %get-tuple-element.257), channel_id=1, source_target_pairs={{0,16},{8,24},{16,0},{24,8},{1,17},{9,25},{17,1},{25,9},{2,18},{10... | collective-permute-start | bytes 786440 | tf_op jit(solution)/shard_map/ppermute | solution.py:768
  77.5 20.5 %collective-permute-start.9 = (bf16[2,256,256]{2,1,0:T(8,128)(2,1)}, bf16[2,256,256]{2,1,0:T(8,128)(2,1)S(1)}, u32[]{:S(2)}, u32[]{:S(2)}) collective-permute-start(bf16[2,256,256]{2,1,0:T(8,128)(2,1)} %get-tuple-element.258), channel_id=1, source_target_pairs={{0,8},{8,16},{16,24},{24,0},{1,9},{9,17},{17,25},{25,1},{2,10},{10... | collective-permute-start | bytes 786440 | tf_op jit(solution)/shard_map/ppermute | solution.py:768
  99.4 80.1 %all-gather.8.cloned.1.call-start = ((), (), s32[]{:S(2)}) async-start(), calls=%async_computation.1 | async-start | bytes 2621440 | tf_op jit(solution)/shard_map/all_gather | solution.py:961
  100.2 379.3 %all-reduce.17.cloned.1.call-start = ((), (), s32[]{:S(2)}) async-start(), calls=%async_computation.2 | async-start | bytes 12582912 | tf_op jit(solution)/shard_map/psum | solution.py:1098
  100.6 11.4 %collective-permute-start.15 = (bf16[512,256]{1,0:T(8,128)(2,1)S(1)}, bf16[512,256]{1,0:T(8,128)(2,1)S(1)}, u32[]{:S(2)}, u32[]{:S(2)}) collective-permute-start(bf16[512,256]{1,0:T(8,128)(2,1)S(1)} %slice.375), channel_id=1, source_target_pairs={{0,2},{1,3},{2,0},{3,1},{4,6},{5,7},{6,4},{7,5},{8,10},{9,11},{10,... | collective-permute-start | bytes 786440 | tf_op jit(solution)/shard_map/ppermute | solution.py:763
  194.6 74.0 %collective-permute-start.24 = (f16[528,128]{1,0:T(8,128)(2,1)}, f16[528,128]{1,0:T(8,128)(2,1)}, u32[]{:S(2)}, u32[]{:S(2)}) collective-permute-start(f16[528,128]{1,0:T(8,128)(2,1)} %concatenate.124), channel_id=1, source_target_pairs={{0,2},{1,3},{2,0},{3,1},{4,6},{5,7},{6,4},{7,5},{8,10},{9,11},{10,... | collective-permute-start | bytes 405512 | tf_op jit(solution)/shard_map/ppermute | solution.py:763
  195.2 76.7 %collective-permute-start.23 = (f16[528,128]{1,0:T(8,128)(2,1)}, f16[528,128]{1,0:T(8,128)(2,1)}, u32[]{:S(2)}, u32[]{:S(2)}) collective-permute-start(f16[528,128]{1,0:T(8,128)(2,1)} %concatenate.122), channel_id=1, source_target_pairs={{0,1},{1,0},{2,3},{3,2},{4,5},{5,4},{6,7},{7,6},{8,9},{9,8},{10,11... | collective-permute-start | bytes 405512 | tf_op jit(solution)/shard_map/ppermute | solution.py:763
  196.7 77.1 %collective-permute-start.25 = (f16[528,128]{1,0:T(8,128)(2,1)}, f16[528,128]{1,0:T(8,128)(2,1)}, u32[]{:S(2)}, u32[]{:S(2)}) collective-permute-start(f16[528,128]{1,0:T(8,128)(2,1)} %concatenate.126), channel_id=1, source_target_pairs={{0,3},{1,2},{2,1},{3,0},{4,7},{5,6},{6,5},{7,4},{8,11},{9,10},{10,... | collective-permute-start | bytes 405512 | tf_op jit(solution)/shard_map/ppermute | solution.py:763
  265.8 21.4 %collective-permute-start.22 = (f16[528,128]{1,0:T(8,128)(2,1)S(1)}, f16[528,128]{1,0:T(8,128)(2,1)S(1)}, u32[]{:S(2)}, u32[]{:S(2)}) collective-permute-start(f16[528,128]{1,0:T(8,128)(2,1)S(1)} %concatenate.132), channel_id=1, source_target_pairs={{0,3},{1,2},{2,1},{3,0},{4,7},{5,6},{6,5},{7,4},{8,11},{9,10},{10,... | collective-permute-start | bytes 405512 | tf_op jit(solution)/shard_map/ppermute | solution.py:763
  267.2 22.8 %collective-permute-start.21 = (f16[528,128]{1,0:T(8,128)(2,1)S(1)}, f16[528,128]{1,0:T(8,128)(2,1)S(1)}, u32[]{:S(2)}, u32[]{:S(2)}) collective-permute-start(f16[528,128]{1,0:T(8,128)(2,1)S(1)} %concatenate.130), channel_id=1, source_target_pairs={{0,2},{1,3},{2,0},{3,1},{4,6},{5,7},{6,4},{7,5},{8,10},{9,11},{10,... | collective-permute-start | bytes 405512 | tf_op jit(solution)/shard_map/ppermute | solution.py:763
  268.6 22.7 %collective-permute-start.20 = (f16[528,128]{1,0:T(8,128)(2,1)S(1)}, f16[528,128]{1,0:T(8,128)(2,1)S(1)}, u32[]{:S(2)}, u32[]{:S(2)}) collective-permute-start(f16[528,128]{1,0:T(8,128)(2,1)S(1)} %concatenate.128), channel_id=1, source_target_pairs={{0,1},{1,0},{2,3},{3,2},{4,5},{5,4},{6,7},{7,6},{8,9},{9,8},{10,11... | collective-permute-start | bytes 405512 | tf_op jit(solution)/shard_map/ppermute | solution.py:763
  285.2 21.8 %collective-permute-start.26 = (bf16[4,272,256]{2,1,0:T(8,128)(2,1)}, bf16[4,272,256]{2,1,0:T(8,128)(2,1)S(1)}, u32[]{:S(2)}, u32[]{:S(2)}) collective-permute-start(bf16[4,272,256]{2,1,0:T(8,128)(2,1)} %get-tuple-element.168), channel_id=1, source_target_pairs={{0,1},{1,0},{2,3},{3,2},{4,5},{5,4},{6,7},{7,6},{8,9},{9,8},{10,11... | collective-permute-start | bytes 1671176 | tf_op jit(solution)/shard_map/ppermute | solution.py:763
  285.9 27.0 %collective-permute-start.27 = (bf16[4,272,256]{2,1,0:T(8,128)(2,1)}, bf16[4,272,256]{2,1,0:T(8,128)(2,1)}, u32[]{:S(2)}, u32[]{:S(2)}) collective-permute-start(bf16[4,272,256]{2,1,0:T(8,128)(2,1)} %get-tuple-element.169), channel_id=1, source_target_pairs={{0,2},{1,3},{2,0},{3,1},{4,6},{5,7},{6,4},{7,5},{8,10},{9,11},{10,... | collective-permute-start | bytes 1671176 | tf_op jit(solution)/shard_map/ppermute | solution.py:763
  287.2 25.9 %collective-permute-start.28 = (bf16[4,272,256]{2,1,0:T(8,128)(2,1)}, bf16[4,272,256]{2,1,0:T(8,128)(2,1)}, u32[]{:S(2)}, u32[]{:S(2)}) collective-permute-start(bf16[4,272,256]{2,1,0:T(8,128)(2,1)} %get-tuple-element.170), channel_id=1, source_target_pairs={{0,3},{1,2},{2,1},{3,0},{4,7},{5,6},{6,5},{7,4},{8,11},{9,10},{10,... | collective-permute-start | bytes 1671176 | tf_op jit(solution)/shard_map/ppermute | solution.py:763
  301.1 23.9 %collective-permute-start.35 = (bf16[4,272,256]{2,1,0:T(8,128)(2,1)}, bf16[4,272,256]{2,1,0:T(8,128)(2,1)}, u32[]{:S(2)}, u32[]{:S(2)}) collective-permute-start(bf16[4,272,256]{2,1,0:T(8,128)(2,1)} %get-tuple-element.175), channel_id=1, source_target_pairs={{0,1},{1,0},{2,3},{3,2},{4,5},{5,4},{6,7},{7,6},{8,9},{9,8},{10,11... | collective-permute-start | bytes 1671176 | tf_op jit(solution)/shard_map/ppermute | solution.py:763
  301.8 30.3 %collective-permute-start.36 = (bf16[4,272,256]{2,1,0:T(8,128)(2,1)}, bf16[4,272,256]{2,1,0:T(8,128)(2,1)}, u32[]{:S(2)}, u32[]{:S(2)}) collective-permute-start(bf16[4,272,256]{2,1,0:T(8,128)(2,1)} %get-tuple-element.176), channel_id=1, source_target_pairs={{0,2},{1,3},{2,0},{3,1},{4,6},{5,7},{6,4},{7,5},{8,10},{9,11},{10,... | collective-permute-start | bytes 1671176 | tf_op jit(solution)/shard_map/ppermute | solution.py:763
  307.0 25.1 %collective-permute-start.37 = (bf16[4,272,256]{2,1,0:T(8,128)(2,1)}, bf16[4,272,256]{2,1,0:T(8,128)(2,1)}, u32[]{:S(2)}, u32[]{:S(2)}) collective-permute-start(bf16[4,272,256]{2,1,0:T(8,128)(2,1)} %get-tuple-element.177), channel_id=1, source_target_pairs={{0,3},{1,2},{2,1},{3,0},{4,7},{5,6},{6,5},{7,4},{8,11},{9,10},{10,... | collective-permute-start | bytes 1671176 | tf_op jit(solution)/shard_map/ppermute | solution.py:763
  343.5 15.5 %collective-permute-start.49 = (f16[272,256]{1,0:T(8,128)(2,1)}, f16[272,256]{1,0:T(8,128)(2,1)}, u32[]{:S(2)}, u32[]{:S(2)}) collective-permute-start(f16[272,256]{1,0:T(8,128)(2,1)} %concatenate.144), channel_id=1, source_target_pairs={{0,8},{8,16},{16,24},{24,0},{1,9},{9,17},{17,25},{25,1},{2,10},{10... | collective-permute-start | bytes 417800 | tf_op jit(solution)/shard_map/ppermute | solution.py:768
  353.1 12.2 %collective-permute-start.48 = (f16[272,256]{1,0:T(8,128)(2,1)}, f16[272,256]{1,0:T(8,128)(2,1)S(1)}, u32[]{:S(2)}, u32[]{:S(2)}) collective-permute-start(f16[272,256]{1,0:T(8,128)(2,1)} %concatenate.143), channel_id=1, source_target_pairs={{0,16},{8,24},{16,0},{24,8},{1,17},{9,25},{17,1},{25,9},{2,18},{10... | collective-permute-start | bytes 417800 | tf_op jit(solution)/shard_map/ppermute | solution.py:768
  355.5 12.2 %collective-permute-start.47 = (f16[272,256]{1,0:T(8,128)(2,1)}, f16[272,256]{1,0:T(8,128)(2,1)}, u32[]{:S(2)}, u32[]{:S(2)}) collective-permute-start(f16[272,256]{1,0:T(8,128)(2,1)} %concatenate.142), channel_id=1, source_target_pairs={{0,24},{8,0},{16,8},{24,16},{1,25},{9,1},{17,9},{25,17},{2,26},{10... | collective-permute-start | bytes 417800 | tf_op jit(solution)/shard_map/ppermute | solution.py:768
  357.0 13.4 %collective-permute-start.44 = (f16[272,256]{1,0:T(8,128)(2,1)}, f16[272,256]{1,0:T(8,128)(2,1)}, u32[]{:S(2)}, u32[]{:S(2)}) collective-permute-start(f16[272,256]{1,0:T(8,128)(2,1)} %concatenate.138), channel_id=1, source_target_pairs={{0,24},{8,0},{16,8},{24,16},{1,25},{9,1},{17,9},{25,17},{2,26},{10... | collective-permute-start | bytes 417800 | tf_op jit(solution)/shard_map/ppermute | solution.py:768
  357.5 19.1 %collective-permute-start.45 = (f16[272,256]{1,0:T(8,128)(2,1)}, f16[272,256]{1,0:T(8,128)(2,1)}, u32[]{:S(2)}, u32[]{:S(2)}) collective-permute-start(f16[272,256]{1,0:T(8,128)(2,1)} %concatenate.139), channel_id=1, source_target_pairs={{0,16},{8,24},{16,0},{24,8},{1,17},{9,25},{17,1},{25,9},{2,18},{10... | collective-permute-start | bytes 417800 | tf_op jit(solution)/shard_map/ppermute | solution.py:768
  359.0 19.5 %collective-permute-start.46 = (f16[272,256]{1,0:T(8,128)(2,1)}, f16[272,256]{1,0:T(8,128)(2,1)}, u32[]{:S(2)}, u32[]{:S(2)}) collective-permute-start(f16[272,256]{1,0:T(8,128)(2,1)} %concatenate.140), channel_id=1, source_target_pairs={{0,8},{8,16},{16,24},{24,0},{1,9},{9,17},{17,25},{25,1},{2,10},{10... | collective-permute-start | bytes 417800 | tf_op jit(solution)/shard_map/ppermute | solution.py:768
  365.3 30.6 %collective-permute-start.29 = (f16[1024,256]{1,0:T(8,128)(2,1)}, f16[1024,256]{1,0:T(8,128)(2,1)S(1)}, u32[]{:S(2)}, u32[]{:S(2)}) collective-permute-start(f16[1024,256]{1,0:T(8,128)(2,1)} %fusion), channel_id=1, source_target_pairs={{0,1},{1,0},{2,3},{3,2},{4,5},{5,4},{6,7},{7,6},{8,9},{9,8},{10,11... | collective-permute-start | bytes 1572872 | tf_op jit(solution)/shard_map/ppermute | solution.py:763
  367.7 30.2 %collective-permute-start.30 = (f16[1024,256]{1,0:T(8,128)(2,1)}, f16[1024,256]{1,0:T(8,128)(2,1)S(1)}, u32[]{:S(2)}, u32[]{:S(2)}) collective-permute-start(f16[1024,256]{1,0:T(8,128)(2,1)} %fusion.1), channel_id=1, source_target_pairs={{0,2},{1,3},{2,0},{3,1},{4,6},{5,7},{6,4},{7,5},{8,10},{9,11},{10,... | collective-permute-start | bytes 1572872 | tf_op jit(solution)/shard_map/ppermute | solution.py:763
  370.3 31.1 %collective-permute-start.31 = (f16[1024,256]{1,0:T(8,128)(2,1)}, f16[1024,256]{1,0:T(8,128)(2,1)S(1)}, u32[]{:S(2)}, u32[]{:S(2)}) collective-permute-start(f16[1024,256]{1,0:T(8,128)(2,1)} %fusion.2), channel_id=1, source_target_pairs={{0,3},{1,2},{2,1},{3,0},{4,7},{5,6},{6,5},{7,4},{8,11},{9,10},{10,... | collective-permute-start | bytes 1572872 | tf_op jit(solution)/shard_map/ppermute | solution.py:763
  376.6 17.0 %collective-permute-start.50 = (f32[622,128]{1,0:T(8,128)S(1)}, f32[622,128]{1,0:T(8,128)S(1)}, u32[]{:S(2)}, u32[]{:S(2)}) collective-permute-start(f32[622,128]{1,0:T(8,128)S(1)} %concatenate.146), channel_id=1, source_target_pairs={{0,4},{4,0},{1,5},{5,1},{2,6},{6,2},{3,7},{7,3},{8,12},{12,8},{9,1... | collective-permute-start | bytes 955400 | tf_op jit(solution)/shard_map/ppermute | solution.py:846
  378.5 23.4 %collective-permute-start.38 = (f16[1024,256]{1,0:T(8,128)(2,1)}, f16[1024,256]{1,0:T(8,128)(2,1)S(1)}, u32[]{:S(2)}, u32[]{:S(2)}) collective-permute-start(f16[1024,256]{1,0:T(8,128)(2,1)} %fusion.3), channel_id=1, source_target_pairs={{0,1},{1,0},{2,3},{3,2},{4,5},{5,4},{6,7},{7,6},{8,9},{9,8},{10,11... | collective-permute-start | bytes 1572872 | tf_op jit(solution)/shard_map/ppermute | solution.py:763
  394.4 25.3 %collective-permute-start.39 = (f16[1024,256]{1,0:T(8,128)(2,1)S(1)}, f16[1024,256]{1,0:T(8,128)(2,1)S(1)}, u32[]{:S(2)}, u32[]{:S(2)}) collective-permute-start(f16[1024,256]{1,0:T(8,128)(2,1)S(1)} %copy-done.46), channel_id=1, source_target_pairs={{0,2},{1,3},{2,0},{3,1},{4,6},{5,7},{6,4},{7,5},{8,10},{9,11},{10,... | collective-permute-start | bytes 1572872 | tf_op jit(solution)/shard_map/ppermute | solution.py:763
  395.8 29.0 %collective-permute-start.40 = (f16[1024,256]{1,0:T(8,128)(2,1)S(1)}, f16[1024,256]{1,0:T(8,128)(2,1)S(1)}, u32[]{:S(2)}, u32[]{:S(2)}) collective-permute-start(f16[1024,256]{1,0:T(8,128)(2,1)S(1)} %copy-done.45), channel_id=1, source_target_pairs={{0,3},{1,2},{2,1},{3,0},{4,7},{5,6},{6,5},{7,4},{8,11},{9,10},{10,... | collective-permute-start | bytes 1572872 | tf_op jit(solution)/shard_map/ppermute | solution.py:763
  397.9 39.5 %collective-permute-start.51 = (f32[622,128]{1,0:T(8,128)S(1)}, f32[622,128]{1,0:T(8,128)S(1)}, u32[]{:S(2)}, u32[]{:S(2)}) collective-permute-start(f32[622,128]{1,0:T(8,128)S(1)} %add.284), channel_id=1, source_target_pairs={{0,8},{8,0},{16,24},{24,16},{1,9},{9,1},{17,25},{25,17},{2,10},{10... | collective-permute-start | bytes 955400 | tf_op jit(solution)/shard_map/ppermute | solution.py:846
  401.8 35.5 %collective-permute-start.34 = (bf16[256,256]{1,0:T(8,128)(2,1)S(1)}, bf16[256,256]{1,0:T(8,128)(2,1)S(1)}, u32[]{:S(2)}, u32[]{:S(2)}) collective-permute-start(bf16[256,256]{1,0:T(8,128)(2,1)S(1)} %get-tuple-element.263), channel_id=1, source_target_pairs={{0,8},{8,16},{16,24},{24,0},{1,9},{9,17},{17,25},{25,1},{2,10},{10... | collective-permute-start | bytes 393224 | tf_op jit(solution)/shard_map/ppermute | solution.py:768
  401.9 33.8 %collective-permute-start.33 = (bf16[256,256]{1,0:T(8,128)(2,1)S(1)}, bf16[256,256]{1,0:T(8,128)(2,1)S(1)}, u32[]{:S(2)}, u32[]{:S(2)}) collective-permute-start(bf16[256,256]{1,0:T(8,128)(2,1)S(1)} %get-tuple-element.264), channel_id=1, source_target_pairs={{0,16},{8,24},{16,0},{24,8},{1,17},{9,25},{17,1},{25,9},{2,18},{10... | collective-permute-start | bytes 393224 | tf_op jit(solution)/shard_map/ppermute | solution.py:768
  419.7 13.3 %collective-permute-start.32 = (bf16[256,256]{1,0:T(8,128)(2,1)S(1)}, bf16[256,256]{1,0:T(8,128)(2,1)S(1)}, u32[]{:S(2)}, u32[]{:S(2)}) collective-permute-start(bf16[256,256]{1,0:T(8,128)(2,1)S(1)} %get-tuple-element.265), channel_id=1, source_target_pairs={{0,24},{8,0},{16,8},{24,16},{1,25},{9,1},{17,9},{25,17},{2,26},{10... | collective-permute-start | bytes 393224 | tf_op jit(solution)/shard_map/ppermute | solution.py:768
  425.3 24.6 %collective-permute-start.43 = (bf16[256,256]{1,0:T(8,128)(2,1)S(1)}, bf16[256,256]{1,0:T(8,128)(2,1)S(1)}, u32[]{:S(2)}, u32[]{:S(2)}) collective-permute-start(bf16[256,256]{1,0:T(8,128)(2,1)S(1)} %get-tuple-element.266), channel_id=1, source_target_pairs={{0,8},{8,16},{16,24},{24,0},{1,9},{9,17},{17,25},{25,1},{2,10},{10... | collective-permute-start | bytes 393224 | tf_op jit(solution)/shard_map/ppermute | solution.py:768
  433.0 16.9 %collective-permute-start.42 = (bf16[256,256]{1,0:T(8,128)(2,1)S(1)}, bf16[256,256]{1,0:T(8,128)(2,1)S(1)}, u32[]{:S(2)}, u32[]{:S(2)}) collective-permute-start(bf16[256,256]{1,0:T(8,128)(2,1)S(1)} %get-tuple-element.267), channel_id=1, source_target_pairs={{0,16},{8,24},{16,0},{24,8},{1,17},{9,25},{17,1},{25,9},{2,18},{10... | collective-permute-start | bytes 393224 | tf_op jit(solution)/shard_map/ppermute | solution.py:768
  435.7 14.1 %collective-permute-start.41 = (bf16[256,256]{1,0:T(8,128)(2,1)S(1)}, bf16[256,256]{1,0:T(8,128)(2,1)S(1)}, u32[]{:S(2)}, u32[]{:S(2)}) collective-permute-start(bf16[256,256]{1,0:T(8,128)(2,1)S(1)} %get-tuple-element.268), channel_id=1, source_target_pairs={{0,24},{8,0},{16,8},{24,16},{1,25},{9,1},{17,9},{25,17},{2,26},{10... | collective-permute-start | bytes 393224 | tf_op jit(solution)/shard_map/ppermute | solution.py:768
  437.5 35.5 %collective-permute-start.52 = (f32[622,128]{1,0:T(8,128)S(1)}, f32[622,128]{1,0:T(8,128)S(1)}, u32[]{:S(2)}, u32[]{:S(2)}) collective-permute-start(f32[622,128]{1,0:T(8,128)S(1)} %add.285), channel_id=1, source_target_pairs={{0,16},{8,24},{16,0},{24,8},{1,17},{9,25},{17,1},{25,9},{2,18},{10... | collective-permute-start | bytes 955400 | tf_op jit(solution)/shard_map/ppermute | solution.py:846
  (56 other events, 526.7 us)
Sparse Core Ops, SparseCore 0:
  14.3 30.4 all-gather.9
  99.5 37.9 all-gather.5
  139.4 35.4 all-gather.7
  285.4 180.5 all-reduce.16
